TPU v7x, 32 devices: a whole 2x2x4 slice. The times are simulated.
32 devices in a mesh: seq: 4 (over x, core), chan: 8 (over z, y).
Axes of the slice: x: 2, y: 2, z: 4, core: 2. Of those that a mesh axis runs over, the one named last changes fastest.
Arguments:
- values: bfloat16 [1024, 4096], P('chan', 'seq'), may hold values from -6 to 6
- gate_acts: bfloat16 [1024, 4096], P('chan', 'seq'), may hold values from -6 to 6
- cotangent: bfloat16 [1024, 4096], P('chan', 'seq'), may hold values from -6 to 6
- filter_taps: float32 [1024, 4096], P('chan', 'seq'), may hold values from -160 to 160
- w_value: bfloat16 [1024, 1024], replicated, may hold values from -0.1875 to 0.1875
- w_gate: bfloat16 [1024, 1024], replicated, may hold values from -0.1875 to 0.1875
Outputs:
- input_grad: bfloat16 [4096, 1024], P(('seq', 'chan'))
- filter_grad: float32 [1024, 4096], P('chan', 'seq')
All inputs are finite; a program needn't handle non-finite values.
Results may differ from a plain program's by a relative error of at most 0.005.
Values may be sent and summed in bfloat16 or wider, within the bound.
No kernel may reach another device: no remote copies, remote signals or barrier semaphores. Data moves between devices by JAX's collectives and lax.ppermute only.
A program may use at most 128 MiB of HBM per device.

v0:
```python
import math

import jax
import jax.numpy as jnp
from jax import lax
from jax.sharding import PartitionSpec as P

exact_mode = lax.Precision.HIGHEST


def from_partner(block, axis, apart):
    count = lax.axis_size(axis)
    route = []
    for low in range(count):
        high = low | 1 << apart
        if high != low and high < count:
            route += [(low, high), (high, low)]
    return lax.ppermute(block, axis, route)


def complex_times(left_re, left_im, right_re, right_im):
    return (left_re * right_re - left_im * right_im, left_re * right_im + left_im * right_re)


def dft_tables(seq_len):
    ladder = jnp.arange(seq_len, dtype=jnp.int32)
    product = ladder[:, None] * ladder[None, :] % seq_len
    angle = product.astype(jnp.float32) * (2.0 * math.pi / seq_len)
    return (jnp.cos(angle), jnp.sin(angle))


def local_dft(stacked, tables, inverse):
    cos_tab, sin_tab = tables
    rows = stacked.shape[1]
    seq_len = stacked.shape[2]
    flat = stacked.reshape(2 * rows, seq_len)
    first = jnp.dot(flat, cos_tab, precision=exact_mode).reshape(2, rows, seq_len)
    second = jnp.dot(flat, sin_tab, precision=exact_mode).reshape(2, rows, seq_len)
    if inverse:
        real_part = (first[0] - second[1]) / seq_len
        imag_part = (first[1] + second[0]) / seq_len
    else:
        real_part = first[0] + second[1]
        imag_part = first[1] - second[0]
    return jnp.stack([real_part, imag_part])


def pair_twiddle(my_index, bit_level, seq_len):
    stride = 2**bit_level
    within = my_index % stride * seq_len + jnp.arange(seq_len, dtype=jnp.int32)
    angle = within.astype(jnp.float32) * (math.pi / (seq_len * stride))
    high_side = my_index // stride % 2
    return (jnp.cos(angle), -jnp.sin(angle), high_side)


def partner(stacked, bit_level):
    return from_partner(stacked, "seq", bit_level)


def forward_pairs(stacked, tables, my_index, n_seq):
    seq_len = stacked.shape[2]
    for bit_level in reversed(range(n_seq.bit_length() - 1)):
        tw_re, tw_im, high_side = pair_twiddle(my_index, bit_level, seq_len)
        is_high = high_side == 1
        sign = (1 - 2 * high_side).astype(jnp.float32)
        other = partner(stacked, bit_level)
        mixed = other + sign * stacked
        w_re = jnp.where(is_high, tw_re, 1.0)
        w_im = jnp.where(is_high, tw_im, 0.0)
        real_part, imag_part = complex_times(mixed[0], mixed[1], w_re, w_im)
        stacked = jnp.stack([real_part, imag_part])
    return local_dft(stacked, tables, False)


def inverse_pairs(stacked, tables, my_index, n_seq):
    seq_len = stacked.shape[2]
    stacked = local_dft(stacked, tables, True)
    for bit_level in range(n_seq.bit_length() - 1):
        tw_re, tw_im, high_side = pair_twiddle(my_index, bit_level, seq_len)
        is_high = high_side == 1
        sign = (1 - 2 * high_side).astype(jnp.float32)
        w_re = jnp.where(is_high, tw_re, 1.0)
        w_im = jnp.where(is_high, -tw_im, 0.0)
        real_part, imag_part = complex_times(stacked[0], stacked[1], w_re, w_im)
        turned = jnp.stack([real_part, imag_part])
        other = partner(turned, bit_level)
        stacked = 0.5 * (other + sign * turned)
    return stacked


def spread_grads(values, gate_acts, cotangent, filter_taps, n_seq, my_index):
    channels = values.shape[0]
    seq_len = values.shape[1]
    total = seq_len * n_seq
    factor = 1.0 / math.sqrt(total)
    tables = dft_tables(seq_len)
    positions = my_index * seq_len + jnp.arange(seq_len, dtype=jnp.int32)
    angle = positions.astype(jnp.float32) * (math.pi / total)
    shift_re = jnp.cos(angle)
    shift_im = -jnp.sin(angle)
    upstream = cotangent.astype(jnp.float32) * gate_acts.astype(jnp.float32)
    base = jnp.concatenate([filter_taps * factor, values.astype(jnp.float32), upstream], 0)
    stacked = jnp.stack(
        [
            jnp.concatenate([base, base * shift_re], 0),
            jnp.concatenate([jnp.zeros_like(base), base * shift_im], 0),
        ]
    )
    spectra = forward_pairs(stacked, tables, my_index, n_seq)

    def section(index):
        return (
            spectra[0, index * channels : (index + 1) * channels],
            spectra[1, index * channels : (index + 1) * channels],
        )

    real_rows = []
    imag_rows = []
    for half_start in (0, 3):
        kern_re, kern_im = section(half_start)
        sig_re, sig_im = section(half_start + 1)
        grad_re, grad_im = section(half_start + 2)
        conv_re, conv_im = complex_times(kern_re, kern_im, sig_re, sig_im)
        vgrad_re, vgrad_im = complex_times(kern_re, -kern_im, grad_re, grad_im)
        tgrad_re, tgrad_im = complex_times(grad_re, grad_im, sig_re, -sig_im)
        real_rows = real_rows + [conv_re, vgrad_re, tgrad_re]
        imag_rows = imag_rows + [conv_im, vgrad_im, tgrad_im]
    products = jnp.stack([jnp.concatenate(real_rows, 0), jnp.concatenate(imag_rows, 0)])
    signals = inverse_pairs(products, tables, my_index, n_seq)
    width3 = 3 * channels
    merged = 0.5 * (
        signals[0, :width3] + shift_re * signals[0, width3:] + shift_im * signals[1, width3:]
    )
    conv_out = merged[:channels]
    value_grad = merged[channels : 2 * channels].astype(jnp.bfloat16)
    taps_grad = merged[2 * channels :] * factor
    gate_grad = (cotangent.astype(jnp.float32) * conv_out).astype(jnp.bfloat16)
    return (value_grad, gate_grad, taps_grad)


def local(values, gate_acts, cotangent, filter_taps, w_value, w_gate):
    n_seq = lax.axis_size("seq")
    my_index = lax.axis_index("seq")
    value_grad, gate_grad, taps_grad = spread_grads(
        values, gate_acts, cotangent, filter_taps, n_seq, my_index
    )
    got_value, got_gate = (
        lax.all_to_all(value_grad, "chan", split_axis=1, concat_axis=0, tiled=True),
        lax.all_to_all(gate_grad, "chan", split_axis=1, concat_axis=0, tiled=True),
    )
    contract = (((0,), (1,)), ((), ()))
    input_grad = lax.dot_general(got_value, w_value, contract, preferred_element_type=jnp.float32)
    input_grad = input_grad + lax.dot_general(
        got_gate, w_gate, contract, preferred_element_type=jnp.float32
    )
    return (input_grad.astype(jnp.bfloat16), taps_grad)


def solution(mesh):
    return jax.shard_map(
        local,
        mesh=mesh,
        in_specs=(P("chan", "seq"), P("chan", "seq"), P("chan", "seq"), P("chan", "seq"), P(), P()),
        out_specs=(P(("seq", "chan"), None), P("chan", "seq")),
        check_vma=False,
    )
```

profile of v0, /device:TPU:0, one launch (start us, length us, event | category | flops | bytes accessed | tf_op | source)
XLA Modules:
  0.0 531.9 jit_solution(7978439033758660992)
XLA Ops:
  0.7 1.3 copy.15
  2.0 1.2 copy.13
  3.2 1.1 copy.16
  4.3 1.1 copy.14
  6.4 3.4 pad_maximum_fusion
  9.8 0.8 copy-done.2
  10.6 2.9 collective-permute-start
  13.6 135.8 %collective-permute-done = f32[2,768,1024]{1,2,0:T(8,128)} collective-permute-done((f32[2,768,1024]{1,2,0:T(8,128)}, f32[2,768,1024]{1,2,0:T(8,128)}, u32[]{:S(2)}, u32[]{:S(2)}) %collective-permute-start) | collective-permute-done | bytes 6291488 | tf_op jit(solution)/shard_map/ppermute | solution.py:18
  149.4 5.4 %multiply_add_fusion.1 = f32[2,768,1024]{1,2,0:T(8,128)S(1)} fusion(f32[2,768,1024]{1,2,0:T(8,128)} %collective-permute-done, f32[]{:T(128)S(6)} %convert_element_type.80, f32[1,768,1024]{1,2,0:T(8,128)} %copy-done.2, f32[1,768,1024]{1,2,0:T(8,128)} %copy-done.1), kind=kLoop, calls=%fused_computation.12 | loop fusion | flops 4718592 | bytes 18874372 | tf_op jit(solution)/shard_map/add | solution.py:67
  154.8 1.0 multiply_subtract_fusion.2
  155.8 3.3 pad_maximum_fusion.1
  159.4 0.9 copy-done.5
  160.4 16.2 %fusion.70 = f32[1024,1024]{1,0:T(8,128)} fusion(), kind=kLoop, calls=%fused_computation.36.clone.1.clone.1 | loop fusion | flops 14680064 | bytes 4194304 | tf_op jit(solution)/shard_map/dot_general | solution.py:37
  176.6 16.3 %fusion.74 = f32[1024,1024]{1,0:T(8,128)} fusion(), kind=kLoop, calls=%fused_computation.35.clone.1.clone.1 | loop fusion | flops 14680064 | bytes 4194304 | tf_op jit(solution)/shard_map/dot_general | solution.py:38
  192.9 16.2 %fusion.68 = f32[1024,1024]{1,0:T(8,128)} fusion(), kind=kLoop, calls=%fused_computation.36.clone.clone.1 | loop fusion | flops 14680064 | bytes 4194304 | tf_op jit(solution)/shard_map/dot_general | solution.py:37
  209.1 16.3 %fusion.72 = f32[1024,1024]{1,0:T(8,128)} fusion(), kind=kLoop, calls=%fused_computation.35.clone.clone.1 | loop fusion | flops 14680064 | bytes 4194304 | tf_op jit(solution)/shard_map/dot_general | solution.py:38
  225.5 3.9 multiply_add_fusion
  229.4 1.0 multiply_subtract_fusion.1
  230.4 3.0 pad_maximum_fusion.2
  233.4 6.6 %copy.17 = f32[2,768,1024]{2,1,0:T(8,128)} copy(f32[2,768,1024]{1,2,0:T(8,128)} %pad_maximum_fusion.2) | data formatting | bytes 12582912 | tf_op jit(solution)/shard_map/stack | solution.py:71
  240.0 24.2 %fusion.12 = f32[1536,1024]{1,0:T(8,128)S(1)} fusion(f32[1536,1024]{1,0:T(8,128)} %bitcast.182, f32[1024,1024]{1,0:T(8,128)} %fusion.70), kind=kOutput, calls=%fused_computation.38 | convolution fusion | flops 19327352832 | bytes 16777216 | tf_op jit(solution)/shard_map/dot_general | solution.py:37
  264.2 22.5 %fusion.16 = f32[1536,1024]{1,0:T(8,128)} fusion(f32[1536,1024]{1,0:T(8,128)S(1)} %bitcast.183, f32[1024,1024]{1,0:T(8,128)S(1)} %copy-done.11), kind=kOutput, calls=%fused_computation.40 | convolution fusion | flops 19327352832 | bytes 16777216 | tf_op jit(solution)/shard_map/dot_general | solution.py:38
  286.7 4.3 fusion.6
  291.7 0.4 subtract_dynamic-update-slice_fusion.1
  293.2 1.1 pad_maximum_fusion.3
  294.3 1.1 copy-done.10
  295.3 22.1 %fusion.10 = f32[1536,1024]{0,1:T(8,128)S(1)} fusion(f32[1536,1024]{1,0:T(8,128)S(1)} %bitcast.180, f32[1024,1024]{1,0:T(8,128)S(1)} %copy-done.10), kind=kOutput, calls=%fused_computation.37 | convolution fusion | flops 19327352832 | bytes 16777216 | tf_op jit(solution)/shard_map/dot_general | solution.py:37
  317.5 22.0 %fusion.14 = f32[1536,1024]{0,1:T(8,128)S(1)} fusion(f32[1536,1024]{1,0:T(8,128)S(1)} %bitcast.181, f32[1024,1024]{1,0:T(8,128)S(1)} %copy-done.9), kind=kOutput, calls=%fused_computation.39 | convolution fusion | flops 19327352832 | bytes 16777216 | tf_op jit(solution)/shard_map/dot_general | solution.py:38
  339.4 1.3 subtract_bitcast_fusion
  341.1 0.6 collective-permute-start.2
  341.8 9.9 %collective-permute-done.2 = f32[2,768,1024]{1,2,0:T(8,128)} collective-permute-done((f32[2,768,1024]{1,2,0:T(8,128)S(1)}, f32[2,768,1024]{1,2,0:T(8,128)}, u32[]{:S(2)}, u32[]{:S(2)}) %collective-permute-start.2) | collective-permute-done | bytes 6291488 | tf_op jit(solution)/shard_map/ppermute | solution.py:18
  351.6 4.0 add_multiply_fusion.1
  355.7 1.2 multiply_subtract_fusion
  356.9 0.4 pad_maximum_fusion.5
  357.3 1.8 collective-permute-start.3
  359.1 136.1 %collective-permute-done.3 = f32[2,768,1024]{1,2,0:T(8,128)} collective-permute-done((f32[2,768,1024]{1,2,0:T(8,128)S(1)}, f32[2,768,1024]{1,2,0:T(8,128)}, u32[]{:S(2)}, u32[]{:S(2)}) %collective-permute-start.3) | collective-permute-done | bytes 6291488 | tf_op jit(solution)/shard_map/ppermute | solution.py:18
  495.3 4.0 add_multiply_fusion
  499.7 1.2 copy-done.8
  500.9 0.9 copy.18
  501.7 6.1 %all-to-all-start = ((bf16[128,8,128]{2,0,1:T(8,128)(2,1)}), bf16[128,8,128]{2,0,1:T(8,128)(2,1)S(1)}, u32[]{:S(2)}, u32[]{:S(2)}) async-start(bf16[128,8,128]{2,0,1:T(8,128)(2,1)} %copy.18), calls=%async_computation | async-start | bytes 524288 | tf_op jit(solution)/shard_map/all_to_all | solution.py:148
  507.8 1.3 slice_multiply_fusion
  509.1 0.8 copy.19
  509.9 6.5 %all-to-all-done = bf16[128,8,128]{2,0,1:T(8,128)(2,1)S(1)} async-done(((bf16[128,8,128]{2,0,1:T(8,128)(2,1)}), bf16[128,8,128]{2,0,1:T(8,128)(2,1)S(1)}, u32[]{:S(2)}, u32[]{:S(2)}) %all-to-all-start) | async-done | bytes 262176 | tf_op jit(solution)/shard_map/all_to_all | solution.py:148
  516.4 3.6 all-to-all-start.1
  520.0 1.0 copy.20
  521.0 0.8 fusion.47
  521.9 6.7 %all-to-all-done.1 = bf16[128,8,128]{2,0,1:T(8,128)(2,1)S(1)} async-done(((bf16[128,8,128]{2,0,1:T(8,128)(2,1)}), bf16[128,8,128]{2,0,1:T(8,128)(2,1)S(1)}, u32[]{:S(2)}, u32[]{:S(2)}) %all-to-all-start.1) | async-done | bytes 262176 | tf_op jit(solution)/shard_map/all_to_all | solution.py:149
  528.6 3.1 fusion.23
  (44 shorter events, 3.8 us)
Async XLA Ops:
  0.6 520.4 %copy-start = (bf16[1024,1024]{1,0:T(8,128)(2,1)S(1)}, bf16[1024,1024]{1,0:T(8,128)(2,1)}, u32[]{:S(2)}) copy-start(bf16[1024,1024]{1,0:T(8,128)(2,1)} %param.10) | copy-start | bytes 6291460
  6.2 3.7 copy-start.1
  6.4 4.2 copy-start.2
  10.6 138.8 %collective-permute-start = (f32[2,768,1024]{1,2,0:T(8,128)}, f32[2,768,1024]{1,2,0:T(8,128)}, u32[]{:S(2)}, u32[]{:S(2)}) collective-permute-start(f32[2,768,1024]{1,2,0:T(8,128)} %pad_maximum_fusion), channel_id=1, source_target_pairs={{0,16},{16,0},{8,24},{24,8},{1,17},{17,1},{9,25},{25,9},{2,18},{18... | collective-permute-start | bytes 18874376 | tf_op jit(solution)/shard_map/ppermute | solution.py:18
  155.8 3.6 copy-start.3
  155.8 4.4 copy-start.5
  160.3 65.2 %collective-permute-start.1 = (f32[2,768,1024]{1,2,0:T(8,128)}, f32[2,768,1024]{1,2,0:T(8,128)}, u32[]{:S(2)}, u32[]{:S(2)}) collective-permute-start(f32[2,768,1024]{1,2,0:T(8,128)} %pad_maximum_fusion.1), channel_id=1, source_target_pairs={{0,8},{8,0},{16,24},{24,16},{1,9},{9,1},{17,25},{25,17},{2,10},{10... | collective-permute-start | bytes 18874376 | tf_op jit(solution)/shard_map/ppermute | solution.py:18
  192.9 32.5 %copy-start.6 = (f32[1,768,1024]{1,2,0:T(8,128)S(1)}, f32[1,768,1024]{1,2,0:T(8,128)}, u32[]{:S(2)}) copy-start(f32[1,768,1024]{1,2,0:T(8,128)} %copy-done.5) | copy-start | bytes 9437188
  209.1 16.3 %copy-start.4 = (f32[1,768,1024]{1,2,0:T(8,128)S(1)}, f32[1,768,1024]{1,2,0:T(8,128)}, u32[]{:S(2)}) copy-start(f32[1,768,1024]{1,2,0:T(8,128)} %copy-done.3) | copy-start | bytes 9437188
  240.0 24.2 %copy-start.7 = (f32[2,768,1024]{2,1,0:T(8,128)S(1)}, f32[2,768,1024]{2,1,0:T(8,128)}, u32[]{:S(2)}) copy-start(f32[2,768,1024]{2,1,0:T(8,128)} %copy.17) | copy-start | bytes 18874372
  240.0 24.2 %copy-start.11 = (f32[1024,1024]{1,0:T(8,128)S(1)}, f32[1024,1024]{1,0:T(8,128)}, u32[]{:S(2)}) copy-start(f32[1024,1024]{1,0:T(8,128)} %fusion.74) | copy-start | bytes 12582916
  293.1 2.2 copy-start.10
  295.3 22.1 %copy-start.9 = (f32[1024,1024]{1,0:T(8,128)S(1)}, f32[1024,1024]{1,0:T(8,128)}, u32[]{:S(2)}) copy-start(f32[1024,1024]{1,0:T(8,128)} %fusion.72) | copy-start | bytes 12582916
  341.1 10.5 %collective-permute-start.2 = (f32[2,768,1024]{1,2,0:T(8,128)S(1)}, f32[2,768,1024]{1,2,0:T(8,128)}, u32[]{:S(2)}, u32[]{:S(2)}) collective-permute-start(f32[2,768,1024]{1,2,0:T(8,128)S(1)} %pad_maximum_fusion.4), channel_id=1, source_target_pairs={{0,8},{8,0},{16,24},{24,16},{1,9},{9,1},{17,25},{25,17},{2,10},{10... | collective-permute-start | bytes 18874376 | tf_op jit(solution)/shard_map/ppermute | solution.py:18
  357.3 138.0 %collective-permute-start.3 = (f32[2,768,1024]{1,2,0:T(8,128)S(1)}, f32[2,768,1024]{1,2,0:T(8,128)}, u32[]{:S(2)}, u32[]{:S(2)}) collective-permute-start(f32[2,768,1024]{1,2,0:T(8,128)S(1)} %pad_maximum_fusion.5), channel_id=1, source_target_pairs={{0,16},{16,0},{8,24},{24,8},{1,17},{17,1},{9,25},{25,9},{2,18},{18... | collective-permute-start | bytes 18874376 | tf_op jit(solution)/shard_map/ppermute | solution.py:18
  499.7 1.2 copy-start.8
  501.7 14.7 %all-to-all-start = ((bf16[128,8,128]{2,0,1:T(8,128)(2,1)}), bf16[128,8,128]{2,0,1:T(8,128)(2,1)S(1)}, u32[]{:S(2)}, u32[]{:S(2)}) async-start(bf16[128,8,128]{2,0,1:T(8,128)(2,1)} %copy.18), calls=%async_computation | async-start | bytes 524288 | tf_op jit(solution)/shard_map/all_to_all | solution.py:148
  516.4 12.1 %all-to-all-start.1 = ((bf16[128,8,128]{2,0,1:T(8,128)(2,1)}), bf16[128,8,128]{2,0,1:T(8,128)(2,1)S(1)}, u32[]{:S(2)}, u32[]{:S(2)}) async-start(bf16[128,8,128]{2,0,1:T(8,128)(2,1)} %copy.19), calls=%async_computation.1 | async-start | bytes 524288 | tf_op jit(solution)/shard_map/all_to_all | solution.py:149
where the time goes:
time: 540 us; the launch traced here: 532 us
  waiting for transfers between devices  295 us (55%)
  other arithmetic  107 us (20%)
  matrix products  94.7 us (18%)
  local copies, waits for them, and re-layouts  18.5 us (3%)
  starting transfers between devices  15 us (3%)
    ppermute x4, waiting for transfers between devices, from_partner(): return lax.ppermute(block, axis, route)  282 us
    dot_general x2, matrix products, local_dft(): jnp.dot(flat, cos_tab, precision=exact_mode).reshape(2, rows, seq_len)  46.3 us
    dot_general x2, matrix products, local_dft(): jnp.dot(flat, sin_tab, precision=exact_mode).reshape(2, rows, seq_len)  44.5 us
    dot_general x2, other arithmetic, local_dft(): jnp.dot(flat, sin_tab, precision=exact_mode).reshape(2, rows, seq_len)  32.7 us
    dot_general x2, other arithmetic, local_dft(): jnp.dot(flat, cos_tab, precision=exact_mode).reshape(2, rows, seq_len)  32.4 us
  transfers between devices with their start and end apart: 6, of which 5 were waited for; matrix products, arithmetic and copies ran while one was open for 13% of the time, Pallas kernels for 0%

commit v1 on v0

v1 whole, which is shorter than its diff:
```python
import functools
import math

import jax
import jax.numpy as jnp
import numpy as np
from jax import lax
from jax.experimental import pallas as pl
from jax.experimental.pallas import tpu as pltpu
from jax.sharding import PartitionSpec as P

LANES = 128
VALUE, TAPS, COT, GATE = range(4)


def halves(table):
    high = table.astype(jnp.bfloat16)
    low = (table - high.astype(np.float64)).astype(jnp.bfloat16)
    return high, low


def dft_tables(total):
    outer = total // LANES
    k1 = np.arange(outer) + 0.25
    a = np.arange(outer)
    b = np.arange(LANES)
    first = np.exp(-2j * np.pi * np.outer(k1, a) / outer)
    first = np.concatenate([first.real, first.imag], 0)
    turn = np.exp(-2j * np.pi * np.outer(k1, b) / total)
    second = np.exp(-2j * np.pi * np.outer(b, b) / LANES)
    second = np.block([[second.real, second.imag], [-second.imag, second.real]])
    back_second = second.T / total / math.sqrt(total)
    back_first = np.exp(2j * np.pi * np.outer(a, k1) / outer)
    back_first = np.concatenate([back_first.real, -back_first.imag], 1)

    f_hi, f_lo = halves(first)
    s_hi, s_lo = halves(second)
    bs_hi, bs_lo = halves(back_second)
    bf_hi, bf_lo = halves(back_first)
    return (
        np.concatenate([f_hi, f_lo], 1),
        np.concatenate([f_hi, f_hi, f_lo], 1),
        np.concatenate([s_hi, s_hi, s_lo], 0),
        turn.real.astype(np.float32),
        turn.imag.astype(np.float32),
        np.concatenate([bs_hi, bs_hi, bs_lo], 0),
        np.concatenate([bf_hi, bf_hi, bf_lo], 1),
    )


def split_terms(x):
    high = x.astype(jnp.bfloat16)
    low = (x - high.astype(jnp.float32)).astype(jnp.bfloat16)
    return high, low


def dot(left, right):
    return jnp.dot(left, right, preferred_element_type=jnp.float32)


def wide_dot(x, table):
    high, low = split_terms(x)
    return dot(jnp.concatenate([high, low, high], 1), table)


def mixer_kernel(
    n_seq,
    group,
    *rest,
):
    blocks = rest[:n_seq]
    f2, f3, s3, turn_re, turn_im, bs3, bf3 = rest[n_seq : n_seq + 7]
    grads, taps_out = rest[n_seq + 7 : n_seq + 9]
    sig, taps, up, cot, grads32, taps32 = rest[n_seq + 9 :]
    me = lax.axis_index("seq")
    _, channels, seq_len = blocks[0].shape
    outer = sig.shape[0] // channels
    own_outer = seq_len // LANES

    for k in range(n_seq):
        source = lax.bitwise_xor(me, k)
        for part in range(own_outer):
            cols = pl.ds(part * LANES, LANES)
            v, f, c, g = (blocks[k][i, :, cols].astype(jnp.float32) for i in range(4))
            rows = pl.ds(source * own_outer + part, channels, stride=outer)
            sig[rows, :] = v
            taps[rows, :] = f
            up[rows, :] = c * g
            cot[rows, :] = c

    def some(step, carry):
        base = step * group
        tr, ti = turn_re[...], turn_im[...]

        def forward(ref, exact):
            turned = []
            for pair in range(group // 2):
                xs = [
                    ref[pl.ds(pl.multiple_of((base + 2 * pair + i) * outer, outer), outer), :]
                    for i in range(2)
                ]
                x = jnp.concatenate(xs, 1)
                if exact:
                    high = x.astype(jnp.bfloat16)
                    y = dot(f2[...], jnp.concatenate([high, high], 0))
                else:
                    high, low = split_terms(x)
                    y = dot(f3[...], jnp.concatenate([high, low, high], 0))
                for i in range(2):
                    re = y[:outer, i * LANES : (i + 1) * LANES]
                    im = y[outer:, i * LANES : (i + 1) * LANES]
                    turned.append(jnp.concatenate([re * tr - im * ti, re * ti + im * tr], 1))
            spec = wide_dot(jnp.concatenate(turned, 0), s3[...])
            return spec[:, :LANES], spec[:, LANES:]

        def backward(re, im):
            mid = wide_dot(jnp.concatenate([re, im], 1), bs3[...])
            for pair in range(group // 2):
                cols = []
                for i in range(2):
                    rows = slice((2 * pair + i) * outer, (2 * pair + i + 1) * outer)
                    re, im = mid[rows, :LANES], mid[rows, LANES:]
                    cols.append(jnp.concatenate([re * tr + im * ti, im * tr - re * ti], 0))
                high, low = split_terms(jnp.concatenate(cols, 1))
                y = dot(bf3[...], jnp.concatenate([high, low, high], 0))
                for i in range(2):
                    yield base + 2 * pair + i, y[:, i * LANES : (i + 1) * LANES]

        kr, ki = forward(taps, True)
        vr, vi = forward(sig, True)
        ur, ui = forward(up, False)
        for ch, y in backward(kr * vr - ki * vi, kr * vi + ki * vr):
            held = cot[pl.ds(pl.multiple_of(ch * outer, outer), outer), :]
            grads32[pl.ds(channels + ch, outer, stride=2 * channels), :] = y * held
        for ch, y in backward(kr * ur + ki * ui, kr * ui - ki * ur):
            grads32[pl.ds(ch, outer, stride=2 * channels), :] = y
        for ch, y in backward(ur * vr + ui * vi, ui * vr - ur * vi):
            taps32[pl.ds(ch, outer, stride=channels), :] = y
        return carry

    lax.fori_loop(0, channels // group, some, 0)

    for a in range(outer):
        grads[a] = grads32[a * 2 * channels : (a + 1) * 2 * channels, :].astype(jnp.bfloat16)
    for k in range(n_seq):
        source = lax.bitwise_xor(me, k)
        for part in range(own_outer):
            start = pl.multiple_of((source * own_outer + part) * channels, channels)
            taps_out[k, :, pl.ds(part * LANES, LANES)] = taps32[pl.ds(start, channels), :].astype(jnp.bfloat16)


def project_kernel(n_seq, n_chan, grads, w_value, w_gate, own_taps, *rest):
    taps_in = rest[: n_seq - 1]
    out, taps_out, held = rest[n_seq - 1 :]
    me = lax.axis_index("seq")
    share = own_taps.shape[1]
    for s in range(n_seq):
        for c in range(n_chan):
            for g in range(2):
                held[g, pl.ds((c * n_seq + s) * share, share), :] = grads[
                    s * n_chan + c, g * share : (g + 1) * share, :
                ].astype(held.dtype)
    sides = [held[g].astype(jnp.bfloat16) for g in range(2)]
    total = dot(w_value[...], sides[0]) + dot(w_gate[...], sides[1])
    out[...] = total.T.astype(jnp.bfloat16)
    for k in range(n_seq):
        got = own_taps[0] if k == 0 else taps_in[k - 1][...]
        taps_out[lax.bitwise_xor(me, k)] = got.astype(jnp.float32)


def local(n_seq, n_chan, values, gate_acts, cotangent, filter_taps, w_value, w_gate):
    rows, seq_len = values.shape
    total = seq_len * n_seq
    channels = rows // n_seq
    outer = total // LANES
    tokens = total // (n_seq * n_chan)
    group = min(8, channels)
    me = lax.axis_index("seq")
    vmem = pl.BlockSpec(memory_space=pltpu.VMEM)

    taps16 = filter_taps.astype(jnp.bfloat16)
    fields = (values, taps16, cotangent, gate_acts)

    def route(k):
        return [(i, i ^ k) for i in range(n_seq)]

    got = {}
    for k in reversed(range(n_seq)):
        start = (me ^ k) * channels
        block = jnp.stack([lax.dynamic_slice_in_dim(x, start, channels, 0) for x in fields])
        got[k] = lax.ppermute(block, "seq", route(k)) if k else block

    tables = [jnp.asarray(t) for t in dft_tables(total)]
    args = [*(got[k] for k in range(n_seq)), *tables]
    long = pltpu.VMEM((channels * outer, LANES), jnp.float32)
    grads, taps_blocks = pl.pallas_call(
        functools.partial(mixer_kernel, n_seq, group),
        out_shape=(
            jax.ShapeDtypeStruct((outer, 2 * channels, LANES), jnp.bfloat16),
            jax.ShapeDtypeStruct((n_seq, channels, seq_len), jnp.bfloat16),
        ),
        in_specs=[vmem] * len(args),
        out_specs=(vmem, vmem),
        scratch_shapes=[long] * 4 + [pltpu.VMEM((2 * channels * outer, LANES), jnp.float32), long],
        compiler_params=pltpu.CompilerParams(vmem_limit_bytes=48 * 2**20),
        name="mixer",
    )(*args)

    if tokens != LANES:
        grads = grads.reshape(outer, 2 * channels, LANES // tokens, tokens).transpose(0, 2, 1, 3)
        grads = grads.reshape(n_seq * n_chan, 2 * channels, tokens)
    spread = lax.all_to_all(grads, ("seq", "chan"), 0, 0, tiled=True)
    taps_got = [lax.ppermute(taps_blocks[k], "seq", route(k)) for k in range(1, n_seq)]

    features = w_value.shape[0]
    args = [spread, w_value, w_gate, taps_blocks, *taps_got]
    held = jnp.bfloat16 if channels % 16 == 0 else jnp.float32
    input_grad, taps_grad = pl.pallas_call(
        functools.partial(project_kernel, n_seq, n_chan),
        out_shape=(
            jax.ShapeDtypeStruct((tokens, features), jnp.bfloat16),
            jax.ShapeDtypeStruct((n_seq, channels, seq_len), jnp.float32),
        ),
        in_specs=[vmem] * len(args),
        out_specs=(vmem, vmem),
        scratch_shapes=[pltpu.VMEM((2, rows * n_chan, tokens), held)],
        compiler_params=pltpu.CompilerParams(vmem_limit_bytes=32 * 2**20),
        name="project",
    )(*args)
    return input_grad, taps_grad.reshape(rows, seq_len)


def solution(mesh):
    return jax.shard_map(
        functools.partial(local, mesh.shape["seq"], mesh.shape["chan"]),
        mesh=mesh,
        in_specs=(P("chan", "seq"), P("chan", "seq"), P("chan", "seq"), P("chan", "seq"), P(), P()),
        out_specs=(P(("seq", "chan"), None), P("chan", "seq")),
        check_vma=False,
    )
```

time: 540 us -> 55.1 us (0.10); the launches traced: 532 us -> 54.8 us
  waiting for transfers between devices: 295 us -> 25.2 us
  other arithmetic: 107 us -> 1.22 us
  matrix products: 94.7 us -> 0 us
  local copies, waits for them, and re-layouts: 18.5 us -> 3.82 us
  Pallas kernels: 0 us -> 12.3 us
    ppermute x4 -> x6, waiting for transfers between devices: 282 us -> 18.2 us  [the longest x3 10.8 us: local(): got[k] = lax.ppermute(block, 'seq', route(k)) if k else block]
    dot_general x6 -> x0, matrix products: 94.7 us -> none  [the longest x2 46.3 us: local_dft(): jnp.dot(flat, cos_tab, precision=exact_mode).reshape(2, rows, seq_len)]
    dot_general x4 -> x0, other arithmetic: 65.1 us -> none  [the longest x2 32.7 us: local_dft(): jnp.dot(flat, sin_tab, precision=exact_mode).reshape(2, rows, seq_len)]
    pallas_call x0 -> x2, Pallas kernels: none -> 12.3 us  [the longest x1 10 us: local(): pl.pallas_call(functools.partial(mixer_kernel, n_seq, group), out_shape=(...]
    another operation x7 -> x4, other arithmetic: 11.9 us -> 0.14 us  [local(): jnp.stack([lax.dynamic_slice_in_dim(x, start, channels, 0) for x in fields])]
    mul x7 -> x0, other arithmetic: 10.2 us -> none  [the longest x2 8.08 us: inverse_pairs(): stacked = 0.5 * (other + sign * turned)]
    add x2 -> x0, other arithmetic: 9.35 us -> none  [forward_pairs(): mixed = other + sign * stacked]
    sub x5 -> x0, other arithmetic: 8.79 us -> none  [the longest x4 4.47 us: complex_times(): left_re * right_re - left_im * right_im]
  transfers between devices with their start and end apart: 6 -> 7, of which waited for: 5 -> 5; matrix products, arithmetic and copies ran while one was open for 13% -> 0% of each run, Pallas kernels for 0% -> 0%
where the time goes in v1:
time: 55.1 us; the launch traced here: 54.8 us
  waiting for transfers between devices  25.2 us (46%)
  Pallas kernels  12.3 us (22%)
  starting transfers between devices  11.5 us (21%)
  local copies, waits for them, and re-layouts  3.82 us (7%)
  other arithmetic  1.22 us (2%)
  between operations  0.83 us (2%)
    ppermute x3, waiting for transfers between devices, local(): got[k] = lax.ppermute(block, 'seq', route(k)) if k else block  10.8 us
    pallas_call x1, Pallas kernels, local(): pl.pallas_call(functools.partial(mixer_kernel, n_seq, group), out_shape=(...  10 us
    ppermute x3, waiting for transfers between devices, local(): lax.ppermute(taps_blocks[k], 'seq', route(k))  7.37 us
    all_to_all x1, waiting for transfers between devices, local(): spread = lax.all_to_all(grads, ('seq', 'chan'), 0, 0, tiled=True)  6.99 us
    all_to_all x1, starting transfers between devices, local(): spread = lax.all_to_all(grads, ('seq', 'chan'), 0, 0, tiled=True)  6.28 us
    ppermute x3, starting transfers between devices, local(): got[k] = lax.ppermute(block, 'seq', route(k)) if k else block  3.24 us
    pallas_call x1, Pallas kernels, local(): pl.pallas_call(functools.partial(project_kernel, n_seq, n_chan), out_shap...  2.22 us
    another operation x2, local copies, waits for them, and re-layouts, local(): jnp.stack([lax.dynamic_slice_in_dim(x, start, channels, 0) for x in fields])  2.16 us
  transfers between devices with their start and end apart: 7, of which 5 were waited for; matrix products, arithmetic and copies ran while one was open for 0% of the time, Pallas kernels for 0%

profile of v1, /device:TPU:0, one launch (start us, length us, event | category | flops | bytes accessed | tf_op | source)
XLA Modules:
  0.0 54.8 jit_solution(16719407849000842704)
XLA Ops:
  0.6 1.1 %convert_element_type.3 = bf16[128,1024]{1,0:T(8,128)(2,1)S(1)} convert(f32[128,1024]{1,0:T(8,128)} %param.16) | non-fusion elementwise | flops 131072 | bytes 786432 | tf_op jit(solution)/shard_map/convert_element_type | solution.py:181
  1.7 0.0 copy-start.2
  1.8 0.0 copy-start.3
  1.8 0.0 copy-start.4
  1.8 0.0 copy-start.5
  1.8 0.0 copy-start.6
  1.8 0.0 copy-start.7
  1.8 0.0 copy-start.8
  1.8 1.0 %dynamic-slice_bitcast_fusion.2 = (bf16[1,32,1024]{2,1,0:T(8,128)(2,1)S(1)}, bf16[1,32,1024]{2,1,0:T(8,128)(2,1)S(1)}, bf16[1,32,1024]{2,1,0:T(8,128)(2,1)S(1)},...) fusion(bf16[128,1024]{1,0:T(8,128)(2,1)S(1)} %convert_element_t, ...), kind=kLoop, calls=%fused_computation.9 | loop fusion | bytes 1048592 | tf_op jit(solution)/shard_map/stack | solution.py:190
  2.9 1.1 %dynamic-slice_bitcast_fusion = (bf16[1,32,1024]{2,1,0:T(8,128)(2,1)S(1)}, bf16[1,32,1024]{2,1,0:T(8,128)(2,1)S(1)}, bf16[1,32,1024]{2,1,0:T(8,128)(2,1)S(1)}, b...) fusion(bf16[128,1024]{1,0:T(8,128)(2,1)} %param.14, ...), kind=kLoop, calls=%fused_computation.7 | loop fusion | bytes 1048592 | tf_op jit(solution)/shard_map/stack | solution.py:190
  4.1 3.0 %collective-permute-start.1 = (bf16[4,32,1024]{2,1,0:T(8,128)(2,1)S(1)}, bf16[4,32,1024]{2,1,0:T(8,128)(2,1)S(1)}, u32[]{:S(2)}, u32[]{:S(2)}) collective-permute-start(bf16[4,32,1024]{2,1,0:T(8,128)(2,1)S(1)} %pad_maximum_fusion.2), channel_id=1, source_target_pairs={{0,16},{8,24},{16,0},{24,8},{1,17},{9,25},{17,1},{25,9},{2,18},{10... | collective-permute-start | bytes 786440 | tf_op jit(solution)/shard_map/ppermute | solution.py:191
  7.1 0.1 collective-permute-start
  7.2 0.0 copy-start
  7.2 0.2 collective-permute-start.2
  7.4 6.8 %collective-permute-done.1.rest_2_ = bf16[4,32,1024]{2,1,0:T(8,128)(2,1)S(1)} collective-permute-done((bf16[4,32,1024]{2,1,0:T(8,128)(2,1)S(1)}, bf16[4,32,1024]{2,1,0:T(8,128)(2,1)S(1)}, u32[]{:S(2)}, u32[]{:S(2)}) %collective-permute-start.1) | collective-permute-done | bytes 262176 | tf_op jit(solution)/shard_map/ppermute | solution.py:191
  14.2 0.0 collective-permute-done.rest_1_
  14.2 4.0 %collective-permute-done.2.rest_3_ = bf16[4,32,1024]{2,1,0:T(8,128)(2,1)S(1)} collective-permute-done((bf16[4,32,1024]{2,1,0:T(8,128)(2,1)S(1)}, bf16[4,32,1024]{2,1,0:T(8,128)(2,1)S(1)}, u32[]{:S(2)}, u32[]{:S(2)}) %collective-permute-start.2) | collective-permute-done | bytes 262176 | tf_op jit(solution)/shard_map/ppermute | solution.py:191
  18.2 0.0 copy-done.2
  18.2 0.0 copy-done.3
  18.2 0.0 copy-done.4
  18.2 0.0 copy-done.5
  18.3 0.0 copy-done.6
  18.3 0.0 copy-done.7
  18.3 0.0 copy-done.8
  18.3 10.0 %mixer.1 = (bf16[32,64,128]{2,1,0:T(8,128)(2,1)}, bf16[4,32,1024]{2,1,0:T(8,128)(2,1)S(1)}) custom-call(bf16[4,32,1024]{2,1,0:T(8,128)(2,1)S(1)} %pad_maximum_fusion.rest_0_, bf16[4,32,1024]{2,1,0:T(8,128)(2,1)S(1)} %collective-permute-done.rest_1_, bf16[4,32,1024]{2,1,0:T(8,128)(2,1)S(1)} %collective-permute-done.1.rest_2_, ...), custom_call_target="tpu_custom_call" | custom-call | tf_op jit(solution)/shard_map/mixer/pallas_call | solution.py:196
  28.3 6.3 %all-to-all-start = ((bf16[32,64,128]{2,1,0:T(8,128)(2,1)}), bf16[32,64,128]{2,1,0:T(8,128)(2,1)S(1)}, u32[]{:S(2)}, u32[]{:S(2)}) async-start(bf16[32,64,128]{2,1,0:T(8,128)(2,1)} %get-tuple-element.6), calls=%async_computation | async-start | bytes 1048576 | tf_op jit(solution)/shard_map/all_to_all | solution.py:212
  34.6 1.6 %collective-permute-start.5 = (bf16[32,1024]{1,0:T(8,128)(2,1)S(1)}, bf16[32,1024]{1,0:T(8,128)(2,1)S(1)}, u32[]{:S(2)}, u32[]{:S(2)}) collective-permute-start(bf16[32,1024]{1,0:T(8,128)(2,1)S(1)} %get-tuple-element.10), channel_id=1, source_target_pairs={{0,24},{8,16},{16,8},{24,0},{1,25},{9,17},{17,9},{25,1},{2,26},{10... | collective-permute-start | bytes 196616 | tf_op jit(solution)/shard_map/ppermute | solution.py:213
  36.2 0.4 collective-permute-start.4
  36.6 0.0 collective-permute-start.3
  36.6 4.6 %collective-permute-done.5.rest_2_ = bf16[32,1024]{1,0:T(8,128)(2,1)S(1)} collective-permute-done((bf16[32,1024]{1,0:T(8,128)(2,1)S(1)}, bf16[32,1024]{1,0:T(8,128)(2,1)S(1)}, u32[]{:S(2)}, u32[]{:S(2)}) %collective-permute-start.5) | collective-permute-done | bytes 65568 | tf_op jit(solution)/shard_map/ppermute | solution.py:213
  41.2 2.7 %collective-permute-done.4.rest_1_ = bf16[32,1024]{1,0:T(8,128)(2,1)S(1)} collective-permute-done((bf16[32,1024]{1,0:T(8,128)(2,1)S(1)}, bf16[32,1024]{1,0:T(8,128)(2,1)S(1)}, u32[]{:S(2)}, u32[]{:S(2)}) %collective-permute-start.4) | collective-permute-done | bytes 65568 | tf_op jit(solution)/shard_map/ppermute | solution.py:213
  44.0 0.0 collective-permute-done.3.rest_0_
  44.0 7.0 %all-to-all-done.grads = bf16[32,64,128]{2,1,0:T(8,128)(2,1)S(1)} async-done(((bf16[32,64,128]{2,1,0:T(8,128)(2,1)}), bf16[32,64,128]{2,1,0:T(8,128)(2,1)S(1)}, u32[]{:S(2)}, u32[]{:S(2)}) %all-to-all-start) | async-done | bytes 524320 | tf_op jit(solution)/shard_map/all_to_all | solution.py:212
  51.0 0.0 copy-done
  51.0 0.0 copy-start.1
  51.0 1.6 %copy-done.1 = bf16[1024,1024]{1,0:T(8,128)(2,1)S(1)} copy-done((bf16[1024,1024]{1,0:T(8,128)(2,1)S(1)}, bf16[1024,1024]{1,0:T(8,128)(2,1)}, u32[]{:S(2)}) %copy-start.1) | copy-done | bytes 2097176
  52.6 2.2 %project.1 = (bf16[128,1024]{1,0:T(8,128)(2,1)}, f32[4,32,1024]{2,1,0:T(8,128)}) custom-call(bf16[32,64,128]{2,1,0:T(8,128)(2,1)S(1)} %all-to-all-done.grads, bf16[1024,1024]{1,0:T(8,128)(2,1)S(1)} %copy-done, bf16[1024,1024]{1,0:T(8,128)(2,1)S(1)} %copy-done.1, bf16[4,32,1024]{2,1,0:T(8,128)(2,1)S(1)} %get-tuple-element.7.own_taps, ...), custom_call_target="tpu_custom_call" | custom-call | tf_op jit(solution)/shard_map/project/pallas_call | solution.py:218
  (5 shorter events, 0.2 us)
Async XLA Ops:
  1.7 16.5 %copy-start.2 = (bf16[768,256]{1,0:T(8,128)(2,1)S(1)}, bf16[768,256]{1,0:T(8,128)(2,1)}, u32[]{:S(2)}) copy-start(bf16[768,256]{1,0:T(8,128)(2,1)} %constant.36.clone.rest_9_) | copy-start | bytes 1179652
  1.8 16.5 %copy-start.3 = (bf16[768,256]{1,0:T(8,128)(2,1)S(1)}, bf16[768,256]{1,0:T(8,128)(2,1)}, u32[]{:S(2)}) copy-start(bf16[768,256]{1,0:T(8,128)(2,1)} %constant.33.clone.rest_6_) | copy-start | bytes 1179652
  1.8 16.5 %copy-start.4 = (bf16[32,192]{1,0:T(8,128)(2,1)S(1)}, bf16[32,192]{1,0:T(8,128)(2,1)}, u32[]{:S(2)}) copy-start(bf16[32,192]{1,0:T(8,128)(2,1)} %constant.37.clone.rest_10_) | copy-start | bytes 36868
  1.8 16.5 %copy-start.5 = (f32[32,128]{1,0:T(8,128)S(1)}, f32[32,128]{1,0:T(8,128)}, u32[]{:S(2)}) copy-start(f32[32,128]{1,0:T(8,128)} %constant.35.clone.rest_8_) | copy-start | bytes 49156
  1.8 16.5 %copy-start.6 = (f32[32,128]{1,0:T(8,128)S(1)}, f32[32,128]{1,0:T(8,128)}, u32[]{:S(2)}) copy-start(f32[32,128]{1,0:T(8,128)} %constant.34.clone.rest_7_) | copy-start | bytes 49156
  1.8 16.5 %copy-start.7 = (bf16[64,96]{1,0:T(8,128)(2,1)S(1)}, bf16[64,96]{1,0:T(8,128)(2,1)}, u32[]{:S(2)}) copy-start(bf16[64,96]{1,0:T(8,128)(2,1)} %constant.32.clone.rest_5_) | copy-start | bytes 36868
  1.8 16.5 %copy-start.8 = (bf16[64,64]{1,0:T(8,128)(2,1)S(1)}, bf16[64,64]{1,0:T(8,128)(2,1)}, u32[]{:S(2)}) copy-start(bf16[64,64]{1,0:T(8,128)(2,1)} %constant.31.clone.rest_4_) | copy-start | bytes 24580
  4.1 10.1 %collective-permute-start.1 = (bf16[4,32,1024]{2,1,0:T(8,128)(2,1)S(1)}, bf16[4,32,1024]{2,1,0:T(8,128)(2,1)S(1)}, u32[]{:S(2)}, u32[]{:S(2)}) collective-permute-start(bf16[4,32,1024]{2,1,0:T(8,128)(2,1)S(1)} %pad_maximum_fusion.2), channel_id=1, source_target_pairs={{0,16},{8,24},{16,0},{24,8},{1,17},{9,25},{17,1},{25,9},{2,18},{10... | collective-permute-start | bytes 786440 | tf_op jit(solution)/shard_map/ppermute | solution.py:191
  7.1 7.1 %collective-permute-start = (bf16[4,32,1024]{2,1,0:T(8,128)(2,1)S(1)}, bf16[4,32,1024]{2,1,0:T(8,128)(2,1)S(1)}, u32[]{:S(2)}, u32[]{:S(2)}) collective-permute-start(bf16[4,32,1024]{2,1,0:T(8,128)(2,1)S(1)} %pad_maximum_fusion.1), channel_id=1, source_target_pairs={{0,8},{8,0},{16,24},{24,16},{1,9},{9,1},{17,25},{25,17},{2,10},{10... | collective-permute-start | bytes 786440 | tf_op jit(solution)/shard_map/ppermute | solution.py:191
  7.2 43.8 %copy-start = (bf16[1024,1024]{1,0:T(8,128)(2,1)S(1)}, bf16[1024,1024]{1,0:T(8,128)(2,1)}, u32[]{:S(2)}) copy-start(bf16[1024,1024]{1,0:T(8,128)(2,1)} %w_value.1) | copy-start | bytes 6291460
  7.2 11.0 %collective-permute-start.2 = (bf16[4,32,1024]{2,1,0:T(8,128)(2,1)S(1)}, bf16[4,32,1024]{2,1,0:T(8,128)(2,1)S(1)}, u32[]{:S(2)}, u32[]{:S(2)}) collective-permute-start(bf16[4,32,1024]{2,1,0:T(8,128)(2,1)S(1)} %pad_maximum_fusion.3), channel_id=1, source_target_pairs={{0,24},{8,16},{16,8},{24,0},{1,25},{9,17},{17,9},{25,1},{2,26},{10... | collective-permute-start | bytes 786440 | tf_op jit(solution)/shard_map/ppermute | solution.py:191
  28.3 22.6 %all-to-all-start = ((bf16[32,64,128]{2,1,0:T(8,128)(2,1)}), bf16[32,64,128]{2,1,0:T(8,128)(2,1)S(1)}, u32[]{:S(2)}, u32[]{:S(2)}) async-start(bf16[32,64,128]{2,1,0:T(8,128)(2,1)} %get-tuple-element.6), calls=%async_computation | async-start | bytes 1048576 | tf_op jit(solution)/shard_map/all_to_all | solution.py:212
  34.6 6.6 %collective-permute-start.5 = (bf16[32,1024]{1,0:T(8,128)(2,1)S(1)}, bf16[32,1024]{1,0:T(8,128)(2,1)S(1)}, u32[]{:S(2)}, u32[]{:S(2)}) collective-permute-start(bf16[32,1024]{1,0:T(8,128)(2,1)S(1)} %get-tuple-element.10), channel_id=1, source_target_pairs={{0,24},{8,16},{16,8},{24,0},{1,25},{9,17},{17,9},{25,1},{2,26},{10... | collective-permute-start | bytes 196616 | tf_op jit(solution)/shard_map/ppermute | solution.py:213
  36.2 7.7 %collective-permute-start.4 = (bf16[32,1024]{1,0:T(8,128)(2,1)S(1)}, bf16[32,1024]{1,0:T(8,128)(2,1)S(1)}, u32[]{:S(2)}, u32[]{:S(2)}) collective-permute-start(bf16[32,1024]{1,0:T(8,128)(2,1)S(1)} %get-tuple-element.11), channel_id=1, source_target_pairs={{0,16},{8,24},{16,0},{24,8},{1,17},{9,25},{17,1},{25,9},{2,18},{10... | collective-permute-start | bytes 196616 | tf_op jit(solution)/shard_map/ppermute | solution.py:213
  36.6 7.4 %collective-permute-start.3 = (bf16[32,1024]{1,0:T(8,128)(2,1)S(1)}, bf16[32,1024]{1,0:T(8,128)(2,1)S(1)}, u32[]{:S(2)}, u32[]{:S(2)}) collective-permute-start(bf16[32,1024]{1,0:T(8,128)(2,1)S(1)} %get-tuple-element.12), channel_id=1, source_target_pairs={{0,8},{8,0},{16,24},{24,16},{1,9},{9,1},{17,25},{25,17},{2,10},{10... | collective-permute-start | bytes 196616 | tf_op jit(solution)/shard_map/ppermute | solution.py:213
  51.0 1.6 %copy-start.1 = (bf16[1024,1024]{1,0:T(8,128)(2,1)S(1)}, bf16[1024,1024]{1,0:T(8,128)(2,1)}, u32[]{:S(2)}) copy-start(bf16[1024,1024]{1,0:T(8,128)(2,1)} %w_gate.1) | copy-start | bytes 6291460

commit v2 on v1

v2 whole, which is shorter than its diff:
```python
import functools
import math

import jax
import jax.numpy as jnp
import numpy as np
from jax import lax
from jax.experimental import pallas as pl
from jax.experimental.pallas import tpu as pltpu
from jax.sharding import PartitionSpec as P

LANES = 128
VALUE, TAPS, COT, GATE = range(4)
CHUNKS = 2
ONE_SPREAD = True
SLABS = 8
KEPT = 3
PAD = 8


def halves(table):
    high = table.astype(jnp.bfloat16)
    low = (table - high.astype(np.float64)).astype(jnp.bfloat16)
    return high, low


def dft_tables(total):
    outer = total // LANES
    k1 = np.arange(outer) + 0.25
    a = np.arange(outer)
    b = np.arange(LANES)
    first = np.exp(-2j * np.pi * np.outer(k1, a) / outer)
    first = np.concatenate([first.real, first.imag], 0)
    turn = np.exp(-2j * np.pi * np.outer(k1, b) / total)
    second = np.exp(-2j * np.pi * np.outer(b, b) / LANES)
    second = np.block([[second.real, second.imag], [-second.imag, second.real]])
    back_second = second.T / total / math.sqrt(total)
    back_first = np.exp(2j * np.pi * np.outer(a, k1) / outer)
    back_first = np.concatenate([back_first.real, -back_first.imag], 1)

    f_hi, f_lo = halves(first)
    s_hi, s_lo = halves(second)
    bs_hi, bs_lo = halves(back_second)
    bf_hi, bf_lo = halves(back_first)
    return (
        np.concatenate([f_hi, f_lo], 1),
        np.concatenate([f_hi, f_hi, f_lo], 1),
        np.concatenate([s_hi, s_hi, s_lo], 0),
        turn.real.astype(np.float32),
        turn.imag.astype(np.float32),
        np.concatenate([bs_hi, bs_hi, bs_lo], 0),
        np.concatenate([bf_hi, bf_hi, bf_lo], 1),
    )


def split_terms(x):
    high = x.astype(jnp.bfloat16)
    low = (x - high.astype(jnp.float32)).astype(jnp.bfloat16)
    return high, low


def dot(left, right):
    return jnp.dot(left, right, preferred_element_type=jnp.float32)


def wide_dot(x, table):
    high, low = split_terms(x)
    return dot(jnp.concatenate([high, low, high], 1), table)


def prep_kernel(n_seq, n_tables, values, filter_taps, cotangent, gate_acts, *rest):
    tables, rest = rest[:n_tables], rest[n_tables:]
    outs, held, (wide, sems, table_sems) = rest[: -n_tables - 3], rest[-n_tables - 3 : -3], rest[-3:]
    me = lax.axis_index("seq")
    chunks = len(outs) // n_seq
    rows = outs[0].shape[1]
    fields = {VALUE: values, COT: cotangent, GATE: gate_acts}
    copies = []
    for chunk in range(chunks):
        for k in reversed(range(n_seq)):
            at = chunk * n_seq + k
            start = pl.multiple_of((lax.bitwise_xor(me, k) * chunks + chunk) * rows, rows)
            mine = pl.ds(start, rows)
            copies.append([pltpu.make_async_copy(filter_taps.at[mine, :], wide.at[at], sems.at[at, TAPS])])
            for field, ref in fields.items():
                copies[-1].append(pltpu.make_async_copy(ref.at[mine, :], outs[at].at[field], sems.at[at, field]))
            for copy in copies[-1]:
                copy.start()
    brought = [pltpu.make_async_copy(tables[i], held[i], table_sems.at[i]) for i in range(n_tables)]
    for copy in brought:
        copy.start()
    for chunk in range(chunks):
        for k in reversed(range(n_seq)):
            at = chunk * n_seq + k
            group = copies[chunk * n_seq + n_seq - 1 - k]
            group[0].wait()
            outs[at][TAPS] = wide[at].astype(jnp.bfloat16)
            for copy in group[1:]:
                copy.wait()
    for copy in brought:
        copy.wait()


def mixer_kernel(
    n_seq,
    group,
    last,
    n_before,
    *rest,
):
    blocks, rest = rest[:n_seq], rest[n_seq:]
    (f2, f3, s3, turn_re, turn_im, bs3, bf3), rest = rest[:7], rest[7:]
    if last:
        before, rest = rest[:n_before], rest[n_before:]
    else:
        before = ()
    grads, taps_out, sig, taps, up, cot, grads32, taps32 = rest
    me = lax.axis_index("seq")
    _, channels, seq_len = blocks[0].shape
    outer = sig.shape[0] // channels - PAD
    pitch, wide, narrow = outer + PAD, 2 * channels + PAD, channels + PAD
    own_outer = seq_len // LANES

    for k in range(n_seq):
        source = lax.bitwise_xor(me, k)
        for part in range(own_outer):
            cols = pl.ds(part * LANES, LANES)
            v, f, c, g = (blocks[k][i, :, cols].astype(jnp.float32) for i in range(4))
            rows = pl.ds(source * own_outer + part, channels, stride=pitch)
            sig[rows, :] = v
            taps[rows, :] = f
            up[rows, :] = c * g
            cot[rows, :] = c

    def some(step, carry):
        base = step * group
        tr, ti = turn_re[...], turn_im[...]

        def forward(ref, exact):
            turned = []
            for pair in range(group // 2):
                xs = [
                    ref[pl.ds(pl.multiple_of((base + 2 * pair + i) * pitch, PAD), outer), :]
                    for i in range(2)
                ]
                x = jnp.concatenate(xs, 1)
                if exact:
                    high = x.astype(jnp.bfloat16)
                    y = dot(f2[...], jnp.concatenate([high, high], 0))
                else:
                    high, low = split_terms(x)
                    y = dot(f3[...], jnp.concatenate([high, low, high], 0))
                for i in range(2):
                    re = y[:outer, i * LANES : (i + 1) * LANES]
                    im = y[outer:, i * LANES : (i + 1) * LANES]
                    turned.append(jnp.concatenate([re * tr - im * ti, re * ti + im * tr], 1))
            spec = wide_dot(jnp.concatenate(turned, 0), s3[...])
            return spec[:, :LANES], spec[:, LANES:]

        def backward(re, im):
            mid = wide_dot(jnp.concatenate([re, im], 1), bs3[...])
            for pair in range(group // 2):
                cols = []
                for i in range(2):
                    rows = slice((2 * pair + i) * outer, (2 * pair + i + 1) * outer)
                    re, im = mid[rows, :LANES], mid[rows, LANES:]
                    cols.append(jnp.concatenate([re * tr + im * ti, im * tr - re * ti], 0))
                high, low = split_terms(jnp.concatenate(cols, 1))
                y = dot(bf3[...], jnp.concatenate([high, low, high], 0))
                for i in range(2):
                    yield base + 2 * pair + i, y[:, i * LANES : (i + 1) * LANES]

        kr, ki = forward(taps, True)
        vr, vi = forward(sig, True)
        ur, ui = forward(up, False)
        for ch, y in backward(kr * vr - ki * vi, kr * vi + ki * vr):
            held = cot[pl.ds(pl.multiple_of(ch * pitch, PAD), outer), :]
            grads32[pl.ds(channels + ch, outer, stride=wide), :] = y * held
        for ch, y in backward(kr * ur + ki * ui, kr * ui - ki * ur):
            grads32[pl.ds(ch, outer, stride=wide), :] = y
        for ch, y in backward(ur * vr + ui * vi, ui * vr - ur * vi):
            taps32[pl.ds(ch, outer, stride=narrow), :] = y
        return carry

    lax.fori_loop(0, channels // group, some, 0)

    first = grads.shape[1] - 2 * channels
    for a in range(outer):
        if first:
            grads[a, :first, :] = before[0][a]
        grads[a, first:, :] = grads32[a * wide : a * wide + 2 * channels, :].astype(jnp.bfloat16)
    first = taps_out.shape[1] - channels
    for k in range(n_seq):
        source = lax.bitwise_xor(me, k)
        if first:
            taps_out[k, :first, :] = before[-1][k]
        for part in range(own_outer):
            start = (source * own_outer + part) * narrow
            start = pl.multiple_of(start, PAD) if narrow % PAD == 0 else start
            taps_out[k, first:, pl.ds(part * LANES, LANES)] = taps32[pl.ds(start, channels), :].astype(jnp.bfloat16)


def taps_kernel(n_seq, w_value, w_gate, *rest):
    taps_in, (out, w_held, sems) = rest[:n_seq], rest[n_seq:]
    me = lax.axis_index("seq")
    rows = w_value.shape[0]
    keep = w_held.shape[0] - rows
    copies = [
        pltpu.make_async_copy(w_value, w_held.at[:rows, :], sems.at[0]),
        pltpu.make_async_copy(w_gate.at[:keep, :], w_held.at[rows:, :], sems.at[1]),
    ]
    for copy in copies:
        copy.start()
    for k in range(n_seq):
        out[lax.bitwise_xor(me, k)] = taps_in[k][...].astype(jnp.float32)
    for copy in copies:
        copy.wait()


def project_kernel(n_seq, n_chan, n_spread, chunks, w_held, w_gate, *rest):
    spread, (out, held, gate_held, sems) = rest[:n_spread], rest[n_spread:]
    features = w_gate.shape[0]
    slab = features // SLABS
    copies = []
    for i in range(SLABS - KEPT):
        rows = pl.ds((KEPT + i) * slab, slab)
        copies.append(pltpu.make_async_copy(w_gate.at[rows, :], gate_held.at[pl.ds(i * slab, slab), :], sems.at[i]))
        copies[-1].start()
    per = chunks // n_spread
    share = spread[0].shape[1] // 2 // per
    for s in range(n_seq):
        for c in range(n_chan):
            for chunk in range(chunks):
                for g in range(2):
                    start = ((c * n_seq + s) * chunks + chunk) * share
                    at = (chunk % per * 2 + g) * share
                    piece = spread[chunk // per][s * n_chan + c, at : at + share, :]
                    held[g, pl.ds(start, share), :] = piece.astype(held.dtype)
    sides = [held[g].astype(jnp.bfloat16) for g in range(2)]
    split = KEPT * slab
    total = dot(w_held[:features, :], sides[0])
    out[:, :split] = (total[:split] + dot(w_held[features:, :], sides[1])).T.astype(jnp.bfloat16)
    for copy in copies:
        copy.wait()
    out[:, split:] = (total[split:] + dot(gate_held[...], sides[1])).T.astype(jnp.bfloat16)


def local(n_seq, n_chan, values, gate_acts, cotangent, filter_taps, w_value, w_gate):
    rows, seq_len = values.shape
    total = seq_len * n_seq
    channels = rows // n_seq
    outer = total // LANES
    tokens = total // (n_seq * n_chan)
    me = lax.axis_index("seq")
    vmem = pl.BlockSpec(memory_space=pltpu.VMEM)
    hbm = pl.BlockSpec(memory_space=pltpu.HBM)

    def like(x):
        return pltpu.VMEM(x.shape, x.dtype)

    def stay(x):
        return pltpu.with_memory_space_constraint(x, pltpu.HBM)

    def route(k):
        return [(i, i ^ k) for i in range(n_seq)]

    chunks = CHUNKS if channels % (16 * CHUNKS) == 0 else 1
    part = channels // chunks
    tables = [jnp.asarray(t) for t in dft_tables(total)]
    if part % 16 == 0:
        *sent, = pl.pallas_call(
            functools.partial(prep_kernel, n_seq, len(tables)),
            out_shape=[pltpu.VMEM((4, part, seq_len), jnp.bfloat16)] * (chunks * n_seq)
            + [like(t) for t in tables],
            in_specs=[hbm] * (4 + len(tables)),
            out_specs=[vmem] * (chunks * n_seq + len(tables)),
            scratch_shapes=[
                pltpu.VMEM((chunks * n_seq, part, seq_len), jnp.float32),
                pltpu.SemaphoreType.DMA((chunks * n_seq, 4)),
                pltpu.SemaphoreType.DMA((len(tables),)),
            ],
            compiler_params=pltpu.CompilerParams(vmem_limit_bytes=8 * 2**20),
            cost_estimate=pl.CostEstimate(flops=0, bytes_accessed=4 * 2**20, transcendentals=0),
            name="prep",
        )(*(stay(x) for x in (values, filter_taps, cotangent, gate_acts, *tables)))
        tables = sent[chunks * n_seq :]
    else:
        fields = (values, filter_taps.astype(jnp.bfloat16), cotangent, gate_acts)
        sent = [
            jnp.stack([lax.dynamic_slice_in_dim(x, (me ^ k) * channels, channels, 0) for x in fields])
            for k in range(n_seq)
        ]

    got = {}
    for chunk in range(chunks):
        for k in reversed(range(n_seq)):
            block = sent[chunk * n_seq + k]
            got[chunk, k] = lax.ppermute(block, "seq", route(k)) if k else block

    long = pltpu.VMEM((part * (outer + PAD), LANES), jnp.float32)
    spread, taps_block, before = [], None, []
    for chunk in range(chunks):
        last = chunk == chunks - 1
        args = [*(got[chunk, k] for k in range(n_seq)), *tables]
        if last:
            args += before
        outs = [
            jax.ShapeDtypeStruct((outer, 2 * part * (chunks if last and ONE_SPREAD else 1), LANES), jnp.bfloat16),
            jax.ShapeDtypeStruct((n_seq, part * (chunks if last else 1), seq_len), jnp.bfloat16),
        ]
        grads, taps_block = pl.pallas_call(
            functools.partial(mixer_kernel, n_seq, min(16, part), last, len(before)),
            out_shape=outs,
            in_specs=[vmem] * len(args),
            out_specs=[vmem] * len(outs),
            scratch_shapes=[long] * 4
            + [pltpu.VMEM((outer * (x * part + PAD), LANES), jnp.float32) for x in (2, 1)],
            compiler_params=pltpu.CompilerParams(vmem_limit_bytes=24 * 2**20),
            cost_estimate=pl.CostEstimate(flops=5 * 10**9, bytes_accessed=2 * 2**20, transcendentals=0),
            name="mixer",
        )(*args)
        before = [grads, taps_block] if ONE_SPREAD else [taps_block]
        if ONE_SPREAD and not last:
            continue
        if tokens != LANES:
            width = grads.shape[1]
            grads = grads.reshape(outer, width, LANES // tokens, tokens).transpose(0, 2, 1, 3)
            grads = grads.reshape(n_seq * n_chan, width, tokens)
        spread.append(lax.all_to_all(grads, ("seq", "chan"), 0, 0, tiled=True))

    taps_got = [lax.ppermute(taps_block[k], "seq", route(k)) if k else taps_block[0] for k in range(n_seq)]
    taps_grad, w_held = pl.pallas_call(
        functools.partial(taps_kernel, n_seq),
        out_shape=[
            jax.ShapeDtypeStruct((n_seq, channels, seq_len), jnp.float32),
            pltpu.VMEM((w_value.shape[0] * (SLABS + KEPT) // SLABS, w_value.shape[1]), w_value.dtype),
        ],
        in_specs=[hbm] * 2 + [vmem] * n_seq,
        out_specs=[vmem] * 2,
        scratch_shapes=[pltpu.SemaphoreType.DMA((2,))],
        compiler_params=pltpu.CompilerParams(vmem_limit_bytes=8 * 2**20),
        name="taps",
    )(stay(w_value), stay(w_gate), *taps_got)

    held = jnp.bfloat16 if part % 16 == 0 else jnp.float32
    args = [w_held, stay(w_gate), *spread]
    input_grad = pl.pallas_call(
        functools.partial(project_kernel, n_seq, n_chan, len(spread), chunks),
        out_shape=jax.ShapeDtypeStruct((tokens, w_value.shape[0]), jnp.bfloat16),
        in_specs=[vmem, hbm] + [vmem] * len(spread),
        out_specs=vmem,
        scratch_shapes=[
            pltpu.VMEM((2, rows * n_chan, tokens), held),
            pltpu.VMEM((w_gate.shape[0] * (SLABS - KEPT) // SLABS, w_gate.shape[1]), w_gate.dtype),
            pltpu.SemaphoreType.DMA((SLABS - KEPT,)),
        ],
        compiler_params=pltpu.CompilerParams(vmem_limit_bytes=16 * 2**20),
        name="project",
    )(*args)
    return input_grad, taps_grad.reshape(rows, seq_len)


def solution(mesh):
    return jax.shard_map(
        functools.partial(local, mesh.shape["seq"], mesh.shape["chan"]),
        mesh=mesh,
        in_specs=(P("chan", "seq"), P("chan", "seq"), P("chan", "seq"), P("chan", "seq"), P(), P()),
        out_specs=(P(("seq", "chan"), None), P("chan", "seq")),
        check_vma=False,
    )
```

time: 55.1 us -> 47.1 us (0.85)
  waiting for transfers between devices: 25.2 us -> 19 us
  local copies, waits for them, and re-layouts: 3.82 us -> 0.02 us
  Pallas kernels: 12.3 us -> 14.1 us
  starting transfers between devices: 11.5 us -> 13.1 us
  other arithmetic: 1.22 us -> 0 us
    ppermute x6 -> x9, waiting for transfers between devices: 18.2 us -> 14.6 us  [the longest x3 7.37 us: local(): lax.ppermute(taps_block[k], 'seq', route(k))]
    all_to_all x1, waiting for transfers between devices: 6.99 us -> 4.41 us  [local(): spread.append(lax.all_to_all(grads, ('seq', 'chan'), 0, 0, tiled=True))]
    another operation x2 -> x0, local copies, waits for them, and re-layouts: 2.16 us -> none  [local(): jnp.stack([lax.dynamic_slice_in_dim(x, start, channels, 0) for x in fields])]
    ppermute x6 -> x9, starting transfers between devices: 5.21 us -> 7.19 us  [the longest x6 5.23 us: local(): got[chunk, k] = lax.ppermute(block, 'seq', route(k)) if k else block]
    pallas_call x2 -> x5, Pallas kernels: 12.3 us -> 14.1 us  [the longest x2 6.54 us: local(): pl.pallas_call(functools.partial(mixer_kernel, n_seq, min(16, part), last...]
    unnamed x18 -> x0, local copies, waits for them, and re-layouts: 1.65 us -> none
    convert_element_type x1 -> x0, other arithmetic: 1.07 us -> none  [local(): taps16 = filter_taps.astype(jnp.bfloat16)]
  transfers between devices with their start and end apart: 7 -> 10, of which waited for: 5 -> 7; matrix products, arithmetic and copies ran while one was open for 0% -> 0% of each run, Pallas kernels for 0% -> 12%
where the time goes in v2:
time: 47.1 us; the launch traced here: 46.9 us
  waiting for transfers between devices  19 us (40%)
  Pallas kernels  14.1 us (30%)
  starting transfers between devices  13.1 us (28%)
  between operations  0.69 us (1%)
    ppermute x3, waiting for transfers between devices, local(): lax.ppermute(taps_block[k], 'seq', route(k))  7.37 us
    ppermute x6, waiting for transfers between devices, local(): got[chunk, k] = lax.ppermute(block, 'seq', route(k)) if k else block  7.18 us
    pallas_call x2, Pallas kernels, local(): pl.pallas_call(functools.partial(mixer_kernel, n_seq, min(16, part), last...  6.54 us
    all_to_all x1, starting transfers between devices, local(): spread.append(lax.all_to_all(grads, ('seq', 'chan'), 0, 0, tiled=True))  5.92 us
    ppermute x6, starting transfers between devices, local(): got[chunk, k] = lax.ppermute(block, 'seq', route(k)) if k else block  5.23 us
    all_to_all x1, waiting for transfers between devices, local(): spread.append(lax.all_to_all(grads, ('seq', 'chan'), 0, 0, tiled=True))  4.41 us
    pallas_call x1, Pallas kernels, local(): pl.pallas_call(functools.partial(project_kernel, n_seq, n_chan, len(sprea...  2.94 us
    pallas_call x1, Pallas kernels, local(): pl.pallas_call(functools.partial(taps_kernel, n_seq), out_shape=[jax.Shap...  2.57 us
  transfers between devices with their start and end apart: 10, of which 7 were waited for; matrix products, arithmetic and copies ran while one was open for 0% of the time, Pallas kernels for 12%

profile of v2, /device:TPU:0, one launch (start us, length us, event | category | flops | bytes accessed | tf_op | source)
XLA Modules:
  0.0 46.9 jit_solution(548559308152877434)
XLA Ops:
  0.6 2.0 %prep.1 = (bf16[4,16,1024]{2,1,0:T(8,128)(2,1)S(1)}, bf16[4,16,1024]{2,1,0:T(8,128)(2,1)S(1)}, bf16[4,16,1024]{2,1,0:T(8,128)(2,1)S(1)}, bf16[4,16,1024]{2,1,0:T...) custom-call(bf16[128,1024]{1,0:T(8,128)(2,1)} %values.1, ...), custom_call_target="tpu_custom_call" | custom-call | bytes 4194304 | tf_op jit(solution)/shard_map/prep/pallas_call | solution.py:271
  2.7 0.5 %collective-permute-start.3 = (bf16[4,16,1024]{2,1,0:T(8,128)(2,1)S(1)}, bf16[4,16,1024]{2,1,0:T(8,128)(2,1)S(1)}, u32[]{:S(2)}, u32[]{:S(2)}) collective-permute-start(bf16[4,16,1024]{2,1,0:T(8,128)(2,1)S(1)} %get-tuple-element.35), channel_id=1, source_target_pairs={{0,8},{8,0},{16,24},{24,16},{1,9},{9,1},{17,25},{25,17},{2,10},{10... | collective-permute-start | bytes 393224 | tf_op jit(solution)/shard_map/ppermute | solution.py:298
  3.2 2.6 %collective-permute-start.4 = (bf16[4,16,1024]{2,1,0:T(8,128)(2,1)S(1)}, bf16[4,16,1024]{2,1,0:T(8,128)(2,1)S(1)}, u32[]{:S(2)}, u32[]{:S(2)}) collective-permute-start(bf16[4,16,1024]{2,1,0:T(8,128)(2,1)S(1)} %get-tuple-element.36), channel_id=1, source_target_pairs={{0,16},{8,24},{16,0},{24,8},{1,17},{9,25},{17,1},{25,9},{2,18},{10... | collective-permute-start | bytes 393224 | tf_op jit(solution)/shard_map/ppermute | solution.py:298
  5.8 0.1 collective-permute-start.5
  5.8 0.1 collective-permute-start
  6.0 1.9 %collective-permute-start.1 = (bf16[4,16,1024]{2,1,0:T(8,128)(2,1)S(1)}, bf16[4,16,1024]{2,1,0:T(8,128)(2,1)S(1)}, u32[]{:S(2)}, u32[]{:S(2)}) collective-permute-start(bf16[4,16,1024]{2,1,0:T(8,128)(2,1)S(1)} %get-tuple-element.25), channel_id=1, source_target_pairs={{0,16},{8,24},{16,0},{24,8},{1,17},{9,25},{17,1},{25,9},{2,18},{10... | collective-permute-start | bytes 393224 | tf_op jit(solution)/shard_map/ppermute | solution.py:298
  7.9 0.0 collective-permute-done.3.rest_1_
  7.9 0.0 collective-permute-start.2
  7.9 2.2 %collective-permute-done.4.rest_2_ = bf16[4,16,1024]{2,1,0:T(8,128)(2,1)S(1)} collective-permute-done((bf16[4,16,1024]{2,1,0:T(8,128)(2,1)S(1)}, bf16[4,16,1024]{2,1,0:T(8,128)(2,1)S(1)}, u32[]{:S(2)}, u32[]{:S(2)}) %collective-permute-start.4) | collective-permute-done | bytes 131104 | tf_op jit(solution)/shard_map/ppermute | solution.py:298
  10.1 2.3 %collective-permute-done.5.rest_3_ = bf16[4,16,1024]{2,1,0:T(8,128)(2,1)S(1)} collective-permute-done((bf16[4,16,1024]{2,1,0:T(8,128)(2,1)S(1)}, bf16[4,16,1024]{2,1,0:T(8,128)(2,1)S(1)}, u32[]{:S(2)}, u32[]{:S(2)}) %collective-permute-start.5) | collective-permute-done | bytes 131104 | tf_op jit(solution)/shard_map/ppermute | solution.py:298
  12.4 2.9 %mixer.2 = (bf16[32,32,128]{2,1,0:T(8,128)(2,1)S(1)}, bf16[4,16,1024]{2,1,0:T(8,128)(2,1)S(1)}) custom-call(bf16[4,16,1024]{2,1,0:T(8,128)(2,1)S(1)} %get-tuple-element.34.rest_0_, bf16[4,16,1024]{2,1,0:T(8,128)(2,1)S(1)} %collective-permute-done.3.rest_1_, bf16[4,16,1024]{2,1,0:T(8,128)(2,1)S(1)} %collective-permute-done.4.rest_2_, ...), custom_call_target="tpu_custom_call" | custom-call | flops 5000000000 | bytes 2097152 | tf_op jit(solution)/shard_map/mixer/pallas_call | solution.py:311
  15.3 0.0 collective-permute-done.rest_1_
  15.3 0.4 collective-permute-done.1.rest_2_
  15.7 2.3 %collective-permute-done.2.rest_3_ = bf16[4,16,1024]{2,1,0:T(8,128)(2,1)S(1)} collective-permute-done((bf16[4,16,1024]{2,1,0:T(8,128)(2,1)S(1)}, bf16[4,16,1024]{2,1,0:T(8,128)(2,1)S(1)}, u32[]{:S(2)}, u32[]{:S(2)}) %collective-permute-start.2) | collective-permute-done | bytes 131104 | tf_op jit(solution)/shard_map/ppermute | solution.py:298
  18.0 3.6 %mixer.3 = (bf16[32,64,128]{2,1,0:T(8,128)(2,1)}, bf16[4,32,1024]{2,1,0:T(8,128)(2,1)S(1)}) custom-call(bf16[4,16,1024]{2,1,0:T(8,128)(2,1)S(1)} %get-tuple-element.23.rest_0_, bf16[4,16,1024]{2,1,0:T(8,128)(2,1)S(1)} %collective-permute-done.rest_1_, bf16[4,16,1024]{2,1,0:T(8,128)(2,1)S(1)} %collective-permute-done.1.rest_2_, ...), custom_call_target="tpu_custom_call" | custom-call | flops 5000000000 | bytes 2097152 | tf_op jit(solution)/shard_map/mixer/pallas_call | solution.py:311
  21.6 5.9 %all-to-all-start = ((bf16[32,64,128]{2,1,0:T(8,128)(2,1)}), bf16[32,64,128]{2,1,0:T(8,128)(2,1)S(1)}, u32[]{:S(2)}, u32[]{:S(2)}) async-start(bf16[32,64,128]{2,1,0:T(8,128)(2,1)} %get-tuple-element.42), calls=%async_computation | async-start | bytes 1048576 | tf_op jit(solution)/shard_map/all_to_all | solution.py:329
  27.6 1.6 %collective-permute-start.8 = (bf16[32,1024]{1,0:T(8,128)(2,1)S(1)}, bf16[32,1024]{1,0:T(8,128)(2,1)S(1)}, u32[]{:S(2)}, u32[]{:S(2)}) collective-permute-start(bf16[32,1024]{1,0:T(8,128)(2,1)S(1)} %get-tuple-element.44), channel_id=1, source_target_pairs={{0,24},{8,16},{16,8},{24,0},{1,25},{9,17},{17,9},{25,1},{2,26},{10... | collective-permute-start | bytes 196616 | tf_op jit(solution)/shard_map/ppermute | solution.py:331
  29.2 0.4 collective-permute-start.7
  29.6 0.0 collective-permute-start.6
  29.6 4.6 %collective-permute-done.8.rest_3_ = bf16[32,1024]{1,0:T(8,128)(2,1)S(1)} collective-permute-done((bf16[32,1024]{1,0:T(8,128)(2,1)S(1)}, bf16[32,1024]{1,0:T(8,128)(2,1)S(1)}, u32[]{:S(2)}, u32[]{:S(2)}) %collective-permute-start.8) | collective-permute-done | bytes 65568 | tf_op jit(solution)/shard_map/ppermute | solution.py:331
  34.2 2.7 %collective-permute-done.7.rest_2_ = bf16[32,1024]{1,0:T(8,128)(2,1)S(1)} collective-permute-done((bf16[32,1024]{1,0:T(8,128)(2,1)S(1)}, bf16[32,1024]{1,0:T(8,128)(2,1)S(1)}, u32[]{:S(2)}, u32[]{:S(2)}) %collective-permute-start.7) | collective-permute-done | bytes 65568 | tf_op jit(solution)/shard_map/ppermute | solution.py:331
  36.9 0.0 collective-permute-done.6.rest_1_
  36.9 2.6 %taps.1 = (f32[4,32,1024]{2,1,0:T(8,128)}, bf16[1408,1024]{1,0:T(8,128)(2,1)S(1)}) custom-call(bf16[1024,1024]{1,0:T(8,128)(2,1)} %w_value.1, bf16[1024,1024]{1,0:T(8,128)(2,1)} %w_gate.3, bf16[32,1024]{1,0:T(8,128)(2,1)S(1)} %get-tuple-element.47.rest_0_, bf16[32,1024]{1,0:T(8,128)(2,1)S(1)} %collective-permute-done.6.rest_1_, ...), custom_call_target="tpu_custom_call" | custom-call | tf_op jit(solution)/shard_map/taps/pallas_call | solution.py:332
  39.5 4.4 %all-to-all-done.rest_0_ = bf16[32,64,128]{2,1,0:T(8,128)(2,1)S(1)} async-done(((bf16[32,64,128]{2,1,0:T(8,128)(2,1)}), bf16[32,64,128]{2,1,0:T(8,128)(2,1)S(1)}, u32[]{:S(2)}, u32[]{:S(2)}) %all-to-all-start) | async-done | bytes 524320 | tf_op jit(solution)/shard_map/all_to_all | solution.py:329
  43.9 2.9 %project.1 = bf16[128,1024]{1,0:T(8,128)(2,1)} custom-call(bf16[1408,1024]{1,0:T(8,128)(2,1)S(1)} %get-tuple-element.41.w_held, bf16[1024,1024]{1,0:T(8,128)(2,1)} %w_gate.3, bf16[32,64,128]{2,1,0:T(8,128)(2,1)S(1)} %all-to-all-done.rest_0_), custom_call_target="tpu_custom_call" | custom-call | tf_op jit(solution)/shard_map/project/pallas_call | solution.py:347
  (1 shorter events, 0.0 us)
Async XLA Ops:
  2.7 5.2 %collective-permute-start.3 = (bf16[4,16,1024]{2,1,0:T(8,128)(2,1)S(1)}, bf16[4,16,1024]{2,1,0:T(8,128)(2,1)S(1)}, u32[]{:S(2)}, u32[]{:S(2)}) collective-permute-start(bf16[4,16,1024]{2,1,0:T(8,128)(2,1)S(1)} %get-tuple-element.35), channel_id=1, source_target_pairs={{0,8},{8,0},{16,24},{24,16},{1,9},{9,1},{17,25},{25,17},{2,10},{10... | collective-permute-start | bytes 393224 | tf_op jit(solution)/shard_map/ppermute | solution.py:298
  3.2 6.9 %collective-permute-start.4 = (bf16[4,16,1024]{2,1,0:T(8,128)(2,1)S(1)}, bf16[4,16,1024]{2,1,0:T(8,128)(2,1)S(1)}, u32[]{:S(2)}, u32[]{:S(2)}) collective-permute-start(bf16[4,16,1024]{2,1,0:T(8,128)(2,1)S(1)} %get-tuple-element.36), channel_id=1, source_target_pairs={{0,16},{8,24},{16,0},{24,8},{1,17},{9,25},{17,1},{25,9},{2,18},{10... | collective-permute-start | bytes 393224 | tf_op jit(solution)/shard_map/ppermute | solution.py:298
  5.8 6.6 %collective-permute-start.5 = (bf16[4,16,1024]{2,1,0:T(8,128)(2,1)S(1)}, bf16[4,16,1024]{2,1,0:T(8,128)(2,1)S(1)}, u32[]{:S(2)}, u32[]{:S(2)}) collective-permute-start(bf16[4,16,1024]{2,1,0:T(8,128)(2,1)S(1)} %get-tuple-element.37), channel_id=1, source_target_pairs={{0,24},{8,16},{16,8},{24,0},{1,25},{9,17},{17,9},{25,1},{2,26},{10... | collective-permute-start | bytes 393224 | tf_op jit(solution)/shard_map/ppermute | solution.py:298
  5.8 9.5 %collective-permute-start = (bf16[4,16,1024]{2,1,0:T(8,128)(2,1)S(1)}, bf16[4,16,1024]{2,1,0:T(8,128)(2,1)S(1)}, u32[]{:S(2)}, u32[]{:S(2)}) collective-permute-start(bf16[4,16,1024]{2,1,0:T(8,128)(2,1)S(1)} %get-tuple-element.24), channel_id=1, source_target_pairs={{0,8},{8,0},{16,24},{24,16},{1,9},{9,1},{17,25},{25,17},{2,10},{10... | collective-permute-start | bytes 393224 | tf_op jit(solution)/shard_map/ppermute | solution.py:298
  6.0 9.8 %collective-permute-start.1 = (bf16[4,16,1024]{2,1,0:T(8,128)(2,1)S(1)}, bf16[4,16,1024]{2,1,0:T(8,128)(2,1)S(1)}, u32[]{:S(2)}, u32[]{:S(2)}) collective-permute-start(bf16[4,16,1024]{2,1,0:T(8,128)(2,1)S(1)} %get-tuple-element.25), channel_id=1, source_target_pairs={{0,16},{8,24},{16,0},{24,8},{1,17},{9,25},{17,1},{25,9},{2,18},{10... | collective-permute-start | bytes 393224 | tf_op jit(solution)/shard_map/ppermute | solution.py:298
  7.9 10.1 %collective-permute-start.2 = (bf16[4,16,1024]{2,1,0:T(8,128)(2,1)S(1)}, bf16[4,16,1024]{2,1,0:T(8,128)(2,1)S(1)}, u32[]{:S(2)}, u32[]{:S(2)}) collective-permute-start(bf16[4,16,1024]{2,1,0:T(8,128)(2,1)S(1)} %get-tuple-element.26), channel_id=1, source_target_pairs={{0,24},{8,16},{16,8},{24,0},{1,25},{9,17},{17,9},{25,1},{2,26},{10... | collective-permute-start | bytes 393224 | tf_op jit(solution)/shard_map/ppermute | solution.py:298
  21.6 22.3 %all-to-all-start = ((bf16[32,64,128]{2,1,0:T(8,128)(2,1)}), bf16[32,64,128]{2,1,0:T(8,128)(2,1)S(1)}, u32[]{:S(2)}, u32[]{:S(2)}) async-start(bf16[32,64,128]{2,1,0:T(8,128)(2,1)} %get-tuple-element.42), calls=%async_computation | async-start | bytes 1048576 | tf_op jit(solution)/shard_map/all_to_all | solution.py:329
  27.6 6.6 %collective-permute-start.8 = (bf16[32,1024]{1,0:T(8,128)(2,1)S(1)}, bf16[32,1024]{1,0:T(8,128)(2,1)S(1)}, u32[]{:S(2)}, u32[]{:S(2)}) collective-permute-start(bf16[32,1024]{1,0:T(8,128)(2,1)S(1)} %get-tuple-element.44), channel_id=1, source_target_pairs={{0,24},{8,16},{16,8},{24,0},{1,25},{9,17},{17,9},{25,1},{2,26},{10... | collective-permute-start | bytes 196616 | tf_op jit(solution)/shard_map/ppermute | solution.py:331
  29.2 7.7 %collective-permute-start.7 = (bf16[32,1024]{1,0:T(8,128)(2,1)S(1)}, bf16[32,1024]{1,0:T(8,128)(2,1)S(1)}, u32[]{:S(2)}, u32[]{:S(2)}) collective-permute-start(bf16[32,1024]{1,0:T(8,128)(2,1)S(1)} %get-tuple-element.45), channel_id=1, source_target_pairs={{0,16},{8,24},{16,0},{24,8},{1,17},{9,25},{17,1},{25,9},{2,18},{10... | collective-permute-start | bytes 196616 | tf_op jit(solution)/shard_map/ppermute | solution.py:331
  29.6 7.4 %collective-permute-start.6 = (bf16[32,1024]{1,0:T(8,128)(2,1)S(1)}, bf16[32,1024]{1,0:T(8,128)(2,1)S(1)}, u32[]{:S(2)}, u32[]{:S(2)}) collective-permute-start(bf16[32,1024]{1,0:T(8,128)(2,1)S(1)} %get-tuple-element.46), channel_id=1, source_target_pairs={{0,8},{8,0},{16,24},{24,16},{1,9},{9,1},{17,25},{25,17},{2,10},{10... | collective-permute-start | bytes 196616 | tf_op jit(solution)/shard_map/ppermute | solution.py:331

commit v3 on v2

v3 whole, which is shorter than its diff:
```python
import functools
import math

import jax
import jax.numpy as jnp
import numpy as np
from jax import lax
from jax.experimental import pallas as pl
from jax.experimental.pallas import tpu as pltpu
from jax.sharding import Mesh
from jax.sharding import PartitionSpec as P

LANES = 128
VALUE, TAPS, COT, GATE = range(4)
SLABS = 8
KEPT = 3
PAD = 8


def halves(table):
    high = table.astype(jnp.bfloat16)
    low = (table - high.astype(np.float64)).astype(jnp.bfloat16)
    return high, low


def dft_tables(total):
    outer = total // LANES
    k1 = np.arange(outer) + 0.25
    a = np.arange(outer)
    b = np.arange(LANES)
    first = np.exp(-2j * np.pi * np.outer(k1, a) / outer)
    first = np.concatenate([first.real, first.imag], 0)
    turn = np.exp(-2j * np.pi * np.outer(k1, b) / total)
    second = np.exp(-2j * np.pi * np.outer(b, b) / LANES)
    second = np.block([[second.real, second.imag], [-second.imag, second.real]])
    back_second = second.T / total / math.sqrt(total)
    back_first = np.exp(2j * np.pi * np.outer(a, k1) / outer)
    back_first = np.concatenate([back_first.real, -back_first.imag], 1)

    f_hi, f_lo = halves(first)
    s_hi, s_lo = halves(second)
    bs_hi, bs_lo = halves(back_second)
    bf_hi, bf_lo = halves(back_first)
    return (
        np.concatenate([f_hi, f_lo], 1),
        np.concatenate([f_hi, f_hi, f_lo], 1),
        np.concatenate([s_hi, s_hi, s_lo], 0),
        turn.real.astype(np.float32),
        turn.imag.astype(np.float32),
        np.concatenate([bs_hi, bs_hi, bs_lo], 0),
        np.concatenate([bf_hi, bf_hi, bf_lo], 1),
    )


def split_terms(x):
    high = x.astype(jnp.bfloat16)
    low = (x - high.astype(jnp.float32)).astype(jnp.bfloat16)
    return high, low


def dot(left, right):
    return jnp.dot(left, right, preferred_element_type=jnp.float32)


def wide_dot(x, table):
    high, low = split_terms(x)
    return dot(jnp.concatenate([high, low, high], 1), table)


def prep_kernel(steps, n_tables, values, filter_taps, cotangent, gate_acts, *rest):
    tables, rest = rest[:n_tables], rest[n_tables:]
    (narrow, wide, sems, table_sems), rest = rest[-4:], rest[:-4]
    outs, held = rest[: len(rest) - n_tables], rest[len(rest) - n_tables :]
    me = lax.axis_index("seq")
    channels = wide.shape[1]
    fields = {VALUE: values, COT: cotangent, GATE: gate_acts}
    copies = []
    for at, k in enumerate(steps):
        mine = pl.ds(pl.multiple_of(lax.bitwise_xor(me, k) * channels, channels), channels)
        copies.append([pltpu.make_async_copy(filter_taps.at[mine, :], wide.at[at], sems.at[at, TAPS])])
        for i, ref in enumerate(fields.values()):
            copies[-1].append(pltpu.make_async_copy(ref.at[mine, :], narrow.at[at, i], sems.at[at, i + (i > 0)]))
        for copy in copies[-1]:
            copy.start()
    brought = [pltpu.make_async_copy(tables[i], held[i], table_sems.at[i]) for i in range(n_tables)]
    for copy in brought:
        copy.start()
    for at in range(len(steps)):
        for copy in copies[at]:
            copy.wait()
        blocks = [wide[at], *(narrow[at, i].astype(jnp.float32) for i in range(3))]
        for field, block in zip((TAPS, VALUE, COT, GATE), blocks):
            first = 0
            for out in outs[at :: len(steps)]:
                size = out.shape[1]
                out[field] = block[first : first + size].astype(jnp.bfloat16)
                first += size
    for copy in brought:
        copy.wait()


def mixer_kernel(
    n_seq,
    group,
    offset,
    places,
    *rest,
):
    blocks, rest = rest[:n_seq], rest[n_seq:]
    (f2, f3, s3, turn_re, turn_im, bs3, bf3), rest = rest[:7], rest[7:]
    before = ()
    if offset:
        before, rest = rest[1:2], rest[2:]
    grads, taps_out, sig, taps, up, cot, grads32, taps32, grads16, sem = rest
    me = lax.axis_index("seq")
    _, channels, seq_len = blocks[0].shape
    outer = sig.shape[0] // channels - PAD
    pitch, wide, narrow = outer + PAD, 2 * channels + PAD, channels + PAD
    own_outer = seq_len // LANES

    for k in range(n_seq):
        source = lax.bitwise_xor(me, k)
        for part in range(own_outer):
            cols = pl.ds(part * LANES, LANES)
            v, f, c, g = (blocks[k][i, :, cols].astype(jnp.float32) for i in range(4))
            rows = pl.ds(source * own_outer + part, channels, stride=pitch)
            sig[rows, :] = v
            taps[rows, :] = f
            up[rows, :] = c * g
            cot[rows, :] = c

    tr, ti = turn_re[...], turn_im[...]

    def forward(ref, exact, base, out):
        turned = []
        ys = []
        for pair in range(group // 2):
            xs = [ref[pl.ds((base + 2 * pair + i) * pitch, outer), :] for i in range(2)]
            x = jnp.concatenate(xs, 1)
            if exact:
                high = x.astype(jnp.bfloat16)
                ys.append(dot(f2[...], jnp.concatenate([high, high], 0)))
            else:
                high, low = split_terms(x)
                ys.append(dot(f3[...], jnp.concatenate([high, low, high], 0)))
        yield
        for y in ys:
            for i in range(2):
                re = y[:outer, i * LANES : (i + 1) * LANES]
                im = y[outer:, i * LANES : (i + 1) * LANES]
                turned.append(jnp.concatenate([re * tr - im * ti, re * ti + im * tr], 1))
        high, low = split_terms(jnp.concatenate(turned, 0))
        yield
        spec = dot(jnp.concatenate([high, low, high], 1), s3[...])
        out += [spec[:, :LANES], spec[:, LANES:]]
        yield

    def backward(left, right, conj, base, put):
        (ar, ai), (br, bi) = left, right
        if conj:
            product = jnp.concatenate([ar * br + ai * bi, ai * br - ar * bi], 1)
        else:
            product = jnp.concatenate([ar * br - ai * bi, ar * bi + ai * br], 1)
        high, low = split_terms(product)
        yield
        mid = dot(jnp.concatenate([high, low, high], 1), bs3[...])
        yield
        terms = []
        for pair in range(group // 2):
            cols = []
            for i in range(2):
                rows = slice((2 * pair + i) * outer, (2 * pair + i + 1) * outer)
                re, im = mid[rows, :LANES], mid[rows, LANES:]
                cols.append(jnp.concatenate([re * tr + im * ti, im * tr - re * ti], 0))
            terms.append(split_terms(jnp.concatenate(cols, 1)))
        yield
        ys = [dot(bf3[...], jnp.concatenate([high, low, high], 0)) for high, low in terms]
        yield
        for pair, y in enumerate(ys):
            for i in range(2):
                put(base + 2 * pair + i, y[:, i * LANES : (i + 1) * LANES])
        yield

    def put_gate(ch, y):
        held = cot[pl.ds(ch * pitch, outer), :]
        grads32[pl.ds(channels + ch, outer, stride=wide), :] = y * held

    def put_value(ch, y):
        grads32[pl.ds(ch, outer, stride=wide), :] = y

    def put_taps(ch, y):
        taps32[pl.ds(ch, outer, stride=narrow), :] = y

    tasks = []
    for base in range(0, channels, group):
        k, v, u = [], [], []
        tasks += [
            forward(taps, True, base, k),
            forward(sig, True, base, v),
            forward(up, False, base, u),
            backward(k, v, False, base, put_gate),
            backward(u, k, True, base, put_value),
            backward(u, v, True, base, put_taps),
        ]
    live = []
    while tasks or live:
        live = [task for task in live if next(task, StopIteration) is None]
        if tasks:
            live.append(tasks.pop(0))
            next(live[-1])

    copy = pltpu.make_async_copy(grads16, grads.at[:, pl.ds(2 * offset, 2 * channels), :], sem)

    def send():
        for a in range(outer):
            grads16[places[a]] = grads32[a * wide : a * wide + 2 * channels, :].astype(jnp.bfloat16)
        copy.start()

    send()
    for k in range(n_seq):
        source = lax.bitwise_xor(me, k)
        for part in range(own_outer):
            start = (source * own_outer + part) * narrow
            start = pl.multiple_of(start, PAD) if narrow % PAD == 0 else start
            cols = pl.ds(part * LANES, LANES)
            parts = [x[k, :, cols] for x in before] + [taps32[pl.ds(start, channels), :]]
            taps_out[k, :, cols] = jnp.concatenate(parts, 0).astype(taps_out.dtype)
    copy.wait()


def taps_kernel(n_seq, w_value, w_gate, *rest):
    taps_in, (out, w_held, sems) = rest[:n_seq], rest[n_seq:]
    me = lax.axis_index("seq")
    rows = w_value.shape[0]
    keep = w_held.shape[0] - rows
    copies = [
        pltpu.make_async_copy(w_value, w_held.at[:rows, :], sems.at[0]),
        pltpu.make_async_copy(w_gate.at[:keep, :], w_held.at[rows:, :], sems.at[1]),
    ]
    for copy in copies:
        copy.start()
    for k in range(n_seq):
        out[lax.bitwise_xor(me, k)] = taps_in[k][...].astype(jnp.float32)
    for copy in copies:
        copy.wait()


def project_kernel(n_seq, n_far, n_near, sizes, w_held, w_gate, spread, out, held, gate_held, sems):
    features = w_gate.shape[0]
    slab = features // SLABS
    copies = []
    for i in range(SLABS - KEPT):
        rows = pl.ds((KEPT + i) * slab, slab)
        copies.append(pltpu.make_async_copy(w_gate.at[rows, :], gate_held.at[pl.ds(i * slab, slab), :], sems.at[i]))
        copies[-1].start()
    share = sum(sizes)
    firsts = [sum(sizes[:i]) for i in range(len(sizes))]
    for source, (near, s, far) in enumerate(np.ndindex(n_near, n_seq, n_far)):
        block = spread[source].astype(jnp.float32)
        rows = pl.ds(((far * n_near + near) * n_seq + s) * share, share)
        for g in range(2):
            pieces = [block[2 * at + g * size : 2 * at + (g + 1) * size] for at, size in zip(firsts, sizes)]
            held[g, rows, :] = jnp.concatenate(pieces, 0).astype(held.dtype)
    sides = [held[g].astype(jnp.bfloat16) for g in range(2)]
    split = KEPT * slab
    total = dot(w_held[:features, :], sides[0])
    out[:, :split] = (total[:split] + dot(w_held[features:, :], sides[1])).T.astype(jnp.bfloat16)
    for copy in copies:
        copy.wait()
    out[:, split:] = (total[split:] + dot(gate_held[...], sides[1])).T.astype(jnp.bfloat16)


def local(n_seq, n_far, n_near, values, gate_acts, cotangent, filter_taps, w_value, w_gate):
    rows, seq_len = values.shape
    n_chan = n_far * n_near
    total = seq_len * n_seq
    channels = rows // n_seq
    outer = total // LANES
    tokens = total // (n_seq * n_chan)
    me = lax.axis_index("seq")
    vmem = pl.BlockSpec(memory_space=pltpu.VMEM)
    hbm = pl.BlockSpec(memory_space=pltpu.HBM)

    def like(x):
        return pltpu.VMEM(x.shape, x.dtype)

    def stay(x):
        return pltpu.with_memory_space_constraint(x, pltpu.HBM)

    def route(k):
        return [(i, i ^ k) for i in range(n_seq)]

    sizes = (channels // 2, channels // 2) if channels % 32 == 0 else (channels,)
    chunks = len(sizes)
    tables = [jnp.asarray(t) for t in dft_tables(total)]

    def prep(steps, tables):
        outs = [pltpu.VMEM((4, size, seq_len), jnp.bfloat16) for size in sizes for _ in steps]
        outs += [like(t) for t in tables]
        got = pl.pallas_call(
            functools.partial(prep_kernel, steps, len(tables)),
            out_shape=outs,
            in_specs=[hbm] * (4 + len(tables)),
            out_specs=[vmem] * len(outs),
            scratch_shapes=[
                pltpu.VMEM((len(steps), 3, channels, seq_len), jnp.bfloat16),
                pltpu.VMEM((len(steps), channels, seq_len), jnp.float32),
                pltpu.SemaphoreType.DMA((len(steps), 4)),
                pltpu.SemaphoreType.DMA((max(len(tables), 1),)),
            ],
            compiler_params=pltpu.CompilerParams(vmem_limit_bytes=8 * 2**20),
            cost_estimate=pl.CostEstimate(flops=0, bytes_accessed=4 * 2**20, transcendentals=0),
            name="prep",
        )(*(stay(x) for x in (values, filter_taps, cotangent, gate_acts, *tables)))
        for chunk in range(chunks):
            for at, k in enumerate(steps):
                sent[chunk, k] = got[chunk * len(steps) + at]
        return got[chunks * len(steps) :]

    sent, got = {}, {}
    if chunks > 1:
        far = tuple(reversed(range(2, n_seq)))
        prep(far, [])
        tables = prep((1, 0), tables)
    else:
        fields = (values, filter_taps.astype(jnp.bfloat16), cotangent, gate_acts)
        for k in range(n_seq):
            rows_k = [lax.dynamic_slice_in_dim(x, (me ^ k) * channels, channels, 0) for x in fields]
            sent[0, k] = jnp.stack(rows_k)
    for chunk in range(chunks):
        for k in reversed(range(n_seq)):
            block = sent[chunk, k]
            got[chunk, k] = lax.ppermute(block, "seq", route(k)) if k else block

    places = list(range(outer))
    if tokens == LANES:
        for s, far, near in np.ndindex(n_seq, n_far, n_near):
            places[(s * n_far + far) * n_near + near] = (near * n_seq + s) * n_far + far
    grads, taps_block, offset = None, None, 0
    for chunk, size in enumerate(sizes):
        args = [*(got[chunk, k] for k in range(n_seq)), *tables]
        specs = [vmem] * len(args)
        aliases = {}
        if chunk:
            aliases = {len(args): 0}
            args += [grads, taps_block]
            specs += [hbm, vmem]
        long = pltpu.VMEM((size * (outer + PAD), LANES), jnp.float32)
        kind = jnp.bfloat16 if chunk == chunks - 1 else jnp.float32
        grads, taps_block = pl.pallas_call(
            functools.partial(mixer_kernel, n_seq, size if size <= 24 else 8, offset, places),
            out_shape=[
                pltpu.HBM((outer, 2 * channels, LANES), jnp.bfloat16),
                pltpu.VMEM((n_seq, offset + size, seq_len), kind),
            ],
            in_specs=specs,
            out_specs=[hbm, vmem],
            input_output_aliases=aliases,
            scratch_shapes=[long] * 4
            + [pltpu.VMEM((outer * (x * size + PAD), LANES), jnp.float32) for x in (2, 1)]
            + [pltpu.VMEM((outer, 2 * size, LANES), jnp.bfloat16), pltpu.SemaphoreType.DMA],
            compiler_params=pltpu.CompilerParams(vmem_limit_bytes=24 * 2**20),
            cost_estimate=pl.CostEstimate(flops=5 * 10**9, bytes_accessed=2 * 2**20, transcendentals=0),
            name="mixer",
        )(*args)
        offset += size
    if tokens != LANES:
        grads = grads.reshape(outer, 2 * channels, LANES // tokens, tokens).transpose(0, 2, 1, 3)
        grads = grads.reshape(n_seq, n_far, n_near, 2 * channels, tokens).transpose(2, 0, 1, 3, 4)
        grads = grads.reshape(n_seq * n_chan, 2 * channels, tokens)
    spread = lax.all_to_all(grads, ("near", "seq", "far"), 0, 0, tiled=True)

    taps_got = [lax.ppermute(taps_block[k], "seq", route(k)) if k else taps_block[0] for k in range(n_seq)]
    taps_grad, w_held = pl.pallas_call(
        functools.partial(taps_kernel, n_seq),
        out_shape=[
            jax.ShapeDtypeStruct((n_seq, channels, seq_len), jnp.float32),
            pltpu.VMEM((w_value.shape[0] * (SLABS + KEPT) // SLABS, w_value.shape[1]), w_value.dtype),
        ],
        in_specs=[hbm] * 2 + [vmem] * n_seq,
        out_specs=[vmem] * 2,
        scratch_shapes=[pltpu.SemaphoreType.DMA((2,))],
        compiler_params=pltpu.CompilerParams(vmem_limit_bytes=8 * 2**20),
        name="taps",
    )(stay(w_value), stay(w_gate), *taps_got)

    held = jnp.bfloat16 if channels % 16 == 0 else jnp.float32
    args = [w_held, stay(w_gate), spread]
    input_grad = pl.pallas_call(
        functools.partial(project_kernel, n_seq, n_far, n_near, sizes),
        out_shape=jax.ShapeDtypeStruct((tokens, w_value.shape[0]), jnp.bfloat16),
        in_specs=[vmem, hbm, vmem],
        out_specs=vmem,
        scratch_shapes=[
            pltpu.VMEM((2, rows * n_chan, tokens), held),
            pltpu.VMEM((w_gate.shape[0] * (SLABS - KEPT) // SLABS, w_gate.shape[1]), w_gate.dtype),
            pltpu.SemaphoreType.DMA((SLABS - KEPT,)),
        ],
        compiler_params=pltpu.CompilerParams(vmem_limit_bytes=16 * 2**20),
        name="project",
    )(*args)
    return input_grad, taps_grad.reshape(rows, seq_len)


def solution(mesh):
    n_seq, n_chan = mesh.shape["seq"], mesh.shape["chan"]
    n_far = math.gcd(n_chan, 4)
    parts = Mesh(mesh.devices.reshape(n_seq, n_far, n_chan // n_far), ("seq", "far", "near"))
    chan = ("far", "near")
    return jax.shard_map(
        functools.partial(local, n_seq, n_far, n_chan // n_far),
        mesh=parts,
        in_specs=(P(chan, "seq"), P(chan, "seq"), P(chan, "seq"), P(chan, "seq"), P(), P()),
        out_specs=(P(("seq", *chan), None), P(chan, "seq")),
        check_vma=False,
    )
```

time: 47.1 us -> 43.5 us (0.924)
  the two profiles are of different devices: /device:TPU:0 before, /device:TPU:1 now
where the time goes in v3:
time: 43.5 us; the launch traced here: 43.2 us
  waiting for transfers between devices  15 us (34%)
  Pallas kernels  13.8 us (32%)
  starting transfers between devices  13.6 us (31%)
  between operations  0.7 us (2%)
    ppermute x3, waiting for transfers between devices, local(): lax.ppermute(taps_block[k], 'seq', route(k))  6.69 us
    all_to_all x1, starting transfers between devices, local(): spread = lax.all_to_all(grads, ('near', 'seq', 'far'), 0, 0, tiled=True)  5.96 us
    pallas_call x2, Pallas kernels, local(): pl.pallas_call(functools.partial(mixer_kernel, n_seq, size if size <= 24...  5.47 us
    ppermute x6, starting transfers between devices, local(): got[chunk, k] = lax.ppermute(block, 'seq', route(k)) if k else block  5.44 us
    ppermute x6, waiting for transfers between devices, local(): got[chunk, k] = lax.ppermute(block, 'seq', route(k)) if k else block  4.57 us
    all_to_all x1, waiting for transfers between devices, local(): spread = lax.all_to_all(grads, ('near', 'seq', 'far'), 0, 0, tiled=True)  3.79 us
    pallas_call x1, Pallas kernels, local(): pl.pallas_call(functools.partial(project_kernel, n_seq, n_far, n_near, si...  2.99 us
    pallas_call x2, Pallas kernels, prep(): pl.pallas_call(functools.partial(prep_kernel, steps, len(tables)), out_sh...  2.77 us
  transfers between devices with their start and end apart: 10, of which 5 were waited for; matrix products, arithmetic and copies ran while one was open for 0% of the time, Pallas kernels for 16%

profile of v3, /device:TPU:1, one launch (start us, length us, event | category | flops | bytes accessed | tf_op | source)
XLA Modules:
  0.0 43.2 jit_solution(7772875148478436777)
XLA Ops:
  0.6 1.2 %prep.3 = (bf16[4,16,1024]{2,1,0:T(8,128)(2,1)S(1)}, bf16[4,16,1024]{2,1,0:T(8,128)(2,1)S(1)}, bf16[4,16,1024]{2,1,0:T(8,128)(2,1)S(1)}, bf16[4,16,1024]{2,1,0:T(8,128)(2,1)S(1)}) custom-call(bf16[128,1024]{1,0:T(8,128)(2,1)} %values.3, f32[128,1024]{1,0:T(8,128)} %filter_taps.3, bf16[128,1024]{1,0:T(8,128)(2,1)} %cotangent.3, bf16[128,1024]{1,0:T(8,128)(2,1)} %gate_acts.3), custom_call_target="tpu_custom_call" | custom-call | bytes 4194304 | tf_op jit(solution)/shard_map/prep/pallas_call | solution.py:300
  1.9 2.1 %collective-permute-start.4 = (bf16[4,16,1024]{2,1,0:T(8,128)(2,1)S(1)}, bf16[4,16,1024]{2,1,0:T(8,128)(2,1)S(1)}, u32[]{:S(2)}, u32[]{:S(2)}) collective-permute-start(bf16[4,16,1024]{2,1,0:T(8,128)(2,1)S(1)} %get-tuple-element.36), channel_id=1, source_target_pairs={{0,16},{8,24},{16,0},{24,8},{1,17},{9,25},{17,1},{25,9},{2,18},{10... | collective-permute-start | bytes 393224 | tf_op jit(solution)/shard_map/ppermute | solution.py:333
  4.0 0.6 %collective-permute-start.5 = (bf16[4,16,1024]{2,1,0:T(8,128)(2,1)S(1)}, bf16[4,16,1024]{2,1,0:T(8,128)(2,1)S(1)}, u32[]{:S(2)}, u32[]{:S(2)}) collective-permute-start(bf16[4,16,1024]{2,1,0:T(8,128)(2,1)S(1)} %get-tuple-element.37), channel_id=1, source_target_pairs={{0,24},{8,16},{16,8},{24,0},{1,25},{9,17},{17,9},{25,1},{2,26},{10... | collective-permute-start | bytes 393224 | tf_op jit(solution)/shard_map/ppermute | solution.py:333
  4.6 1.5 %prep.2 = (bf16[4,16,1024]{2,1,0:T(8,128)(2,1)S(1)}, bf16[4,16,1024]{2,1,0:T(8,128)(2,1)S(1)}, bf16[4,16,1024]{2,1,0:T(8,128)(2,1)S(1)}, bf16[4,16,1024]{2,1,0:T...) custom-call(bf16[128,1024]{1,0:T(8,128)(2,1)} %values.3, ...), custom_call_target="tpu_custom_call" | custom-call | bytes 4194304 | tf_op jit(solution)/shard_map/prep/pallas_call | solution.py:300
  6.2 0.4 collective-permute-start.3
  6.5 1.4 %collective-permute-start.1 = (bf16[4,16,1024]{2,1,0:T(8,128)(2,1)S(1)}, bf16[4,16,1024]{2,1,0:T(8,128)(2,1)S(1)}, u32[]{:S(2)}, u32[]{:S(2)}) collective-permute-start(bf16[4,16,1024]{2,1,0:T(8,128)(2,1)S(1)} %get-tuple-element.25), channel_id=1, source_target_pairs={{0,16},{8,24},{16,0},{24,8},{1,17},{9,25},{17,1},{25,9},{2,18},{10... | collective-permute-start | bytes 393224 | tf_op jit(solution)/shard_map/ppermute | solution.py:333
  8.0 0.4 collective-permute-start.2
  8.4 0.0 collective-permute-done.4.rest_2_
  8.4 0.5 %collective-permute-start = (bf16[4,16,1024]{2,1,0:T(8,128)(2,1)S(1)}, bf16[4,16,1024]{2,1,0:T(8,128)(2,1)S(1)}, u32[]{:S(2)}, u32[]{:S(2)}) collective-permute-start(bf16[4,16,1024]{2,1,0:T(8,128)(2,1)S(1)} %get-tuple-element.24), channel_id=1, source_target_pairs={{0,8},{8,0},{16,24},{24,16},{1,9},{9,1},{17,25},{25,17},{2,10},{10... | collective-permute-start | bytes 393224 | tf_op jit(solution)/shard_map/ppermute | solution.py:333
  8.9 2.1 %collective-permute-done.5.rest_3_ = bf16[4,16,1024]{2,1,0:T(8,128)(2,1)S(1)} collective-permute-done((bf16[4,16,1024]{2,1,0:T(8,128)(2,1)S(1)}, bf16[4,16,1024]{2,1,0:T(8,128)(2,1)S(1)}, u32[]{:S(2)}, u32[]{:S(2)}) %collective-permute-start.5) | collective-permute-done | bytes 131104 | tf_op jit(solution)/shard_map/ppermute | solution.py:333
  11.0 0.0 collective-permute-done.3.rest_1_
  11.0 2.7 %mixer.2 = (bf16[32,64,128]{2,1,0:T(8,128)(2,1)}, f32[4,16,1024]{2,1,0:T(8,128)S(1)}) custom-call(bf16[4,16,1024]{2,1,0:T(8,128)(2,1)S(1)} %get-tuple-element.34.rest_0_, bf16[4,16,1024]{2,1,0:T(8,128)(2,1)S(1)} %collective-permute-done.3.rest_1_, bf16[4,16,1024]{2,1,0:T(8,128)(2,1)S(1)} %collective-permute-done.4.rest_2_, ...), custom_call_target="tpu_custom_call" | custom-call | flops 5000000000 | bytes 2097152 | tf_op jit(solution)/shard_map/mixer/pallas_call | solution.py:350
  13.7 0.0 collective-permute-done.1.rest_2_
  13.7 2.4 %collective-permute-done.2.rest_3_ = bf16[4,16,1024]{2,1,0:T(8,128)(2,1)S(1)} collective-permute-done((bf16[4,16,1024]{2,1,0:T(8,128)(2,1)S(1)}, bf16[4,16,1024]{2,1,0:T(8,128)(2,1)S(1)}, u32[]{:S(2)}, u32[]{:S(2)}) %collective-permute-start.2) | collective-permute-done | bytes 131104 | tf_op jit(solution)/shard_map/ppermute | solution.py:333
  16.2 0.0 collective-permute-done.rest_1_
  16.2 2.8 %mixer.3 = (bf16[32,64,128]{2,1,0:T(8,128)(2,1)}, bf16[4,32,1024]{2,1,0:T(8,128)(2,1)S(1)}) custom-call(bf16[4,16,1024]{2,1,0:T(8,128)(2,1)S(1)} %get-tuple-element.23.rest_0_, bf16[4,16,1024]{2,1,0:T(8,128)(2,1)S(1)} %collective-permute-done.rest_1_, bf16[4,16,1024]{2,1,0:T(8,128)(2,1)S(1)} %collective-permute-done.1.rest_2_, ...), custom_call_target="tpu_custom_call", output_to_operand_aliasing={{0}: (11, {})} | custom-call | flops 5000000000 | bytes 2097152 | tf_op jit(solution)/shard_map/mixer/pallas_call | solution.py:350
  18.9 6.0 %all-to-all-start = ((bf16[32,64,128]{2,1,0:T(8,128)(2,1)}), bf16[32,64,128]{2,1,0:T(8,128)(2,1)S(1)}, u32[]{:S(2)}, u32[]{:S(2)}) async-start(bf16[32,64,128]{2,1,0:T(8,128)(2,1)} %get-tuple-element.42), calls=%async_computation | async-start | bytes 1048576 | tf_op jit(solution)/shard_map/all_to_all | solution.py:371
  24.9 1.7 %collective-permute-start.8 = (bf16[32,1024]{1,0:T(8,128)(2,1)S(1)}, bf16[32,1024]{1,0:T(8,128)(2,1)S(1)}, u32[]{:S(2)}, u32[]{:S(2)}) collective-permute-start(bf16[32,1024]{1,0:T(8,128)(2,1)S(1)} %get-tuple-element.44), channel_id=1, source_target_pairs={{0,24},{8,16},{16,8},{24,0},{1,25},{9,17},{17,9},{25,1},{2,26},{10... | collective-permute-start | bytes 196616 | tf_op jit(solution)/shard_map/ppermute | solution.py:373
  26.6 0.0 collective-permute-start.7
  26.6 0.5 %collective-permute-start.6 = (bf16[32,1024]{1,0:T(8,128)(2,1)S(1)}, bf16[32,1024]{1,0:T(8,128)(2,1)S(1)}, u32[]{:S(2)}, u32[]{:S(2)}) collective-permute-start(bf16[32,1024]{1,0:T(8,128)(2,1)S(1)} %get-tuple-element.46), channel_id=1, source_target_pairs={{0,8},{8,0},{16,24},{24,16},{1,9},{9,1},{17,25},{25,17},{2,10},{10... | collective-permute-start | bytes 196616 | tf_op jit(solution)/shard_map/ppermute | solution.py:373
  27.1 5.9 %collective-permute-done.8.rest_3_ = bf16[32,1024]{1,0:T(8,128)(2,1)S(1)} collective-permute-done((bf16[32,1024]{1,0:T(8,128)(2,1)S(1)}, bf16[32,1024]{1,0:T(8,128)(2,1)S(1)}, u32[]{:S(2)}, u32[]{:S(2)}) %collective-permute-start.8) | collective-permute-done | bytes 65568 | tf_op jit(solution)/shard_map/ppermute | solution.py:373
  33.0 0.8 %collective-permute-done.7.rest_2_ = bf16[32,1024]{1,0:T(8,128)(2,1)S(1)} collective-permute-done((bf16[32,1024]{1,0:T(8,128)(2,1)S(1)}, bf16[32,1024]{1,0:T(8,128)(2,1)S(1)}, u32[]{:S(2)}, u32[]{:S(2)}) %collective-permute-start.7) | collective-permute-done | bytes 65568 | tf_op jit(solution)/shard_map/ppermute | solution.py:373
  33.8 0.0 collective-permute-done.6.rest_1_
  33.8 2.6 %taps.1 = (f32[4,32,1024]{2,1,0:T(8,128)}, bf16[1408,1024]{1,0:T(8,128)(2,1)S(1)}) custom-call(bf16[1024,1024]{1,0:T(8,128)(2,1)} %w_value.1, bf16[1024,1024]{1,0:T(8,128)(2,1)} %w_gate.3, bf16[32,1024]{1,0:T(8,128)(2,1)S(1)} %get-tuple-element.47.rest_0_, bf16[32,1024]{1,0:T(8,128)(2,1)S(1)} %collective-permute-done.6.rest_1_, ...), custom_call_target="tpu_custom_call" | custom-call | tf_op jit(solution)/shard_map/taps/pallas_call | solution.py:374
  36.4 3.8 %all-to-all-done.spread = bf16[32,64,128]{2,1,0:T(8,128)(2,1)S(1)} async-done(((bf16[32,64,128]{2,1,0:T(8,128)(2,1)}), bf16[32,64,128]{2,1,0:T(8,128)(2,1)S(1)}, u32[]{:S(2)}, u32[]{:S(2)}) %all-to-all-start) | async-done | bytes 524320 | tf_op jit(solution)/shard_map/all_to_all | solution.py:371
  40.2 3.0 %project.1 = bf16[128,1024]{1,0:T(8,128)(2,1)} custom-call(bf16[1408,1024]{1,0:T(8,128)(2,1)S(1)} %get-tuple-element.41.w_held, bf16[1024,1024]{1,0:T(8,128)(2,1)} %w_gate.3, bf16[32,64,128]{2,1,0:T(8,128)(2,1)S(1)} %all-to-all-done.spread), custom_call_target="tpu_custom_call" | custom-call | tf_op jit(solution)/shard_map/project/pallas_call | solution.py:389
  (1 shorter events, 0.0 us)
Async XLA Ops:
  1.9 6.5 %collective-permute-start.4 = (bf16[4,16,1024]{2,1,0:T(8,128)(2,1)S(1)}, bf16[4,16,1024]{2,1,0:T(8,128)(2,1)S(1)}, u32[]{:S(2)}, u32[]{:S(2)}) collective-permute-start(bf16[4,16,1024]{2,1,0:T(8,128)(2,1)S(1)} %get-tuple-element.36), channel_id=1, source_target_pairs={{0,16},{8,24},{16,0},{24,8},{1,17},{9,25},{17,1},{25,9},{2,18},{10... | collective-permute-start | bytes 393224 | tf_op jit(solution)/shard_map/ppermute | solution.py:333
  4.0 7.0 %collective-permute-start.5 = (bf16[4,16,1024]{2,1,0:T(8,128)(2,1)S(1)}, bf16[4,16,1024]{2,1,0:T(8,128)(2,1)S(1)}, u32[]{:S(2)}, u32[]{:S(2)}) collective-permute-start(bf16[4,16,1024]{2,1,0:T(8,128)(2,1)S(1)} %get-tuple-element.37), channel_id=1, source_target_pairs={{0,24},{8,16},{16,8},{24,0},{1,25},{9,17},{17,9},{25,1},{2,26},{10... | collective-permute-start | bytes 393224 | tf_op jit(solution)/shard_map/ppermute | solution.py:333
  6.2 4.8 %collective-permute-start.3 = (bf16[4,16,1024]{2,1,0:T(8,128)(2,1)S(1)}, bf16[4,16,1024]{2,1,0:T(8,128)(2,1)S(1)}, u32[]{:S(2)}, u32[]{:S(2)}) collective-permute-start(bf16[4,16,1024]{2,1,0:T(8,128)(2,1)S(1)} %get-tuple-element.35), channel_id=1, source_target_pairs={{0,8},{8,0},{16,24},{24,16},{1,9},{9,1},{17,25},{25,17},{2,10},{10... | collective-permute-start | bytes 393224 | tf_op jit(solution)/shard_map/ppermute | solution.py:333
  6.5 7.2 %collective-permute-start.1 = (bf16[4,16,1024]{2,1,0:T(8,128)(2,1)S(1)}, bf16[4,16,1024]{2,1,0:T(8,128)(2,1)S(1)}, u32[]{:S(2)}, u32[]{:S(2)}) collective-permute-start(bf16[4,16,1024]{2,1,0:T(8,128)(2,1)S(1)} %get-tuple-element.25), channel_id=1, source_target_pairs={{0,16},{8,24},{16,0},{24,8},{1,17},{9,25},{17,1},{25,9},{2,18},{10... | collective-permute-start | bytes 393224 | tf_op jit(solution)/shard_map/ppermute | solution.py:333
  8.0 8.2 %collective-permute-start.2 = (bf16[4,16,1024]{2,1,0:T(8,128)(2,1)S(1)}, bf16[4,16,1024]{2,1,0:T(8,128)(2,1)S(1)}, u32[]{:S(2)}, u32[]{:S(2)}) collective-permute-start(bf16[4,16,1024]{2,1,0:T(8,128)(2,1)S(1)} %get-tuple-element.26), channel_id=1, source_target_pairs={{0,24},{8,16},{16,8},{24,0},{1,25},{9,17},{17,9},{25,1},{2,26},{10... | collective-permute-start | bytes 393224 | tf_op jit(solution)/shard_map/ppermute | solution.py:333
  8.4 7.8 %collective-permute-start = (bf16[4,16,1024]{2,1,0:T(8,128)(2,1)S(1)}, bf16[4,16,1024]{2,1,0:T(8,128)(2,1)S(1)}, u32[]{:S(2)}, u32[]{:S(2)}) collective-permute-start(bf16[4,16,1024]{2,1,0:T(8,128)(2,1)S(1)} %get-tuple-element.24), channel_id=1, source_target_pairs={{0,8},{8,0},{16,24},{24,16},{1,9},{9,1},{17,25},{25,17},{2,10},{10... | collective-permute-start | bytes 393224 | tf_op jit(solution)/shard_map/ppermute | solution.py:333
  18.9 21.3 %all-to-all-start = ((bf16[32,64,128]{2,1,0:T(8,128)(2,1)}), bf16[32,64,128]{2,1,0:T(8,128)(2,1)S(1)}, u32[]{:S(2)}, u32[]{:S(2)}) async-start(bf16[32,64,128]{2,1,0:T(8,128)(2,1)} %get-tuple-element.42), calls=%async_computation | async-start | bytes 1048576 | tf_op jit(solution)/shard_map/all_to_all | solution.py:371
  24.9 8.1 %collective-permute-start.8 = (bf16[32,1024]{1,0:T(8,128)(2,1)S(1)}, bf16[32,1024]{1,0:T(8,128)(2,1)S(1)}, u32[]{:S(2)}, u32[]{:S(2)}) collective-permute-start(bf16[32,1024]{1,0:T(8,128)(2,1)S(1)} %get-tuple-element.44), channel_id=1, source_target_pairs={{0,24},{8,16},{16,8},{24,0},{1,25},{9,17},{17,9},{25,1},{2,26},{10... | collective-permute-start | bytes 196616 | tf_op jit(solution)/shard_map/ppermute | solution.py:373
  26.6 7.2 %collective-permute-start.7 = (bf16[32,1024]{1,0:T(8,128)(2,1)S(1)}, bf16[32,1024]{1,0:T(8,128)(2,1)S(1)}, u32[]{:S(2)}, u32[]{:S(2)}) collective-permute-start(bf16[32,1024]{1,0:T(8,128)(2,1)S(1)} %get-tuple-element.45), channel_id=1, source_target_pairs={{0,16},{8,24},{16,0},{24,8},{1,17},{9,25},{17,1},{25,9},{2,18},{10... | collective-permute-start | bytes 196616 | tf_op jit(solution)/shard_map/ppermute | solution.py:373
  26.6 7.2 %collective-permute-start.6 = (bf16[32,1024]{1,0:T(8,128)(2,1)S(1)}, bf16[32,1024]{1,0:T(8,128)(2,1)S(1)}, u32[]{:S(2)}, u32[]{:S(2)}) collective-permute-start(bf16[32,1024]{1,0:T(8,128)(2,1)S(1)} %get-tuple-element.46), channel_id=1, source_target_pairs={{0,8},{8,0},{16,24},{24,16},{1,9},{9,1},{17,25},{25,17},{2,10},{10... | collective-permute-start | bytes 196616 | tf_op jit(solution)/shard_map/ppermute | solution.py:373

commit v4 on v3

v4 whole, which is shorter than its diff:
```python
import functools
import math

import jax
import jax.numpy as jnp
import numpy as np
from jax import lax
from jax.experimental import pallas as pl
from jax.experimental.pallas import tpu as pltpu
from jax.sharding import Mesh
from jax.sharding import PartitionSpec as P

LANES = 128
VALUE, TAPS, COT, GATE = range(4)
SLABS = 8
KEPT = 3
PAD = 8


def halves(table):
    high = table.astype(jnp.bfloat16)
    low = (table - high.astype(np.float64)).astype(jnp.bfloat16)
    return high, low


def dft_tables(total, n_seq):
    outer = total // LANES
    k1 = np.arange(outer) + 0.25
    a = np.arange(outer)
    b = np.arange(LANES)
    first = np.exp(-2j * np.pi * np.outer(k1, a) / outer)
    first = np.concatenate([first.real, first.imag], 0)
    turn = np.exp(-2j * np.pi * np.outer(k1, b) / total)
    second = np.exp(-2j * np.pi * np.outer(b, b) / LANES)
    second = np.block([[second.real, second.imag], [-second.imag, second.real]])
    back_second = second.T / total / math.sqrt(total)
    back_first = np.exp(2j * np.pi * np.outer(a, k1) / outer)
    back_first = np.concatenate([back_first.real, -back_first.imag], 1)

    parts = first.reshape(2 * outer, n_seq, outer // n_seq)
    orders = np.arange(n_seq)[:, None] ^ np.arange(n_seq)
    first = np.stack([parts[:, order].reshape(2 * outer, outer) for order in orders])
    f_hi, f_lo = halves(first)
    s_hi, s_lo = halves(second)
    bs_hi, bs_lo = halves(back_second)
    bf_hi, bf_lo = halves(back_first)
    return (
        np.concatenate([f_hi, f_lo], 2),
        np.concatenate([f_hi, f_hi, f_lo], 2),
        np.concatenate([s_hi, s_hi, s_lo], 0),
        turn.real.astype(np.float32),
        turn.imag.astype(np.float32),
        np.concatenate([bs_hi, bs_hi, bs_lo], 0),
        np.concatenate([bf_hi, bf_hi, bf_lo], 1),
    )


def split_terms(x):
    high = x.astype(jnp.bfloat16)
    low = (x - high.astype(jnp.float32)).astype(jnp.bfloat16)
    return high, low


def dot(left, right):
    return jnp.dot(left, right, preferred_element_type=jnp.float32)


def wide_dot(x, table):
    high, low = split_terms(x)
    return dot(jnp.concatenate([high, low, high], 1), table)


def prep_kernel(pairs, n_tables, values, filter_taps, cotangent, gate_acts, *rest):
    tables, rest = rest[:n_tables], rest[n_tables:]
    (narrow, wide, sems, table_sems), rest = rest[-4:], rest[:-4]
    outs, held = rest[: len(rest) - n_tables], rest[len(rest) - n_tables :]
    me = lax.axis_index("seq")
    channels = wide.shape[1] // 2
    n_steps = 2 * len(pairs)
    copies = []
    for at, j in enumerate(pairs):
        start = lax.bitwise_xor(lax.shift_right_logical(me, 1), j) * (2 * channels)
        both = pl.ds(pl.multiple_of(start, 2 * channels), 2 * channels)
        copies.append([pltpu.make_async_copy(filter_taps.at[both, :], wide.at[at], sems.at[at, 3])])
        for i, ref in enumerate((values, cotangent, gate_acts)):
            copies[-1].append(pltpu.make_async_copy(ref.at[both, :], narrow.at[at, i], sems.at[at, i]))
        for copy in copies[-1]:
            copy.start()
    brought = [
        pltpu.make_async_copy(tables[i].at[me] if i < 2 else tables[i], held[i], table_sems.at[i])
        for i in range(n_tables)
    ]
    for copy in brought:
        copy.start()
    for at in range(len(pairs)):
        for copy in copies[at]:
            copy.wait()
        for low in range(2):
            side = lax.bitwise_xor(lax.bitwise_and(me, 1), low) * channels
            mine = pl.ds(pl.multiple_of(side, channels), channels)
            blocks = [wide[at, mine, :], *(narrow[at, i, mine, :].astype(jnp.float32) for i in range(3))]
            for field, block in zip((TAPS, VALUE, COT, GATE), blocks):
                first = 0
                for out in outs[2 * at + low :: n_steps]:
                    size = out.shape[1]
                    out[field] = block[first : first + size].astype(jnp.bfloat16)
                    first += size
    for copy in brought:
        copy.wait()


def in_block(body):
    pl.when(lax.axis_index("seq") >= 0)(body)


def run_behind(tasks):
    tasks, live = list(tasks), []
    while tasks or live:
        live = [task for task in live if next(task, StopIteration) is None]
        if tasks:
            live.append(tasks.pop(0))
            next(live[-1])


def inverse(get, group, outer, turn, tables, put):
    (tr, ti), (bs3, bf3) = turn, tables
    high, low = split_terms(get())
    yield
    mid = dot(jnp.concatenate([high, low, high], 1), bs3[...])
    yield
    terms = []
    for pair in range(group // 2):
        cols = []
        for i in range(2):
            rows = slice((2 * pair + i) * outer, (2 * pair + i + 1) * outer)
            re, im = mid[rows, :LANES], mid[rows, LANES:]
            cols.append(jnp.concatenate([re * tr + im * ti, im * tr - re * ti], 0))
        terms.append(split_terms(jnp.concatenate(cols, 1)))
    yield
    ys = [dot(bf3[...], jnp.concatenate([high, low, high], 0)) for high, low in terms]
    yield
    for pair, y in enumerate(ys):
        for i in range(2):
            put(2 * pair + i, y[:, i * LANES : (i + 1) * LANES])
    yield


def taps_part(taps32, channels, source, part, own_outer):
    start = (source * own_outer + part) * (channels + PAD)
    start = pl.multiple_of(start, PAD) if channels % PAD == 0 else start
    return taps32[pl.ds(start, channels), :]


def mixer_kernel(n_seq, group, offset, places, last, *rest):
    blocks, rest = rest[:n_seq], rest[n_seq:]
    (f2, f3, s3, turn_re, turn_im, bs3, bf3), rest = rest[:7], rest[7:]
    if offset:
        rest = rest[1:]
    if last:
        grads, products, sig, taps, up, cot, grads32, grads16, sems = rest
    else:
        grads, taps_out, sig, taps, up, cot, grads32, grads16, sems, taps32 = rest
    me = lax.axis_index("seq")
    _, channels, seq_len = blocks[0].shape
    outer = sig.shape[0] // channels - PAD
    pitch, wide, narrow = outer + PAD, 2 * channels + PAD, channels + PAD
    own_outer = seq_len // LANES

    def stage(field, ref):
        for k in range(n_seq):
            for part in range(own_outer):
                cols = pl.ds(part * LANES, LANES)
                x = blocks[k][field, :, cols].astype(jnp.float32)
                rows = pl.ds(k * own_outer + part, channels, stride=pitch)
                if field == COT:
                    source = lax.bitwise_xor(me, k)
                    cot[pl.ds(source * own_outer + part, channels, stride=pitch), :] = x
                    x = x * blocks[k][GATE, :, cols].astype(jnp.float32)
                ref[rows, :] = x

    tr, ti = turn_re[...], turn_im[...]

    def forward(ref, field, base, out):
        exact = field != COT
        if base == 0:
            stage(field, ref)
        yield
        turned = []
        ys = []
        for pair in range(group // 2):
            xs = [ref[pl.ds((base + 2 * pair + i) * pitch, outer), :] for i in range(2)]
            x = jnp.concatenate(xs, 1)
            if exact:
                high = x.astype(jnp.bfloat16)
                ys.append(dot(f2[...], jnp.concatenate([high, high], 0)))
            else:
                high, low = split_terms(x)
                ys.append(dot(f3[...], jnp.concatenate([high, low, high], 0)))
        yield
        for y in ys:
            for i in range(2):
                re = y[:outer, i * LANES : (i + 1) * LANES]
                im = y[outer:, i * LANES : (i + 1) * LANES]
                turned.append(jnp.concatenate([re * tr - im * ti, re * ti + im * tr], 1))
        high, low = split_terms(jnp.concatenate(turned, 0))
        yield
        spec = dot(jnp.concatenate([high, low, high], 1), s3[...])
        out += [spec[:, :LANES], spec[:, LANES:]]
        yield

    def times(left, right, conj):
        (ar, ai), (br, bi) = left, right
        if conj:
            return jnp.concatenate([ar * br + ai * bi, ai * br - ar * bi], 1)
        return jnp.concatenate([ar * br - ai * bi, ar * bi + ai * br], 1)

    def backward(left, right, conj, base, put):
        yield
        yield from inverse(
            lambda: times(left, right, conj), group, outer, (tr, ti), (bs3, bf3), lambda ch, y: put(base + ch, y)
        )

    def keep_product(left, right, base):
        products[pl.ds(base * outer, group * outer), :] = times(left, right, True)
        yield

    copies = []

    def send(side):
        rows = slice(side * channels, (side + 1) * channels)
        for a in range(outer):
            grads16[side, places[a]] = grads32[a * wide + rows.start : a * wide + rows.stop, :].astype(jnp.bfloat16)
        to = grads.at[:, pl.ds(2 * offset + side * channels, channels), :]
        copies.append(pltpu.make_async_copy(grads16.at[side], to, sems.at[side]))
        copies[-1].start()

    def put_gate(ch, y):
        held = cot[pl.ds(ch * pitch, outer), :]
        grads32[pl.ds(channels + ch, outer, stride=wide), :] = y * held
        if ch == channels - 1:
            send(1)

    def put_value(ch, y):
        grads32[pl.ds(ch, outer, stride=wide), :] = y
        if ch == channels - 1:
            send(0)

    def put_taps(ch, y):
        taps32[pl.ds(ch, outer, stride=narrow), :] = y

    tasks = []
    for base in range(0, channels, group):
        k, v, u = [], [], []
        tasks += [
            forward(taps, TAPS, base, k),
            forward(sig, VALUE, base, v),
            forward(up, COT, base, u),
            backward(k, v, False, base, put_gate),
            backward(u, k, True, base, put_value),
            keep_product(u, v, base) if last else backward(u, v, True, base, put_taps),
        ]
    run_behind(tasks)

    if not last:
        for k in range(n_seq):
            source = lax.bitwise_xor(me, k)
            for part in range(own_outer):
                taps_out[k, :, pl.ds(part * LANES, LANES)] = taps_part(taps32, channels, source, part, own_outer)
    for copy in copies:
        copy.wait()


def lags_kernel(n_seq, group, channels, products, turn_re, turn_im, bs3, bf3, *rest):
    outs, taps32 = rest[-n_seq - 1 : -1], rest[-1]
    before = rest[: -n_seq - 1]
    me = lax.axis_index("seq")
    outer = products.shape[0] // channels
    own_outer = outs[0].shape[1] // LANES

    def put(ch, y):
        taps32[pl.ds(ch, outer, stride=channels + PAD), :] = y

    turn = turn_re[...], turn_im[...]

    def task(base):
        rows = pl.ds(base * outer, group * outer)
        return inverse(
            lambda: products[rows, :], group, outer, turn, (bs3, bf3), lambda ch, y: put(base + ch, y)
        )

    run_behind(task(base) for base in range(0, channels, group))
    for k in range(n_seq):
        source = lax.bitwise_xor(me, k)
        for part in range(own_outer):
            cols = pl.ds(part * LANES, LANES)
            parts = [x[k, :, cols] for x in before] + [taps_part(taps32, channels, source, part, own_outer)]
            outs[k][:, cols] = jnp.concatenate(parts, 0).astype(jnp.bfloat16)


def taps_kernel(n_seq, w_value, w_gate, *rest):
    taps_in, (out, w_held, sems) = rest[:n_seq], rest[n_seq:]
    me = lax.axis_index("seq")
    rows = w_value.shape[0]
    keep = w_held.shape[0] - rows
    copies = [
        pltpu.make_async_copy(w_value, w_held.at[:rows, :], sems.at[0]),
        pltpu.make_async_copy(w_gate.at[:keep, :], w_held.at[rows:, :], sems.at[1]),
    ]
    for copy in copies:
        copy.start()
    for k in range(n_seq):
        out[lax.bitwise_xor(me, k)] = taps_in[k][...].astype(jnp.float32)
    for copy in copies:
        copy.wait()


def project_kernel(n_seq, n_far, n_near, sizes, w_held, w_gate, spread, out, held, gate_held, total, sem):
    features = w_gate.shape[0]
    split = features - gate_held.shape[0]
    copy = pltpu.make_async_copy(w_gate.at[split:, :], gate_held, sem)
    copy.start()
    share = sum(sizes)
    firsts = [sum(sizes[:i]) for i in range(len(sizes))]

    def before():
        for source, (near, s, far) in enumerate(np.ndindex(n_near, n_seq, n_far)):
            block = spread[source].astype(jnp.float32)
            rows = pl.ds(((far * n_near + near) * n_seq + s) * share, share)
            for g in range(2):
                pieces = [block[2 * at + g * size : 2 * at + (g + 1) * size] for at, size in zip(firsts, sizes)]
                held[g, rows, :] = jnp.concatenate(pieces, 0).astype(held.dtype)
        values, gates = (held[g].astype(jnp.bfloat16) for g in range(2))
        total[...] = dot(w_held[:features, :], values)
        out[:, :split] = (total[:split, :] + dot(w_held[features:, :], gates)).T.astype(jnp.bfloat16)

    in_block(before)
    copy.wait()
    gates = held[1].astype(jnp.bfloat16)
    out[:, split:] = (total[split:, :] + dot(gate_held[...], gates)).T.astype(jnp.bfloat16)


def local(n_seq, n_far, n_near, values, gate_acts, cotangent, filter_taps, w_value, w_gate):
    rows, seq_len = values.shape
    n_chan = n_far * n_near
    total = seq_len * n_seq
    channels = rows // n_seq
    outer = total // LANES
    tokens = total // (n_seq * n_chan)
    me = lax.axis_index("seq")
    vmem = pl.BlockSpec(memory_space=pltpu.VMEM)
    hbm = pl.BlockSpec(memory_space=pltpu.HBM)

    def like(x):
        return pltpu.VMEM(x.shape, x.dtype)

    def stay(x):
        return pltpu.with_memory_space_constraint(x, pltpu.HBM)

    def route(k):
        return [(i, i ^ k) for i in range(n_seq)]

    sizes = (channels // 2, channels // 2) if channels % 32 == 0 else (channels,)
    chunks = len(sizes)
    tables = [jnp.asarray(t) for t in dft_tables(total, n_seq)]

    def prep(pairs, tables):
        steps = [2 * j + low for j in pairs for low in range(2)]
        outs = [pltpu.VMEM((4, size, seq_len), jnp.bfloat16) for size in sizes for _ in steps]
        outs += [pltpu.VMEM(t.shape[1:] if i < 2 else t.shape, t.dtype) for i, t in enumerate(tables)]
        ready = pl.pallas_call(
            functools.partial(prep_kernel, pairs, len(tables)),
            out_shape=outs,
            in_specs=[hbm] * (4 + len(tables)),
            out_specs=[vmem] * len(outs),
            scratch_shapes=[
                pltpu.VMEM((len(pairs), 3, 2 * channels, seq_len), jnp.bfloat16),
                pltpu.VMEM((len(pairs), 2 * channels, seq_len), jnp.float32),
                pltpu.SemaphoreType.DMA((len(pairs), 4)),
                pltpu.SemaphoreType.DMA((max(len(tables), 1),)),
            ],
            compiler_params=pltpu.CompilerParams(vmem_limit_bytes=8 * 2**20),
            cost_estimate=pl.CostEstimate(flops=0, bytes_accessed=4 * 2**20, transcendentals=0),
            name="prep",
        )(*(stay(x) for x in (values, filter_taps, cotangent, gate_acts, *tables)))
        for chunk in range(chunks):
            for at, k in enumerate(steps):
                sent[chunk, k] = ready[chunk * len(steps) + at]
        return ready[chunks * len(steps) :]

    sent, got = {}, {}
    if chunks > 1:
        prep(range(1, n_seq // 2), [])
        tables = prep((0,), tables)
    else:
        fields = (values, filter_taps.astype(jnp.bfloat16), cotangent, gate_acts)
        tables[:2] = [t[me] for t in tables[:2]]
        for k in range(n_seq):
            rows_k = [lax.dynamic_slice_in_dim(x, (me ^ k) * channels, channels, 0) for x in fields]
            sent[0, k] = jnp.stack(rows_k)
    for chunk in range(chunks):
        for k in reversed(range(n_seq)):
            block = sent[chunk, k]
            got[chunk, k] = lax.ppermute(block, "seq", route(k)) if k else block

    places = list(range(outer))
    if tokens == LANES:
        for s, far, near in np.ndindex(n_seq, n_far, n_near):
            places[(s * n_far + far) * n_near + near] = (near * n_seq + s) * n_far + far
    grads, before, offset = None, [], 0
    for chunk, size in enumerate(sizes):
        last = chunk == chunks - 1
        args = [*(got[chunk, k] for k in range(n_seq)), *tables]
        specs = [vmem] * len(args)
        aliases = {}
        if chunk:
            aliases = {len(args): 0}
            args.append(grads)
            specs.append(hbm)
        group = size if size <= 24 else 8
        long = pltpu.VMEM((size * (outer + PAD), LANES), jnp.float32)
        taps32 = pltpu.VMEM((outer * (size + PAD), LANES), jnp.float32)
        grads, more = pl.pallas_call(
            functools.partial(mixer_kernel, n_seq, group, offset, places, last),
            out_shape=[
                pltpu.HBM((outer, 2 * channels, LANES), jnp.bfloat16),
                pltpu.VMEM((size * outer, 2 * LANES) if last else (n_seq, size, seq_len), jnp.float32),
            ],
            in_specs=specs,
            out_specs=[hbm, vmem],
            input_output_aliases=aliases,
            scratch_shapes=[long] * 4
            + [
                pltpu.VMEM((outer * (2 * size + PAD), LANES), jnp.float32),
                pltpu.VMEM((2, outer, size, LANES), jnp.bfloat16),
                pltpu.SemaphoreType.DMA((2,)),
            ]
            + [taps32] * (not last),
            compiler_params=pltpu.CompilerParams(vmem_limit_bytes=24 * 2**20),
            cost_estimate=pl.CostEstimate(flops=5 * 10**9, bytes_accessed=2 * 2**20, transcendentals=0),
            name="mixer",
        )(*args)
        if not last:
            before.append(more)
        offset += size
    if tokens != LANES:
        grads = grads.reshape(outer, 2 * channels, LANES // tokens, tokens).transpose(0, 2, 1, 3)
        grads = grads.reshape(n_seq, n_far, n_near, 2 * channels, tokens).transpose(2, 0, 1, 3, 4)
        grads = grads.reshape(n_seq * n_chan, 2 * channels, tokens)
    spread = lax.all_to_all(grads, ("near", "seq", "far"), 0, 0, tiled=True)

    args = [more, *tables[3:], *before]
    taps_blocks = pl.pallas_call(
        functools.partial(lags_kernel, n_seq, group, size),
        out_shape=[jax.ShapeDtypeStruct((channels, seq_len), jnp.bfloat16)] * n_seq,
        in_specs=[vmem] * len(args),
        out_specs=[vmem] * n_seq,
        scratch_shapes=[taps32],
        compiler_params=pltpu.CompilerParams(vmem_limit_bytes=16 * 2**20),
        cost_estimate=pl.CostEstimate(flops=10**9, bytes_accessed=2**20, transcendentals=0),
        name="lags",
    )(*args)
    taps_got = [lax.ppermute(taps_blocks[k], "seq", route(k)) if k else taps_blocks[0] for k in range(n_seq)]
    taps_grad, w_held = pl.pallas_call(
        functools.partial(taps_kernel, n_seq),
        out_shape=[
            jax.ShapeDtypeStruct((n_seq, channels, seq_len), jnp.float32),
            pltpu.VMEM((w_value.shape[0] * (SLABS + KEPT) // SLABS, w_value.shape[1]), w_value.dtype),
        ],
        in_specs=[hbm] * 2 + [vmem] * n_seq,
        out_specs=[vmem] * 2,
        scratch_shapes=[pltpu.SemaphoreType.DMA((2,))],
        compiler_params=pltpu.CompilerParams(vmem_limit_bytes=8 * 2**20),
        name="taps",
    )(stay(w_value), stay(w_gate), *taps_got)

    held = jnp.bfloat16 if channels % 16 == 0 else jnp.float32
    args = [w_held, stay(w_gate), spread]
    input_grad = pl.pallas_call(
        functools.partial(project_kernel, n_seq, n_far, n_near, sizes),
        out_shape=jax.ShapeDtypeStruct((tokens, w_value.shape[0]), jnp.bfloat16),
        in_specs=[vmem, hbm, vmem],
        out_specs=vmem,
        scratch_shapes=[
            pltpu.VMEM((2, rows * n_chan, tokens), held),
            pltpu.VMEM((w_gate.shape[0] * (SLABS - KEPT) // SLABS, w_gate.shape[1]), w_gate.dtype),
            pltpu.VMEM((w_gate.shape[0], tokens), jnp.float32),
            pltpu.SemaphoreType.DMA,
        ],
        compiler_params=pltpu.CompilerParams(vmem_limit_bytes=16 * 2**20),
        name="project",
    )(*args)
    return input_grad, taps_grad.reshape(rows, seq_len)


def solution(mesh):
    n_seq, n_chan = mesh.shape["seq"], mesh.shape["chan"]
    n_far = math.gcd(n_chan, 4)
    parts = Mesh(mesh.devices.reshape(n_seq, n_far, n_chan // n_far), ("seq", "far", "near"))
    chan = ("far", "near")
    return jax.shard_map(
        functools.partial(local, n_seq, n_far, n_chan // n_far),
        mesh=parts,
        in_specs=(P(chan, "seq"), P(chan, "seq"), P(chan, "seq"), P(chan, "seq"), P(), P()),
        out_specs=(P(("seq", *chan), None), P(chan, "seq")),
        check_vma=False,
    )
```

time: 43.5 us -> 42.8 us (0.984)
  waiting for transfers between devices: 15 us -> 14.3 us
    ppermute x3, waiting for transfers between devices: 6.69 us -> 6.11 us  [local(): lax.ppermute(taps_blocks[k], 'seq', route(k))]
    pallas_call x4 -> x5, Pallas kernels: 8.24 us -> 8.66 us  [the longest x2 5.17 us: local(): pl.pallas_call(functools.partial(mixer_kernel, n_seq, group, offset, plac...]
  transfers between devices with their start and end apart: 10 -> 10, of which waited for: 5 -> 5; matrix products, arithmetic and copies ran while one was open for 0% -> 0% of each run, Pallas kernels for 16% -> 18%
where the time goes in v4:
time: 42.8 us; the launch traced here: 42.5 us
  waiting for transfers between devices  14.3 us (33%)
  Pallas kernels  13.8 us (32%)
  starting transfers between devices  13.6 us (32%)
  between operations  0.7 us (2%)
    ppermute x3, waiting for transfers between devices, local(): lax.ppermute(taps_blocks[k], 'seq', route(k))  6.11 us
    all_to_all x1, starting transfers between devices, local(): spread = lax.all_to_all(grads, ('near', 'seq', 'far'), 0, 0, tiled=True)  5.96 us
    ppermute x6, starting transfers between devices, local(): got[chunk, k] = lax.ppermute(block, 'seq', route(k)) if k else block  5.48 us
    pallas_call x2, Pallas kernels, local(): pl.pallas_call(functools.partial(mixer_kernel, n_seq, group, offset, plac...  5.17 us
    ppermute x6, waiting for transfers between devices, local(): got[chunk, k] = lax.ppermute(block, 'seq', route(k)) if k else block  4.62 us
    all_to_all x1, waiting for transfers between devices, local(): spread = lax.all_to_all(grads, ('near', 'seq', 'far'), 0, 0, tiled=True)  3.61 us
    pallas_call x2, Pallas kernels, prep(): pl.pallas_call(functools.partial(prep_kernel, pairs, len(tables)), out_sh...  2.72 us
    pallas_call x1, Pallas kernels, local(): pl.pallas_call(functools.partial(project_kernel, n_seq, n_far, n_near, si...  2.6 us
  transfers between devices with their start and end apart: 10, of which 5 were waited for; matrix products, arithmetic and copies ran while one was open for 0% of the time, Pallas kernels for 18%

profile of v4, /device:TPU:1, one launch (start us, length us, event | category | flops | bytes accessed | tf_op | source)
XLA Modules:
  0.0 42.5 jit_solution(5176686928789950588)
XLA Ops:
  0.6 1.2 %prep.3 = (bf16[4,16,1024]{2,1,0:T(8,128)(2,1)S(1)}, bf16[4,16,1024]{2,1,0:T(8,128)(2,1)S(1)}, bf16[4,16,1024]{2,1,0:T(8,128)(2,1)S(1)}, bf16[4,16,1024]{2,1,0:T(8,128)(2,1)S(1)}) custom-call(bf16[128,1024]{1,0:T(8,128)(2,1)} %values.3, f32[128,1024]{1,0:T(8,128)} %filter_taps.3, bf16[128,1024]{1,0:T(8,128)(2,1)} %cotangent.3, bf16[128,1024]{1,0:T(8,128)(2,1)} %gate_acts.3), custom_call_target="tpu_custom_call" | custom-call | bytes 4194304 | tf_op jit(solution)/shard_map/prep/pallas_call | solution.py:370
  1.8 2.1 %collective-permute-start.4 = (bf16[4,16,1024]{2,1,0:T(8,128)(2,1)S(1)}, bf16[4,16,1024]{2,1,0:T(8,128)(2,1)S(1)}, u32[]{:S(2)}, u32[]{:S(2)}) collective-permute-start(bf16[4,16,1024]{2,1,0:T(8,128)(2,1)S(1)} %get-tuple-element.40), channel_id=1, source_target_pairs={{0,16},{8,24},{16,0},{24,8},{1,17},{9,25},{17,1},{25,9},{2,18},{10... | collective-permute-start | bytes 393224 | tf_op jit(solution)/shard_map/ppermute | solution.py:403
  3.9 0.6 %collective-permute-start.5 = (bf16[4,16,1024]{2,1,0:T(8,128)(2,1)S(1)}, bf16[4,16,1024]{2,1,0:T(8,128)(2,1)S(1)}, u32[]{:S(2)}, u32[]{:S(2)}) collective-permute-start(bf16[4,16,1024]{2,1,0:T(8,128)(2,1)S(1)} %get-tuple-element.41), channel_id=1, source_target_pairs={{0,24},{8,16},{16,8},{24,0},{1,25},{9,17},{17,9},{25,1},{2,26},{10... | collective-permute-start | bytes 393224 | tf_op jit(solution)/shard_map/ppermute | solution.py:403
  4.6 1.5 %prep.2 = (bf16[4,16,1024]{2,1,0:T(8,128)(2,1)S(1)}, bf16[4,16,1024]{2,1,0:T(8,128)(2,1)S(1)}, bf16[4,16,1024]{2,1,0:T(8,128)(2,1)S(1)}, bf16[4,16,1024]{2,1,0:T...) custom-call(bf16[128,1024]{1,0:T(8,128)(2,1)} %values.3, ...), custom_call_target="tpu_custom_call" | custom-call | bytes 4194304 | tf_op jit(solution)/shard_map/prep/pallas_call | solution.py:370
  6.1 0.4 collective-permute-start.3
  6.5 1.4 %collective-permute-start.1 = (bf16[4,16,1024]{2,1,0:T(8,128)(2,1)S(1)}, bf16[4,16,1024]{2,1,0:T(8,128)(2,1)S(1)}, u32[]{:S(2)}, u32[]{:S(2)}) collective-permute-start(bf16[4,16,1024]{2,1,0:T(8,128)(2,1)S(1)} %get-tuple-element.29), channel_id=1, source_target_pairs={{0,16},{8,24},{16,0},{24,8},{1,17},{9,25},{17,1},{25,9},{2,18},{10... | collective-permute-start | bytes 393224 | tf_op jit(solution)/shard_map/ppermute | solution.py:403
  7.9 0.4 collective-permute-start.2
  8.3 0.0 collective-permute-done.4.rest_2_
  8.3 0.5 %collective-permute-start = (bf16[4,16,1024]{2,1,0:T(8,128)(2,1)S(1)}, bf16[4,16,1024]{2,1,0:T(8,128)(2,1)S(1)}, u32[]{:S(2)}, u32[]{:S(2)}) collective-permute-start(bf16[4,16,1024]{2,1,0:T(8,128)(2,1)S(1)} %get-tuple-element.28), channel_id=1, source_target_pairs={{0,8},{8,0},{16,24},{24,16},{1,9},{9,1},{17,25},{25,17},{2,10},{10... | collective-permute-start | bytes 393224 | tf_op jit(solution)/shard_map/ppermute | solution.py:403
  8.8 2.1 %collective-permute-done.5.rest_3_ = bf16[4,16,1024]{2,1,0:T(8,128)(2,1)S(1)} collective-permute-done((bf16[4,16,1024]{2,1,0:T(8,128)(2,1)S(1)}, bf16[4,16,1024]{2,1,0:T(8,128)(2,1)S(1)}, u32[]{:S(2)}, u32[]{:S(2)}) %collective-permute-start.5) | collective-permute-done | bytes 131104 | tf_op jit(solution)/shard_map/ppermute | solution.py:403
  11.0 0.0 collective-permute-done.3.rest_1_
  11.0 2.7 %mixer.2 = (bf16[32,64,128]{2,1,0:T(8,128)(2,1)}, f32[4,16,1024]{2,1,0:T(8,128)S(1)}) custom-call(bf16[4,16,1024]{2,1,0:T(8,128)(2,1)S(1)} %get-tuple-element.38.rest_0_, bf16[4,16,1024]{2,1,0:T(8,128)(2,1)S(1)} %collective-permute-done.3.rest_1_, bf16[4,16,1024]{2,1,0:T(8,128)(2,1)S(1)} %collective-permute-done.4.rest_2_, ...), custom_call_target="tpu_custom_call" | custom-call | flops 5000000000 | bytes 2097152 | tf_op jit(solution)/shard_map/mixer/pallas_call | solution.py:422
  13.6 0.0 collective-permute-done.1.rest_2_
  13.6 2.5 %collective-permute-done.2.rest_3_ = bf16[4,16,1024]{2,1,0:T(8,128)(2,1)S(1)} collective-permute-done((bf16[4,16,1024]{2,1,0:T(8,128)(2,1)S(1)}, bf16[4,16,1024]{2,1,0:T(8,128)(2,1)S(1)}, u32[]{:S(2)}, u32[]{:S(2)}) %collective-permute-start.2) | collective-permute-done | bytes 131104 | tf_op jit(solution)/shard_map/ppermute | solution.py:403
  16.1 0.0 collective-permute-done.rest_1_
  16.1 2.5 %mixer.3 = (bf16[32,64,128]{2,1,0:T(8,128)(2,1)}, f32[512,256]{1,0:T(8,128)S(1)}) custom-call(bf16[4,16,1024]{2,1,0:T(8,128)(2,1)S(1)} %get-tuple-element.27.rest_0_, bf16[4,16,1024]{2,1,0:T(8,128)(2,1)S(1)} %collective-permute-done.rest_1_, bf16[4,16,1024]{2,1,0:T(8,128)(2,1)S(1)} %collective-permute-done.1.rest_2_, ...), custom_call_target="tpu_custom_call", output_to_operand_aliasing={{0}: (11, {})} | custom-call | flops 5000000000 | bytes 2097152 | tf_op jit(solution)/shard_map/mixer/pallas_call | solution.py:422
  18.7 6.0 %all-to-all-start = ((bf16[32,64,128]{2,1,0:T(8,128)(2,1)}), bf16[32,64,128]{2,1,0:T(8,128)(2,1)S(1)}, u32[]{:S(2)}, u32[]{:S(2)}) async-start(bf16[32,64,128]{2,1,0:T(8,128)(2,1)} %get-tuple-element.50), calls=%async_computation | async-start | bytes 1048576 | tf_op jit(solution)/shard_map/all_to_all | solution.py:449
  24.6 0.8 %lags.1 = (bf16[32,1024]{1,0:T(8,128)(2,1)S(1)}, bf16[32,1024]{1,0:T(8,128)(2,1)S(1)}, bf16[32,1024]{1,0:T(8,128)(2,1)S(1)}, bf16[32,1024]{1,0:T(8,128)(2,1)S(1)}) custom-call(f32[512,256]{1,0:T(8,128)S(1)} %get-tuple-element.43.products, f32[32,128]{1,0:T(8,128)S(1)} %get-tuple-element.34.rest_7_.turn_re, f32[32,128]{1,0:T(8,128)S(1)} %get-tuple-element.35.rest_8_.turn_im, ...), custom_call_target="tpu_custom_call" | custom-call | flops 1000000000 | bytes 1048576 | tf_op jit(solution)/shard_map/lags/pallas_call | solution.py:452
  25.4 0.3 collective-permute-start.6
  25.7 1.5 %collective-permute-start.7 = (bf16[32,1024]{1,0:T(8,128)(2,1)S(1)}, bf16[32,1024]{1,0:T(8,128)(2,1)S(1)}, u32[]{:S(2)}, u32[]{:S(2)}) collective-permute-start(bf16[32,1024]{1,0:T(8,128)(2,1)S(1)} %get-tuple-element.47), channel_id=1, source_target_pairs={{0,16},{8,24},{16,0},{24,8},{1,17},{9,25},{17,1},{25,9},{2,18},{10... | collective-permute-start | bytes 196616 | tf_op jit(solution)/shard_map/ppermute | solution.py:462
  27.2 0.4 collective-permute-start.8
  27.6 0.0 collective-permute-done.6.rest_1_
  27.6 4.0 %collective-permute-done.7.rest_2_ = bf16[32,1024]{1,0:T(8,128)(2,1)S(1)} collective-permute-done((bf16[32,1024]{1,0:T(8,128)(2,1)S(1)}, bf16[32,1024]{1,0:T(8,128)(2,1)S(1)}, u32[]{:S(2)}, u32[]{:S(2)}) %collective-permute-start.7) | collective-permute-done | bytes 65568 | tf_op jit(solution)/shard_map/ppermute | solution.py:462
  31.6 2.2 %collective-permute-done.8.rest_3_ = bf16[32,1024]{1,0:T(8,128)(2,1)S(1)} collective-permute-done((bf16[32,1024]{1,0:T(8,128)(2,1)S(1)}, bf16[32,1024]{1,0:T(8,128)(2,1)S(1)}, u32[]{:S(2)}, u32[]{:S(2)}) %collective-permute-start.8) | collective-permute-done | bytes 65568 | tf_op jit(solution)/shard_map/ppermute | solution.py:462
  33.7 2.6 %taps.1 = (f32[4,32,1024]{2,1,0:T(8,128)}, bf16[1408,1024]{1,0:T(8,128)(2,1)S(1)}) custom-call(bf16[1024,1024]{1,0:T(8,128)(2,1)} %w_value.1, bf16[1024,1024]{1,0:T(8,128)(2,1)} %w_gate.3, bf16[32,1024]{1,0:T(8,128)(2,1)S(1)} %get-tuple-element.45.rest_0_, bf16[32,1024]{1,0:T(8,128)(2,1)S(1)} %collective-permute-done.6.rest_1_, ...), custom_call_target="tpu_custom_call" | custom-call | tf_op jit(solution)/shard_map/taps/pallas_call | solution.py:463
  36.3 3.6 %all-to-all-done.spread = bf16[32,64,128]{2,1,0:T(8,128)(2,1)S(1)} async-done(((bf16[32,64,128]{2,1,0:T(8,128)(2,1)}), bf16[32,64,128]{2,1,0:T(8,128)(2,1)S(1)}, u32[]{:S(2)}, u32[]{:S(2)}) %all-to-all-start) | async-done | bytes 524320 | tf_op jit(solution)/shard_map/all_to_all | solution.py:449
  39.9 2.6 %project.1 = bf16[128,1024]{1,0:T(8,128)(2,1)} custom-call(bf16[1408,1024]{1,0:T(8,128)(2,1)S(1)} %get-tuple-element.49.w_held, bf16[1024,1024]{1,0:T(8,128)(2,1)} %w_gate.3, bf16[32,64,128]{2,1,0:T(8,128)(2,1)S(1)} %all-to-all-done.spread), custom_call_target="tpu_custom_call" | custom-call | tf_op jit(solution)/shard_map/project/pallas_call | solution.py:478
Async XLA Ops:
  1.8 6.5 %collective-permute-start.4 = (bf16[4,16,1024]{2,1,0:T(8,128)(2,1)S(1)}, bf16[4,16,1024]{2,1,0:T(8,128)(2,1)S(1)}, u32[]{:S(2)}, u32[]{:S(2)}) collective-permute-start(bf16[4,16,1024]{2,1,0:T(8,128)(2,1)S(1)} %get-tuple-element.40), channel_id=1, source_target_pairs={{0,16},{8,24},{16,0},{24,8},{1,17},{9,25},{17,1},{25,9},{2,18},{10... | collective-permute-start | bytes 393224 | tf_op jit(solution)/shard_map/ppermute | solution.py:403
  3.9 7.0 %collective-permute-start.5 = (bf16[4,16,1024]{2,1,0:T(8,128)(2,1)S(1)}, bf16[4,16,1024]{2,1,0:T(8,128)(2,1)S(1)}, u32[]{:S(2)}, u32[]{:S(2)}) collective-permute-start(bf16[4,16,1024]{2,1,0:T(8,128)(2,1)S(1)} %get-tuple-element.41), channel_id=1, source_target_pairs={{0,24},{8,16},{16,8},{24,0},{1,25},{9,17},{17,9},{25,1},{2,26},{10... | collective-permute-start | bytes 393224 | tf_op jit(solution)/shard_map/ppermute | solution.py:403
  6.1 4.9 %collective-permute-start.3 = (bf16[4,16,1024]{2,1,0:T(8,128)(2,1)S(1)}, bf16[4,16,1024]{2,1,0:T(8,128)(2,1)S(1)}, u32[]{:S(2)}, u32[]{:S(2)}) collective-permute-start(bf16[4,16,1024]{2,1,0:T(8,128)(2,1)S(1)} %get-tuple-element.39), channel_id=1, source_target_pairs={{0,8},{8,0},{16,24},{24,16},{1,9},{9,1},{17,25},{25,17},{2,10},{10... | collective-permute-start | bytes 393224 | tf_op jit(solution)/shard_map/ppermute | solution.py:403
  6.5 7.1 %collective-permute-start.1 = (bf16[4,16,1024]{2,1,0:T(8,128)(2,1)S(1)}, bf16[4,16,1024]{2,1,0:T(8,128)(2,1)S(1)}, u32[]{:S(2)}, u32[]{:S(2)}) collective-permute-start(bf16[4,16,1024]{2,1,0:T(8,128)(2,1)S(1)} %get-tuple-element.29), channel_id=1, source_target_pairs={{0,16},{8,24},{16,0},{24,8},{1,17},{9,25},{17,1},{25,9},{2,18},{10... | collective-permute-start | bytes 393224 | tf_op jit(solution)/shard_map/ppermute | solution.py:403
  7.9 8.2 %collective-permute-start.2 = (bf16[4,16,1024]{2,1,0:T(8,128)(2,1)S(1)}, bf16[4,16,1024]{2,1,0:T(8,128)(2,1)S(1)}, u32[]{:S(2)}, u32[]{:S(2)}) collective-permute-start(bf16[4,16,1024]{2,1,0:T(8,128)(2,1)S(1)} %get-tuple-element.30), channel_id=1, source_target_pairs={{0,24},{8,16},{16,8},{24,0},{1,25},{9,17},{17,9},{25,1},{2,26},{10... | collective-permute-start | bytes 393224 | tf_op jit(solution)/shard_map/ppermute | solution.py:403
  8.3 7.8 %collective-permute-start = (bf16[4,16,1024]{2,1,0:T(8,128)(2,1)S(1)}, bf16[4,16,1024]{2,1,0:T(8,128)(2,1)S(1)}, u32[]{:S(2)}, u32[]{:S(2)}) collective-permute-start(bf16[4,16,1024]{2,1,0:T(8,128)(2,1)S(1)} %get-tuple-element.28), channel_id=1, source_target_pairs={{0,8},{8,0},{16,24},{24,16},{1,9},{9,1},{17,25},{25,17},{2,10},{10... | collective-permute-start | bytes 393224 | tf_op jit(solution)/shard_map/ppermute | solution.py:403
  18.7 21.3 %all-to-all-start = ((bf16[32,64,128]{2,1,0:T(8,128)(2,1)}), bf16[32,64,128]{2,1,0:T(8,128)(2,1)S(1)}, u32[]{:S(2)}, u32[]{:S(2)}) async-start(bf16[32,64,128]{2,1,0:T(8,128)(2,1)} %get-tuple-element.50), calls=%async_computation | async-start | bytes 1048576 | tf_op jit(solution)/shard_map/all_to_all | solution.py:449
  25.4 2.2 %collective-permute-start.6 = (bf16[32,1024]{1,0:T(8,128)(2,1)S(1)}, bf16[32,1024]{1,0:T(8,128)(2,1)S(1)}, u32[]{:S(2)}, u32[]{:S(2)}) collective-permute-start(bf16[32,1024]{1,0:T(8,128)(2,1)S(1)} %get-tuple-element.46), channel_id=1, source_target_pairs={{0,8},{8,0},{16,24},{24,16},{1,9},{9,1},{17,25},{25,17},{2,10},{10... | collective-permute-start | bytes 196616 | tf_op jit(solution)/shard_map/ppermute | solution.py:462
  25.7 5.8 %collective-permute-start.7 = (bf16[32,1024]{1,0:T(8,128)(2,1)S(1)}, bf16[32,1024]{1,0:T(8,128)(2,1)S(1)}, u32[]{:S(2)}, u32[]{:S(2)}) collective-permute-start(bf16[32,1024]{1,0:T(8,128)(2,1)S(1)} %get-tuple-element.47), channel_id=1, source_target_pairs={{0,16},{8,24},{16,0},{24,8},{1,17},{9,25},{17,1},{25,9},{2,18},{10... | collective-permute-start | bytes 196616 | tf_op jit(solution)/shard_map/ppermute | solution.py:462
  27.2 6.5 %collective-permute-start.8 = (bf16[32,1024]{1,0:T(8,128)(2,1)S(1)}, bf16[32,1024]{1,0:T(8,128)(2,1)S(1)}, u32[]{:S(2)}, u32[]{:S(2)}) collective-permute-start(bf16[32,1024]{1,0:T(8,128)(2,1)S(1)} %get-tuple-element.48), channel_id=1, source_target_pairs={{0,24},{8,16},{16,8},{24,0},{1,25},{9,17},{17,9},{25,1},{2,26},{10... | collective-permute-start | bytes 196616 | tf_op jit(solution)/shard_map/ppermute | solution.py:462

commit v5 on v4

--- a/solution.py
+++ b/solution.py
@@ -70,20 +70,17 @@
     return dot(jnp.concatenate([high, low, high], 1), table)
 
 
-def prep_kernel(pairs, n_tables, values, filter_taps, cotangent, gate_acts, *rest):
+def prep_kernel(jobs, n_tables, values, filter_taps, cotangent, gate_acts, *rest):
     tables, rest = rest[:n_tables], rest[n_tables:]
     (narrow, wide, sems, table_sems), rest = rest[-4:], rest[:-4]
-    outs, held = rest[: len(rest) - n_tables], rest[len(rest) - n_tables :]
+    outs, held = rest[: 2 * len(jobs)], rest[2 * len(jobs) :]
     me = lax.axis_index("seq")
-    channels = wide.shape[1] // 2
-    n_steps = 2 * len(pairs)
     copies = []
-    for at, j in enumerate(pairs):
-        start = lax.bitwise_xor(lax.shift_right_logical(me, 1), j) * (2 * channels)
-        both = pl.ds(pl.multiple_of(start, 2 * channels), 2 * channels)
-        copies.append([pltpu.make_async_copy(filter_taps.at[both, :], wide.at[at], sems.at[at, 3])])
+    for at, (j, chunk) in enumerate(jobs):
+        both = pl.ds(lax.bitwise_xor(lax.shift_right_logical(me, 1), j) * 2, 2)
+        copies.append([pltpu.make_async_copy(filter_taps.at[both, chunk], wide.at[at], sems.at[at, 3])])
         for i, ref in enumerate((values, cotangent, gate_acts)):
-            copies[-1].append(pltpu.make_async_copy(ref.at[both, :], narrow.at[at, i], sems.at[at, i]))
+            copies[-1].append(pltpu.make_async_copy(ref.at[both, chunk], narrow.at[at, i], sems.at[at, i]))
         for copy in copies[-1]:
             copy.start()
     brought = [
@@ -92,19 +89,15 @@
     ]
     for copy in brought:
         copy.start()
-    for at in range(len(pairs)):
+    for at in range(len(jobs)):
         for copy in copies[at]:
             copy.wait()
         for low in range(2):
-            side = lax.bitwise_xor(lax.bitwise_and(me, 1), low) * channels
-            mine = pl.ds(pl.multiple_of(side, channels), channels)
-            blocks = [wide[at, mine, :], *(narrow[at, i, mine, :].astype(jnp.float32) for i in range(3))]
-            for field, block in zip((TAPS, VALUE, COT, GATE), blocks):
-                first = 0
-                for out in outs[2 * at + low :: n_steps]:
-                    size = out.shape[1]
-                    out[field] = block[first : first + size].astype(jnp.bfloat16)
-                    first += size
+            side = lax.bitwise_xor(lax.bitwise_and(me, 1), low)
+            out = outs[2 * at + low]
+            out[TAPS] = wide[at, side].astype(jnp.bfloat16)
+            for i, field in enumerate((VALUE, COT, GATE)):
+                out[field] = narrow[at, i, side]
     for copy in brought:
         copy.wait()
 
@@ -363,34 +356,38 @@
     chunks = len(sizes)
     tables = [jnp.asarray(t) for t in dft_tables(total, n_seq)]
 
-    def prep(pairs, tables):
-        steps = [2 * j + low for j in pairs for low in range(2)]
-        outs = [pltpu.VMEM((4, size, seq_len), jnp.bfloat16) for size in sizes for _ in steps]
+    def prep(jobs, tables):
+        size = channels // chunks
+        outs = [pltpu.VMEM((4, size, seq_len), jnp.bfloat16)] * (2 * len(jobs))
         outs += [pltpu.VMEM(t.shape[1:] if i < 2 else t.shape, t.dtype) for i, t in enumerate(tables)]
+        fields = [
+            x.reshape(n_seq, chunks, size, seq_len) for x in (values, filter_taps, cotangent, gate_acts)
+        ]
         ready = pl.pallas_call(
-            functools.partial(prep_kernel, pairs, len(tables)),
+            functools.partial(prep_kernel, jobs, len(tables)),
             out_shape=outs,
             in_specs=[hbm] * (4 + len(tables)),
             out_specs=[vmem] * len(outs),
             scratch_shapes=[
-                pltpu.VMEM((len(pairs), 3, 2 * channels, seq_len), jnp.bfloat16),
-                pltpu.VMEM((len(pairs), 2 * channels, seq_len), jnp.float32),
-                pltpu.SemaphoreType.DMA((len(pairs), 4)),
+                pltpu.VMEM((len(jobs), 3, 2, size, seq_len), jnp.bfloat16),
+                pltpu.VMEM((len(jobs), 2, size, seq_len), jnp.float32),
+                pltpu.SemaphoreType.DMA((len(jobs), 4)),
                 pltpu.SemaphoreType.DMA((max(len(tables), 1),)),
             ],
             compiler_params=pltpu.CompilerParams(vmem_limit_bytes=8 * 2**20),
             cost_estimate=pl.CostEstimate(flops=0, bytes_accessed=4 * 2**20, transcendentals=0),
             name="prep",
-        )(*(stay(x) for x in (values, filter_taps, cotangent, gate_acts, *tables)))
-        for chunk in range(chunks):
-            for at, k in enumerate(steps):
-                sent[chunk, k] = ready[chunk * len(steps) + at]
-        return ready[chunks * len(steps) :]
+        )(*(stay(x) for x in (*fields, *tables)))
+        for at, (j, chunk) in enumerate(jobs):
+            for low in range(2):
+                sent[chunk, 2 * j + low] = ready[2 * at + low]
+        return ready[2 * len(jobs) :]
 
     sent, got = {}, {}
-    if chunks > 1:
-        prep(range(1, n_seq // 2), [])
-        tables = prep((0,), tables)
+    if chunks > 1 and n_seq > 2:
+        jobs = [(j, chunk) for chunk in range(chunks) for j in reversed(range(n_seq // 2))]
+        prep(jobs[: n_seq // 2 - 1], [])
+        tables = prep(jobs[n_seq // 2 - 1 :], tables)
     else:
         fields = (values, filter_taps.astype(jnp.bfloat16), cotangent, gate_acts)
         tables[:2] = [t[me] for t in tables[:2]]

time: 42.8 us -> 42.7 us (level)
  waiting for transfers between devices: 14.3 us -> 12.3 us
  starting transfers between devices: 13.6 us -> 15.5 us
    ppermute x6, waiting for transfers between devices: 4.62 us -> 2.57 us  [local(): got[chunk, k] = lax.ppermute(block, 'seq', route(k)) if k else block]
    ppermute x6, starting transfers between devices: 5.48 us -> 7.34 us  [local(): got[chunk, k] = lax.ppermute(block, 'seq', route(k)) if k else block]
where the time goes in v5:
time: 42.7 us; the launch traced here: 42.4 us
  starting transfers between devices  15.5 us (36%)
  Pallas kernels  13.9 us (33%)
  waiting for transfers between devices  12.3 us (29%)
  between operations  0.71 us (2%)
    ppermute x6, starting transfers between devices, local(): got[chunk, k] = lax.ppermute(block, 'seq', route(k)) if k else block  7.34 us
    ppermute x3, waiting for transfers between devices, local(): lax.ppermute(taps_blocks[k], 'seq', route(k))  6.11 us
    all_to_all x1, starting transfers between devices, local(): spread = lax.all_to_all(grads, ('near', 'seq', 'far'), 0, 0, tiled=True)  5.96 us
    pallas_call x2, Pallas kernels, local(): pl.pallas_call(functools.partial(mixer_kernel, n_seq, group, offset, plac...  5.17 us
    all_to_all x1, waiting for transfers between devices, local(): spread = lax.all_to_all(grads, ('near', 'seq', 'far'), 0, 0, tiled=True)  3.61 us
    pallas_call x2, Pallas kernels, prep(): pl.pallas_call(functools.partial(prep_kernel, jobs, len(tables)), out_sha...  2.74 us
    pallas_call x1, Pallas kernels, local(): pl.pallas_call(functools.partial(project_kernel, n_seq, n_far, n_near, si...  2.6 us
    pallas_call x1, Pallas kernels, local(): pl.pallas_call(functools.partial(taps_kernel, n_seq), out_shape=[jax.Shap...  2.57 us
  transfers between devices with their start and end apart: 10, of which 5 were waited for; matrix products, arithmetic and copies ran while one was open for 0% of the time, Pallas kernels for 18%

profile of v5, /device:TPU:1, one launch (start us, length us, event | category | flops | bytes accessed | tf_op | source)
XLA Modules:
  0.0 42.4 jit_solution(16046101228849652865)
XLA Ops:
  0.6 1.0 %prep.3 = (bf16[4,16,1024]{2,1,0:T(8,128)(2,1)S(1)}, bf16[4,16,1024]{2,1,0:T(8,128)(2,1)S(1)}) custom-call(bf16[4,2,16,1024]{3,2,1,0:T(8,128)(2,1)} %bitcast.7, f32[4,2,16,1024]{3,2,1,0:T(8,128)} %bitcast.5, bf16[4,2,16,1024]{3,2,1,0:T(8,128)(2,1)} %bitcast.9, bf16[4,2,16,1024]{3,2,1,0:T(8,128)(2,1)} %bitcast.11), custom_call_target="tpu_custom_call" | custom-call | bytes 4194304 | tf_op jit(solution)/shard_map/prep/pallas_call | solution.py:366
  1.7 2.1 %collective-permute-start.4 = (bf16[4,16,1024]{2,1,0:T(8,128)(2,1)S(1)}, bf16[4,16,1024]{2,1,0:T(8,128)(2,1)S(1)}, u32[]{:S(2)}, u32[]{:S(2)}) collective-permute-start(bf16[4,16,1024]{2,1,0:T(8,128)(2,1)S(1)} %get-tuple-element.40), channel_id=1, source_target_pairs={{0,16},{8,24},{16,0},{24,8},{1,17},{9,25},{17,1},{25,9},{2,18},{10... | collective-permute-start | bytes 393224 | tf_op jit(solution)/shard_map/ppermute | solution.py:400
  3.8 0.6 %collective-permute-start.5 = (bf16[4,16,1024]{2,1,0:T(8,128)(2,1)S(1)}, bf16[4,16,1024]{2,1,0:T(8,128)(2,1)S(1)}, u32[]{:S(2)}, u32[]{:S(2)}) collective-permute-start(bf16[4,16,1024]{2,1,0:T(8,128)(2,1)S(1)} %get-tuple-element.41), channel_id=1, source_target_pairs={{0,24},{8,16},{16,8},{24,0},{1,25},{9,17},{17,9},{25,1},{2,26},{10... | collective-permute-start | bytes 393224 | tf_op jit(solution)/shard_map/ppermute | solution.py:400
  4.4 1.7 %prep.2 = (bf16[4,16,1024]{2,1,0:T(8,128)(2,1)S(1)}, bf16[4,16,1024]{2,1,0:T(8,128)(2,1)S(1)}, bf16[4,16,1024]{2,1,0:T(8,128)(2,1)S(1)}, bf16[4,16,1024]{2,1,0:T...) custom-call(bf16[4,2,16,1024]{3,2,1,0:T(8,128)(2,1)} %bitcast.8, ...), custom_call_target="tpu_custom_call" | custom-call | bytes 4194304 | tf_op jit(solution)/shard_map/prep/pallas_call | solution.py:366
  6.1 0.4 collective-permute-start.3
  6.5 0.2 collective-permute-start
  6.7 1.7 %collective-permute-start.1 = (bf16[4,16,1024]{2,1,0:T(8,128)(2,1)S(1)}, bf16[4,16,1024]{2,1,0:T(8,128)(2,1)S(1)}, u32[]{:S(2)}, u32[]{:S(2)}) collective-permute-start(bf16[4,16,1024]{2,1,0:T(8,128)(2,1)S(1)} %get-tuple-element.29), channel_id=1, source_target_pairs={{0,16},{8,24},{16,0},{24,8},{1,17},{9,25},{17,1},{25,9},{2,18},{10... | collective-permute-start | bytes 393224 | tf_op jit(solution)/shard_map/ppermute | solution.py:400
  8.4 0.0 collective-permute-done.4.rest_2_
  8.4 2.3 %collective-permute-start.2 = (bf16[4,16,1024]{2,1,0:T(8,128)(2,1)S(1)}, bf16[4,16,1024]{2,1,0:T(8,128)(2,1)S(1)}, u32[]{:S(2)}, u32[]{:S(2)}) collective-permute-start(bf16[4,16,1024]{2,1,0:T(8,128)(2,1)S(1)} %get-tuple-element.30), channel_id=1, source_target_pairs={{0,24},{8,16},{16,8},{24,0},{1,25},{9,17},{17,9},{25,1},{2,26},{10... | collective-permute-start | bytes 393224 | tf_op jit(solution)/shard_map/ppermute | solution.py:400
  10.7 0.1 collective-permute-done.5.rest_3_
  10.8 0.0 collective-permute-done.3.rest_1_
  10.8 2.7 %mixer.2 = (bf16[32,64,128]{2,1,0:T(8,128)(2,1)}, f32[4,16,1024]{2,1,0:T(8,128)S(1)}) custom-call(bf16[4,16,1024]{2,1,0:T(8,128)(2,1)S(1)} %get-tuple-element.38.rest_0_, bf16[4,16,1024]{2,1,0:T(8,128)(2,1)S(1)} %collective-permute-done.3.rest_1_, bf16[4,16,1024]{2,1,0:T(8,128)(2,1)S(1)} %collective-permute-done.4.rest_2_, ...), custom_call_target="tpu_custom_call" | custom-call | flops 5000000000 | bytes 2097152 | tf_op jit(solution)/shard_map/mixer/pallas_call | solution.py:419
  13.5 0.0 collective-permute-done.rest_1_
  13.5 0.0 collective-permute-done.1.rest_2_
  13.5 2.5 %collective-permute-done.2.rest_3_ = bf16[4,16,1024]{2,1,0:T(8,128)(2,1)S(1)} collective-permute-done((bf16[4,16,1024]{2,1,0:T(8,128)(2,1)S(1)}, bf16[4,16,1024]{2,1,0:T(8,128)(2,1)S(1)}, u32[]{:S(2)}, u32[]{:S(2)}) %collective-permute-start.2) | collective-permute-done | bytes 131104 | tf_op jit(solution)/shard_map/ppermute | solution.py:400
  16.0 2.5 %mixer.3 = (bf16[32,64,128]{2,1,0:T(8,128)(2,1)}, f32[512,256]{1,0:T(8,128)S(1)}) custom-call(bf16[4,16,1024]{2,1,0:T(8,128)(2,1)S(1)} %get-tuple-element.27.rest_0_, bf16[4,16,1024]{2,1,0:T(8,128)(2,1)S(1)} %collective-permute-done.rest_1_, bf16[4,16,1024]{2,1,0:T(8,128)(2,1)S(1)} %collective-permute-done.1.rest_2_, ...), custom_call_target="tpu_custom_call", output_to_operand_aliasing={{0}: (11, {})} | custom-call | flops 5000000000 | bytes 2097152 | tf_op jit(solution)/shard_map/mixer/pallas_call | solution.py:419
  18.5 6.0 %all-to-all-start = ((bf16[32,64,128]{2,1,0:T(8,128)(2,1)}), bf16[32,64,128]{2,1,0:T(8,128)(2,1)S(1)}, u32[]{:S(2)}, u32[]{:S(2)}) async-start(bf16[32,64,128]{2,1,0:T(8,128)(2,1)} %get-tuple-element.50), calls=%async_computation | async-start | bytes 1048576 | tf_op jit(solution)/shard_map/all_to_all | solution.py:446
  24.5 0.8 %lags.1 = (bf16[32,1024]{1,0:T(8,128)(2,1)S(1)}, bf16[32,1024]{1,0:T(8,128)(2,1)S(1)}, bf16[32,1024]{1,0:T(8,128)(2,1)S(1)}, bf16[32,1024]{1,0:T(8,128)(2,1)S(1)}) custom-call(f32[512,256]{1,0:T(8,128)S(1)} %get-tuple-element.43.products, f32[32,128]{1,0:T(8,128)S(1)} %get-tuple-element.34.rest_7_.turn_re, f32[32,128]{1,0:T(8,128)S(1)} %get-tuple-element.35.rest_8_.turn_im, ...), custom_call_target="tpu_custom_call" | custom-call | flops 1000000000 | bytes 1048576 | tf_op jit(solution)/shard_map/lags/pallas_call | solution.py:449
  25.2 0.3 collective-permute-start.6
  25.6 1.5 %collective-permute-start.7 = (bf16[32,1024]{1,0:T(8,128)(2,1)S(1)}, bf16[32,1024]{1,0:T(8,128)(2,1)S(1)}, u32[]{:S(2)}, u32[]{:S(2)}) collective-permute-start(bf16[32,1024]{1,0:T(8,128)(2,1)S(1)} %get-tuple-element.47), channel_id=1, source_target_pairs={{0,16},{8,24},{16,0},{24,8},{1,17},{9,25},{17,1},{25,9},{2,18},{10... | collective-permute-start | bytes 196616 | tf_op jit(solution)/shard_map/ppermute | solution.py:459
  27.1 0.4 collective-permute-start.8
  27.5 0.0 collective-permute-done.6.rest_1_
  27.5 4.0 %collective-permute-done.7.rest_2_ = bf16[32,1024]{1,0:T(8,128)(2,1)S(1)} collective-permute-done((bf16[32,1024]{1,0:T(8,128)(2,1)S(1)}, bf16[32,1024]{1,0:T(8,128)(2,1)S(1)}, u32[]{:S(2)}, u32[]{:S(2)}) %collective-permute-start.7) | collective-permute-done | bytes 65568 | tf_op jit(solution)/shard_map/ppermute | solution.py:459
  31.4 2.2 %collective-permute-done.8.rest_3_ = bf16[32,1024]{1,0:T(8,128)(2,1)S(1)} collective-permute-done((bf16[32,1024]{1,0:T(8,128)(2,1)S(1)}, bf16[32,1024]{1,0:T(8,128)(2,1)S(1)}, u32[]{:S(2)}, u32[]{:S(2)}) %collective-permute-start.8) | collective-permute-done | bytes 65568 | tf_op jit(solution)/shard_map/ppermute | solution.py:459
  33.6 2.6 %taps.1 = (f32[4,32,1024]{2,1,0:T(8,128)}, bf16[1408,1024]{1,0:T(8,128)(2,1)S(1)}) custom-call(bf16[1024,1024]{1,0:T(8,128)(2,1)} %w_value.1, bf16[1024,1024]{1,0:T(8,128)(2,1)} %w_gate.3, bf16[32,1024]{1,0:T(8,128)(2,1)S(1)} %get-tuple-element.45.rest_0_, bf16[32,1024]{1,0:T(8,128)(2,1)S(1)} %collective-permute-done.6.rest_1_, ...), custom_call_target="tpu_custom_call" | custom-call | tf_op jit(solution)/shard_map/taps/pallas_call | solution.py:460
  36.1 3.6 %all-to-all-done.spread = bf16[32,64,128]{2,1,0:T(8,128)(2,1)S(1)} async-done(((bf16[32,64,128]{2,1,0:T(8,128)(2,1)}), bf16[32,64,128]{2,1,0:T(8,128)(2,1)S(1)}, u32[]{:S(2)}, u32[]{:S(2)}) %all-to-all-start) | async-done | bytes 524320 | tf_op jit(solution)/shard_map/all_to_all | solution.py:446
  39.8 2.6 %project.1 = bf16[128,1024]{1,0:T(8,128)(2,1)} custom-call(bf16[1408,1024]{1,0:T(8,128)(2,1)S(1)} %get-tuple-element.49.w_held, bf16[1024,1024]{1,0:T(8,128)(2,1)} %w_gate.3, bf16[32,64,128]{2,1,0:T(8,128)(2,1)S(1)} %all-to-all-done.spread), custom_call_target="tpu_custom_call" | custom-call | tf_op jit(solution)/shard_map/project/pallas_call | solution.py:475
Async XLA Ops:
  1.7 6.7 %collective-permute-start.4 = (bf16[4,16,1024]{2,1,0:T(8,128)(2,1)S(1)}, bf16[4,16,1024]{2,1,0:T(8,128)(2,1)S(1)}, u32[]{:S(2)}, u32[]{:S(2)}) collective-permute-start(bf16[4,16,1024]{2,1,0:T(8,128)(2,1)S(1)} %get-tuple-element.40), channel_id=1, source_target_pairs={{0,16},{8,24},{16,0},{24,8},{1,17},{9,25},{17,1},{25,9},{2,18},{10... | collective-permute-start | bytes 393224 | tf_op jit(solution)/shard_map/ppermute | solution.py:400
  3.8 7.0 %collective-permute-start.5 = (bf16[4,16,1024]{2,1,0:T(8,128)(2,1)S(1)}, bf16[4,16,1024]{2,1,0:T(8,128)(2,1)S(1)}, u32[]{:S(2)}, u32[]{:S(2)}) collective-permute-start(bf16[4,16,1024]{2,1,0:T(8,128)(2,1)S(1)} %get-tuple-element.41), channel_id=1, source_target_pairs={{0,24},{8,16},{16,8},{24,0},{1,25},{9,17},{17,9},{25,1},{2,26},{10... | collective-permute-start | bytes 393224 | tf_op jit(solution)/shard_map/ppermute | solution.py:400
  6.1 4.7 %collective-permute-start.3 = (bf16[4,16,1024]{2,1,0:T(8,128)(2,1)S(1)}, bf16[4,16,1024]{2,1,0:T(8,128)(2,1)S(1)}, u32[]{:S(2)}, u32[]{:S(2)}) collective-permute-start(bf16[4,16,1024]{2,1,0:T(8,128)(2,1)S(1)} %get-tuple-element.39), channel_id=1, source_target_pairs={{0,8},{8,0},{16,24},{24,16},{1,9},{9,1},{17,25},{25,17},{2,10},{10... | collective-permute-start | bytes 393224 | tf_op jit(solution)/shard_map/ppermute | solution.py:400
  6.5 7.0 %collective-permute-start = (bf16[4,16,1024]{2,1,0:T(8,128)(2,1)S(1)}, bf16[4,16,1024]{2,1,0:T(8,128)(2,1)S(1)}, u32[]{:S(2)}, u32[]{:S(2)}) collective-permute-start(bf16[4,16,1024]{2,1,0:T(8,128)(2,1)S(1)} %get-tuple-element.28), channel_id=1, source_target_pairs={{0,8},{8,0},{16,24},{24,16},{1,9},{9,1},{17,25},{25,17},{2,10},{10... | collective-permute-start | bytes 393224 | tf_op jit(solution)/shard_map/ppermute | solution.py:400
  6.7 6.8 %collective-permute-start.1 = (bf16[4,16,1024]{2,1,0:T(8,128)(2,1)S(1)}, bf16[4,16,1024]{2,1,0:T(8,128)(2,1)S(1)}, u32[]{:S(2)}, u32[]{:S(2)}) collective-permute-start(bf16[4,16,1024]{2,1,0:T(8,128)(2,1)S(1)} %get-tuple-element.29), channel_id=1, source_target_pairs={{0,16},{8,24},{16,0},{24,8},{1,17},{9,25},{17,1},{25,9},{2,18},{10... | collective-permute-start | bytes 393224 | tf_op jit(solution)/shard_map/ppermute | solution.py:400
  8.4 7.6 %collective-permute-start.2 = (bf16[4,16,1024]{2,1,0:T(8,128)(2,1)S(1)}, bf16[4,16,1024]{2,1,0:T(8,128)(2,1)S(1)}, u32[]{:S(2)}, u32[]{:S(2)}) collective-permute-start(bf16[4,16,1024]{2,1,0:T(8,128)(2,1)S(1)} %get-tuple-element.30), channel_id=1, source_target_pairs={{0,24},{8,16},{16,8},{24,0},{1,25},{9,17},{17,9},{25,1},{2,26},{10... | collective-permute-start | bytes 393224 | tf_op jit(solution)/shard_map/ppermute | solution.py:400
  18.5 21.3 %all-to-all-start = ((bf16[32,64,128]{2,1,0:T(8,128)(2,1)}), bf16[32,64,128]{2,1,0:T(8,128)(2,1)S(1)}, u32[]{:S(2)}, u32[]{:S(2)}) async-start(bf16[32,64,128]{2,1,0:T(8,128)(2,1)} %get-tuple-element.50), calls=%async_computation | async-start | bytes 1048576 | tf_op jit(solution)/shard_map/all_to_all | solution.py:446
  25.2 2.2 %collective-permute-start.6 = (bf16[32,1024]{1,0:T(8,128)(2,1)S(1)}, bf16[32,1024]{1,0:T(8,128)(2,1)S(1)}, u32[]{:S(2)}, u32[]{:S(2)}) collective-permute-start(bf16[32,1024]{1,0:T(8,128)(2,1)S(1)} %get-tuple-element.46), channel_id=1, source_target_pairs={{0,8},{8,0},{16,24},{24,16},{1,9},{9,1},{17,25},{25,17},{2,10},{10... | collective-permute-start | bytes 196616 | tf_op jit(solution)/shard_map/ppermute | solution.py:459
  25.6 5.8 %collective-permute-start.7 = (bf16[32,1024]{1,0:T(8,128)(2,1)S(1)}, bf16[32,1024]{1,0:T(8,128)(2,1)S(1)}, u32[]{:S(2)}, u32[]{:S(2)}) collective-permute-start(bf16[32,1024]{1,0:T(8,128)(2,1)S(1)} %get-tuple-element.47), channel_id=1, source_target_pairs={{0,16},{8,24},{16,0},{24,8},{1,17},{9,25},{17,1},{25,9},{2,18},{10... | collective-permute-start | bytes 196616 | tf_op jit(solution)/shard_map/ppermute | solution.py:459
  27.1 6.5 %collective-permute-start.8 = (bf16[32,1024]{1,0:T(8,128)(2,1)S(1)}, bf16[32,1024]{1,0:T(8,128)(2,1)S(1)}, u32[]{:S(2)}, u32[]{:S(2)}) collective-permute-start(bf16[32,1024]{1,0:T(8,128)(2,1)S(1)} %get-tuple-element.48), channel_id=1, source_target_pairs={{0,24},{8,16},{16,8},{24,0},{1,25},{9,17},{17,9},{25,1},{2,26},{10... | collective-permute-start | bytes 196616 | tf_op jit(solution)/shard_map/ppermute | solution.py:459

commit v6 on v5

--- a/solution.py
+++ b/solution.py
@@ -155,7 +155,7 @@
         grads, taps_out, sig, taps, up, cot, grads32, grads16, sems, taps32 = rest
     me = lax.axis_index("seq")
     _, channels, seq_len = blocks[0].shape
-    outer = sig.shape[0] // channels - PAD
+    outer = grads.shape[0]
     pitch, wide, narrow = outer + PAD, 2 * channels + PAD, channels + PAD
     own_outer = seq_len // LANES
 
@@ -414,8 +414,8 @@
             args.append(grads)
             specs.append(hbm)
         group = size if size <= 24 else 8
-        long = pltpu.VMEM((size * (outer + PAD), LANES), jnp.float32)
-        taps32 = pltpu.VMEM((outer * (size + PAD), LANES), jnp.float32)
+        long = pltpu.VMEM(((size + 8) * (outer + PAD), LANES), jnp.float32)
+        taps32 = pltpu.VMEM(((outer + 8) * (size + PAD), LANES), jnp.float32)
         grads, more = pl.pallas_call(
             functools.partial(mixer_kernel, n_seq, group, offset, places, last),
             out_shape=[
@@ -427,7 +427,7 @@
             input_output_aliases=aliases,
             scratch_shapes=[long] * 4
             + [
-                pltpu.VMEM((outer * (2 * size + PAD), LANES), jnp.float32),
+                pltpu.VMEM(((outer + 8) * (2 * size + PAD), LANES), jnp.float32),
                 pltpu.VMEM((2, outer, size, LANES), jnp.bfloat16),
                 pltpu.SemaphoreType.DMA((2,)),
             ]

time: 42.7 us -> 42.7 us (level)
  no operation moved by 1% of the time
where the time goes in v6:
time: 42.7 us; the launch traced here: 42.4 us
  starting transfers between devices  15.5 us (36%)
  Pallas kernels  13.9 us (33%)
  waiting for transfers between devices  12.3 us (29%)
  between operations  0.71 us (2%)
    ppermute x6, starting transfers between devices, local(): got[chunk, k] = lax.ppermute(block, 'seq', route(k)) if k else block  7.34 us
    ppermute x3, waiting for transfers between devices, local(): lax.ppermute(taps_blocks[k], 'seq', route(k))  6.11 us
    all_to_all x1, starting transfers between devices, local(): spread = lax.all_to_all(grads, ('near', 'seq', 'far'), 0, 0, tiled=True)  5.96 us
    pallas_call x2, Pallas kernels, local(): pl.pallas_call(functools.partial(mixer_kernel, n_seq, group, offset, plac...  5.17 us
    all_to_all x1, waiting for transfers between devices, local(): spread = lax.all_to_all(grads, ('near', 'seq', 'far'), 0, 0, tiled=True)  3.61 us
    pallas_call x2, Pallas kernels, prep(): pl.pallas_call(functools.partial(prep_kernel, jobs, len(tables)), out_sha...  2.74 us
    pallas_call x1, Pallas kernels, local(): pl.pallas_call(functools.partial(project_kernel, n_seq, n_far, n_near, si...  2.6 us
    pallas_call x1, Pallas kernels, local(): pl.pallas_call(functools.partial(taps_kernel, n_seq), out_shape=[jax.Shap...  2.57 us
  transfers between devices with their start and end apart: 10, of which 5 were waited for; matrix products, arithmetic and copies ran while one was open for 0% of the time, Pallas kernels for 18%

profile of v6, /device:TPU:1, one launch (start us, length us, event | category | flops | bytes accessed | tf_op | source)
XLA Modules:
  0.0 42.4 jit_solution(4653479010810557993)
XLA Ops:
  0.6 1.0 %prep.3 = (bf16[4,16,1024]{2,1,0:T(8,128)(2,1)S(1)}, bf16[4,16,1024]{2,1,0:T(8,128)(2,1)S(1)}) custom-call(bf16[4,2,16,1024]{3,2,1,0:T(8,128)(2,1)} %bitcast.7, f32[4,2,16,1024]{3,2,1,0:T(8,128)} %bitcast.5, bf16[4,2,16,1024]{3,2,1,0:T(8,128)(2,1)} %bitcast.9, bf16[4,2,16,1024]{3,2,1,0:T(8,128)(2,1)} %bitcast.11), custom_call_target="tpu_custom_call" | custom-call | bytes 4194304 | tf_op jit(solution)/shard_map/prep/pallas_call | solution.py:366
  1.7 2.1 %collective-permute-start.4 = (bf16[4,16,1024]{2,1,0:T(8,128)(2,1)S(1)}, bf16[4,16,1024]{2,1,0:T(8,128)(2,1)S(1)}, u32[]{:S(2)}, u32[]{:S(2)}) collective-permute-start(bf16[4,16,1024]{2,1,0:T(8,128)(2,1)S(1)} %get-tuple-element.40), channel_id=1, source_target_pairs={{0,16},{8,24},{16,0},{24,8},{1,17},{9,25},{17,1},{25,9},{2,18},{10... | collective-permute-start | bytes 393224 | tf_op jit(solution)/shard_map/ppermute | solution.py:400
  3.8 0.6 %collective-permute-start.5 = (bf16[4,16,1024]{2,1,0:T(8,128)(2,1)S(1)}, bf16[4,16,1024]{2,1,0:T(8,128)(2,1)S(1)}, u32[]{:S(2)}, u32[]{:S(2)}) collective-permute-start(bf16[4,16,1024]{2,1,0:T(8,128)(2,1)S(1)} %get-tuple-element.41), channel_id=1, source_target_pairs={{0,24},{8,16},{16,8},{24,0},{1,25},{9,17},{17,9},{25,1},{2,26},{10... | collective-permute-start | bytes 393224 | tf_op jit(solution)/shard_map/ppermute | solution.py:400
  4.4 1.7 %prep.2 = (bf16[4,16,1024]{2,1,0:T(8,128)(2,1)S(1)}, bf16[4,16,1024]{2,1,0:T(8,128)(2,1)S(1)}, bf16[4,16,1024]{2,1,0:T(8,128)(2,1)S(1)}, bf16[4,16,1024]{2,1,0:T...) custom-call(bf16[4,2,16,1024]{3,2,1,0:T(8,128)(2,1)} %bitcast.8, ...), custom_call_target="tpu_custom_call" | custom-call | bytes 4194304 | tf_op jit(solution)/shard_map/prep/pallas_call | solution.py:366
  6.1 0.4 collective-permute-start.3
  6.5 0.2 collective-permute-start
  6.7 1.7 %collective-permute-start.1 = (bf16[4,16,1024]{2,1,0:T(8,128)(2,1)S(1)}, bf16[4,16,1024]{2,1,0:T(8,128)(2,1)S(1)}, u32[]{:S(2)}, u32[]{:S(2)}) collective-permute-start(bf16[4,16,1024]{2,1,0:T(8,128)(2,1)S(1)} %get-tuple-element.29), channel_id=1, source_target_pairs={{0,16},{8,24},{16,0},{24,8},{1,17},{9,25},{17,1},{25,9},{2,18},{10... | collective-permute-start | bytes 393224 | tf_op jit(solution)/shard_map/ppermute | solution.py:400
  8.4 0.0 collective-permute-done.4.rest_2_
  8.4 2.3 %collective-permute-start.2 = (bf16[4,16,1024]{2,1,0:T(8,128)(2,1)S(1)}, bf16[4,16,1024]{2,1,0:T(8,128)(2,1)S(1)}, u32[]{:S(2)}, u32[]{:S(2)}) collective-permute-start(bf16[4,16,1024]{2,1,0:T(8,128)(2,1)S(1)} %get-tuple-element.30), channel_id=1, source_target_pairs={{0,24},{8,16},{16,8},{24,0},{1,25},{9,17},{17,9},{25,1},{2,26},{10... | collective-permute-start | bytes 393224 | tf_op jit(solution)/shard_map/ppermute | solution.py:400
  10.7 0.1 collective-permute-done.5.rest_3_
  10.8 0.0 collective-permute-done.3.rest_1_
  10.8 2.7 %mixer.2 = (bf16[32,64,128]{2,1,0:T(8,128)(2,1)}, f32[4,16,1024]{2,1,0:T(8,128)S(1)}) custom-call(bf16[4,16,1024]{2,1,0:T(8,128)(2,1)S(1)} %get-tuple-element.38.rest_0_, bf16[4,16,1024]{2,1,0:T(8,128)(2,1)S(1)} %collective-permute-done.3.rest_1_, bf16[4,16,1024]{2,1,0:T(8,128)(2,1)S(1)} %collective-permute-done.4.rest_2_, ...), custom_call_target="tpu_custom_call" | custom-call | flops 5000000000 | bytes 2097152 | tf_op jit(solution)/shard_map/mixer/pallas_call | solution.py:419
  13.5 0.0 collective-permute-done.rest_1_
  13.5 0.0 collective-permute-done.1.rest_2_
  13.5 2.5 %collective-permute-done.2.rest_3_ = bf16[4,16,1024]{2,1,0:T(8,128)(2,1)S(1)} collective-permute-done((bf16[4,16,1024]{2,1,0:T(8,128)(2,1)S(1)}, bf16[4,16,1024]{2,1,0:T(8,128)(2,1)S(1)}, u32[]{:S(2)}, u32[]{:S(2)}) %collective-permute-start.2) | collective-permute-done | bytes 131104 | tf_op jit(solution)/shard_map/ppermute | solution.py:400
  16.0 2.5 %mixer.3 = (bf16[32,64,128]{2,1,0:T(8,128)(2,1)}, f32[512,256]{1,0:T(8,128)S(1)}) custom-call(bf16[4,16,1024]{2,1,0:T(8,128)(2,1)S(1)} %get-tuple-element.27.rest_0_, bf16[4,16,1024]{2,1,0:T(8,128)(2,1)S(1)} %collective-permute-done.rest_1_, bf16[4,16,1024]{2,1,0:T(8,128)(2,1)S(1)} %collective-permute-done.1.rest_2_, ...), custom_call_target="tpu_custom_call", output_to_operand_aliasing={{0}: (11, {})} | custom-call | flops 5000000000 | bytes 2097152 | tf_op jit(solution)/shard_map/mixer/pallas_call | solution.py:419
  18.5 6.0 %all-to-all-start = ((bf16[32,64,128]{2,1,0:T(8,128)(2,1)}), bf16[32,64,128]{2,1,0:T(8,128)(2,1)S(1)}, u32[]{:S(2)}, u32[]{:S(2)}) async-start(bf16[32,64,128]{2,1,0:T(8,128)(2,1)} %get-tuple-element.50), calls=%async_computation | async-start | bytes 1048576 | tf_op jit(solution)/shard_map/all_to_all | solution.py:446
  24.5 0.8 %lags.1 = (bf16[32,1024]{1,0:T(8,128)(2,1)S(1)}, bf16[32,1024]{1,0:T(8,128)(2,1)S(1)}, bf16[32,1024]{1,0:T(8,128)(2,1)S(1)}, bf16[32,1024]{1,0:T(8,128)(2,1)S(1)}) custom-call(f32[512,256]{1,0:T(8,128)S(1)} %get-tuple-element.43.products, f32[32,128]{1,0:T(8,128)S(1)} %get-tuple-element.34.rest_7_.turn_re, f32[32,128]{1,0:T(8,128)S(1)} %get-tuple-element.35.rest_8_.turn_im, ...), custom_call_target="tpu_custom_call" | custom-call | flops 1000000000 | bytes 1048576 | tf_op jit(solution)/shard_map/lags/pallas_call | solution.py:449
  25.2 0.3 collective-permute-start.6
  25.6 1.5 %collective-permute-start.7 = (bf16[32,1024]{1,0:T(8,128)(2,1)S(1)}, bf16[32,1024]{1,0:T(8,128)(2,1)S(1)}, u32[]{:S(2)}, u32[]{:S(2)}) collective-permute-start(bf16[32,1024]{1,0:T(8,128)(2,1)S(1)} %get-tuple-element.47), channel_id=1, source_target_pairs={{0,16},{8,24},{16,0},{24,8},{1,17},{9,25},{17,1},{25,9},{2,18},{10... | collective-permute-start | bytes 196616 | tf_op jit(solution)/shard_map/ppermute | solution.py:459
  27.1 0.4 collective-permute-start.8
  27.5 0.0 collective-permute-done.6.rest_1_
  27.5 4.0 %collective-permute-done.7.rest_2_ = bf16[32,1024]{1,0:T(8,128)(2,1)S(1)} collective-permute-done((bf16[32,1024]{1,0:T(8,128)(2,1)S(1)}, bf16[32,1024]{1,0:T(8,128)(2,1)S(1)}, u32[]{:S(2)}, u32[]{:S(2)}) %collective-permute-start.7) | collective-permute-done | bytes 65568 | tf_op jit(solution)/shard_map/ppermute | solution.py:459
  31.4 2.2 %collective-permute-done.8.rest_3_ = bf16[32,1024]{1,0:T(8,128)(2,1)S(1)} collective-permute-done((bf16[32,1024]{1,0:T(8,128)(2,1)S(1)}, bf16[32,1024]{1,0:T(8,128)(2,1)S(1)}, u32[]{:S(2)}, u32[]{:S(2)}) %collective-permute-start.8) | collective-permute-done | bytes 65568 | tf_op jit(solution)/shard_map/ppermute | solution.py:459
  33.6 2.6 %taps.1 = (f32[4,32,1024]{2,1,0:T(8,128)}, bf16[1408,1024]{1,0:T(8,128)(2,1)S(1)}) custom-call(bf16[1024,1024]{1,0:T(8,128)(2,1)} %w_value.1, bf16[1024,1024]{1,0:T(8,128)(2,1)} %w_gate.3, bf16[32,1024]{1,0:T(8,128)(2,1)S(1)} %get-tuple-element.45.rest_0_, bf16[32,1024]{1,0:T(8,128)(2,1)S(1)} %collective-permute-done.6.rest_1_, ...), custom_call_target="tpu_custom_call" | custom-call | tf_op jit(solution)/shard_map/taps/pallas_call | solution.py:460
  36.1 3.6 %all-to-all-done.spread = bf16[32,64,128]{2,1,0:T(8,128)(2,1)S(1)} async-done(((bf16[32,64,128]{2,1,0:T(8,128)(2,1)}), bf16[32,64,128]{2,1,0:T(8,128)(2,1)S(1)}, u32[]{:S(2)}, u32[]{:S(2)}) %all-to-all-start) | async-done | bytes 524320 | tf_op jit(solution)/shard_map/all_to_all | solution.py:446
  39.8 2.6 %project.1 = bf16[128,1024]{1,0:T(8,128)(2,1)} custom-call(bf16[1408,1024]{1,0:T(8,128)(2,1)S(1)} %get-tuple-element.49.w_held, bf16[1024,1024]{1,0:T(8,128)(2,1)} %w_gate.3, bf16[32,64,128]{2,1,0:T(8,128)(2,1)S(1)} %all-to-all-done.spread), custom_call_target="tpu_custom_call" | custom-call | tf_op jit(solution)/shard_map/project/pallas_call | solution.py:475
Async XLA Ops:
  1.7 6.7 %collective-permute-start.4 = (bf16[4,16,1024]{2,1,0:T(8,128)(2,1)S(1)}, bf16[4,16,1024]{2,1,0:T(8,128)(2,1)S(1)}, u32[]{:S(2)}, u32[]{:S(2)}) collective-permute-start(bf16[4,16,1024]{2,1,0:T(8,128)(2,1)S(1)} %get-tuple-element.40), channel_id=1, source_target_pairs={{0,16},{8,24},{16,0},{24,8},{1,17},{9,25},{17,1},{25,9},{2,18},{10... | collective-permute-start | bytes 393224 | tf_op jit(solution)/shard_map/ppermute | solution.py:400
  3.8 7.0 %collective-permute-start.5 = (bf16[4,16,1024]{2,1,0:T(8,128)(2,1)S(1)}, bf16[4,16,1024]{2,1,0:T(8,128)(2,1)S(1)}, u32[]{:S(2)}, u32[]{:S(2)}) collective-permute-start(bf16[4,16,1024]{2,1,0:T(8,128)(2,1)S(1)} %get-tuple-element.41), channel_id=1, source_target_pairs={{0,24},{8,16},{16,8},{24,0},{1,25},{9,17},{17,9},{25,1},{2,26},{10... | collective-permute-start | bytes 393224 | tf_op jit(solution)/shard_map/ppermute | solution.py:400
  6.1 4.7 %collective-permute-start.3 = (bf16[4,16,1024]{2,1,0:T(8,128)(2,1)S(1)}, bf16[4,16,1024]{2,1,0:T(8,128)(2,1)S(1)}, u32[]{:S(2)}, u32[]{:S(2)}) collective-permute-start(bf16[4,16,1024]{2,1,0:T(8,128)(2,1)S(1)} %get-tuple-element.39), channel_id=1, source_target_pairs={{0,8},{8,0},{16,24},{24,16},{1,9},{9,1},{17,25},{25,17},{2,10},{10... | collective-permute-start | bytes 393224 | tf_op jit(solution)/shard_map/ppermute | solution.py:400
  6.5 7.0 %collective-permute-start = (bf16[4,16,1024]{2,1,0:T(8,128)(2,1)S(1)}, bf16[4,16,1024]{2,1,0:T(8,128)(2,1)S(1)}, u32[]{:S(2)}, u32[]{:S(2)}) collective-permute-start(bf16[4,16,1024]{2,1,0:T(8,128)(2,1)S(1)} %get-tuple-element.28), channel_id=1, source_target_pairs={{0,8},{8,0},{16,24},{24,16},{1,9},{9,1},{17,25},{25,17},{2,10},{10... | collective-permute-start | bytes 393224 | tf_op jit(solution)/shard_map/ppermute | solution.py:400
  6.7 6.8 %collective-permute-start.1 = (bf16[4,16,1024]{2,1,0:T(8,128)(2,1)S(1)}, bf16[4,16,1024]{2,1,0:T(8,128)(2,1)S(1)}, u32[]{:S(2)}, u32[]{:S(2)}) collective-permute-start(bf16[4,16,1024]{2,1,0:T(8,128)(2,1)S(1)} %get-tuple-element.29), channel_id=1, source_target_pairs={{0,16},{8,24},{16,0},{24,8},{1,17},{9,25},{17,1},{25,9},{2,18},{10... | collective-permute-start | bytes 393224 | tf_op jit(solution)/shard_map/ppermute | solution.py:400
  8.4 7.6 %collective-permute-start.2 = (bf16[4,16,1024]{2,1,0:T(8,128)(2,1)S(1)}, bf16[4,16,1024]{2,1,0:T(8,128)(2,1)S(1)}, u32[]{:S(2)}, u32[]{:S(2)}) collective-permute-start(bf16[4,16,1024]{2,1,0:T(8,128)(2,1)S(1)} %get-tuple-element.30), channel_id=1, source_target_pairs={{0,24},{8,16},{16,8},{24,0},{1,25},{9,17},{17,9},{25,1},{2,26},{10... | collective-permute-start | bytes 393224 | tf_op jit(solution)/shard_map/ppermute | solution.py:400
  18.5 21.3 %all-to-all-start = ((bf16[32,64,128]{2,1,0:T(8,128)(2,1)}), bf16[32,64,128]{2,1,0:T(8,128)(2,1)S(1)}, u32[]{:S(2)}, u32[]{:S(2)}) async-start(bf16[32,64,128]{2,1,0:T(8,128)(2,1)} %get-tuple-element.50), calls=%async_computation | async-start | bytes 1048576 | tf_op jit(solution)/shard_map/all_to_all | solution.py:446
  25.2 2.2 %collective-permute-start.6 = (bf16[32,1024]{1,0:T(8,128)(2,1)S(1)}, bf16[32,1024]{1,0:T(8,128)(2,1)S(1)}, u32[]{:S(2)}, u32[]{:S(2)}) collective-permute-start(bf16[32,1024]{1,0:T(8,128)(2,1)S(1)} %get-tuple-element.46), channel_id=1, source_target_pairs={{0,8},{8,0},{16,24},{24,16},{1,9},{9,1},{17,25},{25,17},{2,10},{10... | collective-permute-start | bytes 196616 | tf_op jit(solution)/shard_map/ppermute | solution.py:459
  25.6 5.8 %collective-permute-start.7 = (bf16[32,1024]{1,0:T(8,128)(2,1)S(1)}, bf16[32,1024]{1,0:T(8,128)(2,1)S(1)}, u32[]{:S(2)}, u32[]{:S(2)}) collective-permute-start(bf16[32,1024]{1,0:T(8,128)(2,1)S(1)} %get-tuple-element.47), channel_id=1, source_target_pairs={{0,16},{8,24},{16,0},{24,8},{1,17},{9,25},{17,1},{25,9},{2,18},{10... | collective-permute-start | bytes 196616 | tf_op jit(solution)/shard_map/ppermute | solution.py:459
  27.1 6.5 %collective-permute-start.8 = (bf16[32,1024]{1,0:T(8,128)(2,1)S(1)}, bf16[32,1024]{1,0:T(8,128)(2,1)S(1)}, u32[]{:S(2)}, u32[]{:S(2)}) collective-permute-start(bf16[32,1024]{1,0:T(8,128)(2,1)S(1)} %get-tuple-element.48), channel_id=1, source_target_pairs={{0,24},{8,16},{16,8},{24,0},{1,25},{9,17},{17,9},{25,1},{2,26},{10... | collective-permute-start | bytes 196616 | tf_op jit(solution)/shard_map/ppermute | solution.py:459

commit v7 on v6

--- a/solution.py
+++ b/solution.py
@@ -307,11 +307,18 @@
         copy.wait()
 
 
-def project_kernel(n_seq, n_far, n_near, sizes, w_held, w_gate, spread, out, held, gate_held, total, sem):
+def project_kernel(n_seq, n_far, n_near, sizes, w_held, w_gate, spread, out, held, gate_held, total, ready, sem, out_sems):
     features = w_gate.shape[0]
     split = features - gate_held.shape[0]
     copy = pltpu.make_async_copy(w_gate.at[split:, :], gate_held, sem)
     copy.start()
+    middle = (split + features) // 2 // LANES * LANES
+    pieces_out = [slice(0, split), slice(split, middle), slice(middle, features)]
+
+    def leaving(i):
+        at = pieces_out[i]
+        return pltpu.make_async_copy(ready.at[:, at], out.at[:, at], out_sems.at[i])
+
     share = sum(sizes)
     firsts = [sum(sizes[:i]) for i in range(len(sizes))]
 
@@ -324,12 +331,19 @@
                 held[g, rows, :] = jnp.concatenate(pieces, 0).astype(held.dtype)
         values, gates = (held[g].astype(jnp.bfloat16) for g in range(2))
         total[...] = dot(w_held[:features, :], values)
-        out[:, :split] = (total[:split, :] + dot(w_held[features:, :], gates)).T.astype(jnp.bfloat16)
+        ready[:, :split] = (total[:split, :] + dot(w_held[features:, :], gates)).T.astype(jnp.bfloat16)
+        leaving(0).start()
 
     in_block(before)
     copy.wait()
     gates = held[1].astype(jnp.bfloat16)
-    out[:, split:] = (total[split:, :] + dot(gate_held[...], gates)).T.astype(jnp.bfloat16)
+    for i in (1, 2):
+        at = pieces_out[i]
+        rest = dot(gate_held[at.start - split : at.stop - split, :], gates)
+        ready[:, at] = (total[at, :] + rest).T.astype(jnp.bfloat16)
+        leaving(i).start()
+    for i in range(3):
+        leaving(i).wait()
 
 
 def local(n_seq, n_far, n_near, values, gate_acts, cotangent, filter_taps, w_value, w_gate):
@@ -476,12 +490,14 @@
         functools.partial(project_kernel, n_seq, n_far, n_near, sizes),
         out_shape=jax.ShapeDtypeStruct((tokens, w_value.shape[0]), jnp.bfloat16),
         in_specs=[vmem, hbm, vmem],
-        out_specs=vmem,
+        out_specs=hbm,
         scratch_shapes=[
             pltpu.VMEM((2, rows * n_chan, tokens), held),
             pltpu.VMEM((w_gate.shape[0] * (SLABS - KEPT) // SLABS, w_gate.shape[1]), w_gate.dtype),
             pltpu.VMEM((w_gate.shape[0], tokens), jnp.float32),
+            pltpu.VMEM((tokens, w_gate.shape[0]), jnp.bfloat16),
             pltpu.SemaphoreType.DMA,
+            pltpu.SemaphoreType.DMA((3,)),
         ],
         compiler_params=pltpu.CompilerParams(vmem_limit_bytes=16 * 2**20),
         name="project",

time: 42.7 us -> 42.6 us (level)
  no operation moved by 1% of the time
where the time goes in v7:
time: 42.6 us; the launch traced here: 42.3 us
  starting transfers between devices  15.5 us (36%)
  Pallas kernels  13.8 us (32%)
  waiting for transfers between devices  12.3 us (29%)
  between operations  0.71 us (2%)
    ppermute x6, starting transfers between devices, local(): got[chunk, k] = lax.ppermute(block, 'seq', route(k)) if k else block  7.34 us
    ppermute x3, waiting for transfers between devices, local(): lax.ppermute(taps_blocks[k], 'seq', route(k))  6.11 us
    all_to_all x1, starting transfers between devices, local(): spread = lax.all_to_all(grads, ('near', 'seq', 'far'), 0, 0, tiled=True)  5.96 us
    pallas_call x2, Pallas kernels, local(): pl.pallas_call(functools.partial(mixer_kernel, n_seq, group, offset, plac...  5.17 us
    all_to_all x1, waiting for transfers between devices, local(): spread = lax.all_to_all(grads, ('near', 'seq', 'far'), 0, 0, tiled=True)  3.61 us
    pallas_call x2, Pallas kernels, prep(): pl.pallas_call(functools.partial(prep_kernel, jobs, len(tables)), out_sha...  2.74 us
    pallas_call x1, Pallas kernels, local(): pl.pallas_call(functools.partial(taps_kernel, n_seq), out_shape=[jax.Shap...  2.57 us
    ppermute x6, waiting for transfers between devices, local(): got[chunk, k] = lax.ppermute(block, 'seq', route(k)) if k else block  2.57 us
  transfers between devices with their start and end apart: 10, of which 5 were waited for; matrix products, arithmetic and copies ran while one was open for 0% of the time, Pallas kernels for 18%

profile of v7, /device:TPU:1, one launch (start us, length us, event | category | flops | bytes accessed | tf_op | source)
XLA Modules:
  0.0 42.3 jit_solution(4887509607021988910)
XLA Ops:
  0.6 1.0 %prep.3 = (bf16[4,16,1024]{2,1,0:T(8,128)(2,1)S(1)}, bf16[4,16,1024]{2,1,0:T(8,128)(2,1)S(1)}) custom-call(bf16[4,2,16,1024]{3,2,1,0:T(8,128)(2,1)} %bitcast.7, f32[4,2,16,1024]{3,2,1,0:T(8,128)} %bitcast.5, bf16[4,2,16,1024]{3,2,1,0:T(8,128)(2,1)} %bitcast.9, bf16[4,2,16,1024]{3,2,1,0:T(8,128)(2,1)} %bitcast.11), custom_call_target="tpu_custom_call" | custom-call | bytes 4194304 | tf_op jit(solution)/shard_map/prep/pallas_call | solution.py:380
  1.7 2.1 %collective-permute-start.4 = (bf16[4,16,1024]{2,1,0:T(8,128)(2,1)S(1)}, bf16[4,16,1024]{2,1,0:T(8,128)(2,1)S(1)}, u32[]{:S(2)}, u32[]{:S(2)}) collective-permute-start(bf16[4,16,1024]{2,1,0:T(8,128)(2,1)S(1)} %get-tuple-element.40), channel_id=1, source_target_pairs={{0,16},{8,24},{16,0},{24,8},{1,17},{9,25},{17,1},{25,9},{2,18},{10... | collective-permute-start | bytes 393224 | tf_op jit(solution)/shard_map/ppermute | solution.py:414
  3.8 0.6 %collective-permute-start.5 = (bf16[4,16,1024]{2,1,0:T(8,128)(2,1)S(1)}, bf16[4,16,1024]{2,1,0:T(8,128)(2,1)S(1)}, u32[]{:S(2)}, u32[]{:S(2)}) collective-permute-start(bf16[4,16,1024]{2,1,0:T(8,128)(2,1)S(1)} %get-tuple-element.41), channel_id=1, source_target_pairs={{0,24},{8,16},{16,8},{24,0},{1,25},{9,17},{17,9},{25,1},{2,26},{10... | collective-permute-start | bytes 393224 | tf_op jit(solution)/shard_map/ppermute | solution.py:414
  4.4 1.7 %prep.2 = (bf16[4,16,1024]{2,1,0:T(8,128)(2,1)S(1)}, bf16[4,16,1024]{2,1,0:T(8,128)(2,1)S(1)}, bf16[4,16,1024]{2,1,0:T(8,128)(2,1)S(1)}, bf16[4,16,1024]{2,1,0:T...) custom-call(bf16[4,2,16,1024]{3,2,1,0:T(8,128)(2,1)} %bitcast.8, ...), custom_call_target="tpu_custom_call" | custom-call | bytes 4194304 | tf_op jit(solution)/shard_map/prep/pallas_call | solution.py:380
  6.1 0.4 collective-permute-start.3
  6.5 0.2 collective-permute-start
  6.7 1.7 %collective-permute-start.1 = (bf16[4,16,1024]{2,1,0:T(8,128)(2,1)S(1)}, bf16[4,16,1024]{2,1,0:T(8,128)(2,1)S(1)}, u32[]{:S(2)}, u32[]{:S(2)}) collective-permute-start(bf16[4,16,1024]{2,1,0:T(8,128)(2,1)S(1)} %get-tuple-element.29), channel_id=1, source_target_pairs={{0,16},{8,24},{16,0},{24,8},{1,17},{9,25},{17,1},{25,9},{2,18},{10... | collective-permute-start | bytes 393224 | tf_op jit(solution)/shard_map/ppermute | solution.py:414
  8.4 0.0 collective-permute-done.4.rest_2_
  8.4 2.3 %collective-permute-start.2 = (bf16[4,16,1024]{2,1,0:T(8,128)(2,1)S(1)}, bf16[4,16,1024]{2,1,0:T(8,128)(2,1)S(1)}, u32[]{:S(2)}, u32[]{:S(2)}) collective-permute-start(bf16[4,16,1024]{2,1,0:T(8,128)(2,1)S(1)} %get-tuple-element.30), channel_id=1, source_target_pairs={{0,24},{8,16},{16,8},{24,0},{1,25},{9,17},{17,9},{25,1},{2,26},{10... | collective-permute-start | bytes 393224 | tf_op jit(solution)/shard_map/ppermute | solution.py:414
  10.7 0.1 collective-permute-done.5.rest_3_
  10.8 0.0 collective-permute-done.3.rest_1_
  10.8 2.7 %mixer.2 = (bf16[32,64,128]{2,1,0:T(8,128)(2,1)}, f32[4,16,1024]{2,1,0:T(8,128)S(1)}) custom-call(bf16[4,16,1024]{2,1,0:T(8,128)(2,1)S(1)} %get-tuple-element.38.rest_0_, bf16[4,16,1024]{2,1,0:T(8,128)(2,1)S(1)} %collective-permute-done.3.rest_1_, bf16[4,16,1024]{2,1,0:T(8,128)(2,1)S(1)} %collective-permute-done.4.rest_2_, ...), custom_call_target="tpu_custom_call" | custom-call | flops 5000000000 | bytes 2097152 | tf_op jit(solution)/shard_map/mixer/pallas_call | solution.py:433
  13.5 0.0 collective-permute-done.rest_1_
  13.5 0.0 collective-permute-done.1.rest_2_
  13.5 2.5 %collective-permute-done.2.rest_3_ = bf16[4,16,1024]{2,1,0:T(8,128)(2,1)S(1)} collective-permute-done((bf16[4,16,1024]{2,1,0:T(8,128)(2,1)S(1)}, bf16[4,16,1024]{2,1,0:T(8,128)(2,1)S(1)}, u32[]{:S(2)}, u32[]{:S(2)}) %collective-permute-start.2) | collective-permute-done | bytes 131104 | tf_op jit(solution)/shard_map/ppermute | solution.py:414
  16.0 2.5 %mixer.3 = (bf16[32,64,128]{2,1,0:T(8,128)(2,1)}, f32[512,256]{1,0:T(8,128)S(1)}) custom-call(bf16[4,16,1024]{2,1,0:T(8,128)(2,1)S(1)} %get-tuple-element.27.rest_0_, bf16[4,16,1024]{2,1,0:T(8,128)(2,1)S(1)} %collective-permute-done.rest_1_, bf16[4,16,1024]{2,1,0:T(8,128)(2,1)S(1)} %collective-permute-done.1.rest_2_, ...), custom_call_target="tpu_custom_call", output_to_operand_aliasing={{0}: (11, {})} | custom-call | flops 5000000000 | bytes 2097152 | tf_op jit(solution)/shard_map/mixer/pallas_call | solution.py:433
  18.5 6.0 %all-to-all-start = ((bf16[32,64,128]{2,1,0:T(8,128)(2,1)}), bf16[32,64,128]{2,1,0:T(8,128)(2,1)S(1)}, u32[]{:S(2)}, u32[]{:S(2)}) async-start(bf16[32,64,128]{2,1,0:T(8,128)(2,1)} %get-tuple-element.50), calls=%async_computation | async-start | bytes 1048576 | tf_op jit(solution)/shard_map/all_to_all | solution.py:460
  24.5 0.8 %lags.1 = (bf16[32,1024]{1,0:T(8,128)(2,1)S(1)}, bf16[32,1024]{1,0:T(8,128)(2,1)S(1)}, bf16[32,1024]{1,0:T(8,128)(2,1)S(1)}, bf16[32,1024]{1,0:T(8,128)(2,1)S(1)}) custom-call(f32[512,256]{1,0:T(8,128)S(1)} %get-tuple-element.43.products, f32[32,128]{1,0:T(8,128)S(1)} %get-tuple-element.34.rest_7_.turn_re, f32[32,128]{1,0:T(8,128)S(1)} %get-tuple-element.35.rest_8_.turn_im, ...), custom_call_target="tpu_custom_call" | custom-call | flops 1000000000 | bytes 1048576 | tf_op jit(solution)/shard_map/lags/pallas_call | solution.py:463
  25.2 0.3 collective-permute-start.6
  25.6 1.5 %collective-permute-start.7 = (bf16[32,1024]{1,0:T(8,128)(2,1)S(1)}, bf16[32,1024]{1,0:T(8,128)(2,1)S(1)}, u32[]{:S(2)}, u32[]{:S(2)}) collective-permute-start(bf16[32,1024]{1,0:T(8,128)(2,1)S(1)} %get-tuple-element.47), channel_id=1, source_target_pairs={{0,16},{8,24},{16,0},{24,8},{1,17},{9,25},{17,1},{25,9},{2,18},{10... | collective-permute-start | bytes 196616 | tf_op jit(solution)/shard_map/ppermute | solution.py:473
  27.1 0.4 collective-permute-start.8
  27.5 0.0 collective-permute-done.6.rest_1_
  27.5 4.0 %collective-permute-done.7.rest_2_ = bf16[32,1024]{1,0:T(8,128)(2,1)S(1)} collective-permute-done((bf16[32,1024]{1,0:T(8,128)(2,1)S(1)}, bf16[32,1024]{1,0:T(8,128)(2,1)S(1)}, u32[]{:S(2)}, u32[]{:S(2)}) %collective-permute-start.7) | collective-permute-done | bytes 65568 | tf_op jit(solution)/shard_map/ppermute | solution.py:473
  31.4 2.2 %collective-permute-done.8.rest_3_ = bf16[32,1024]{1,0:T(8,128)(2,1)S(1)} collective-permute-done((bf16[32,1024]{1,0:T(8,128)(2,1)S(1)}, bf16[32,1024]{1,0:T(8,128)(2,1)S(1)}, u32[]{:S(2)}, u32[]{:S(2)}) %collective-permute-start.8) | collective-permute-done | bytes 65568 | tf_op jit(solution)/shard_map/ppermute | solution.py:473
  33.6 2.6 %taps.1 = (f32[4,32,1024]{2,1,0:T(8,128)}, bf16[1408,1024]{1,0:T(8,128)(2,1)S(1)}) custom-call(bf16[1024,1024]{1,0:T(8,128)(2,1)} %w_value.1, bf16[1024,1024]{1,0:T(8,128)(2,1)} %w_gate.3, bf16[32,1024]{1,0:T(8,128)(2,1)S(1)} %get-tuple-element.45.rest_0_, bf16[32,1024]{1,0:T(8,128)(2,1)S(1)} %collective-permute-done.6.rest_1_, ...), custom_call_target="tpu_custom_call" | custom-call | tf_op jit(solution)/shard_map/taps/pallas_call | solution.py:474
  36.1 3.6 %all-to-all-done.spread = bf16[32,64,128]{2,1,0:T(8,128)(2,1)S(1)} async-done(((bf16[32,64,128]{2,1,0:T(8,128)(2,1)}), bf16[32,64,128]{2,1,0:T(8,128)(2,1)S(1)}, u32[]{:S(2)}, u32[]{:S(2)}) %all-to-all-start) | async-done | bytes 524320 | tf_op jit(solution)/shard_map/all_to_all | solution.py:460
  39.8 2.5 %project.1 = bf16[128,1024]{1,0:T(8,128)(2,1)} custom-call(bf16[1408,1024]{1,0:T(8,128)(2,1)S(1)} %get-tuple-element.49.w_held, bf16[1024,1024]{1,0:T(8,128)(2,1)} %w_gate.3, bf16[32,64,128]{2,1,0:T(8,128)(2,1)S(1)} %all-to-all-done.spread), custom_call_target="tpu_custom_call" | custom-call | tf_op jit(solution)/shard_map/project/pallas_call | solution.py:489
Async XLA Ops:
  1.7 6.7 %collective-permute-start.4 = (bf16[4,16,1024]{2,1,0:T(8,128)(2,1)S(1)}, bf16[4,16,1024]{2,1,0:T(8,128)(2,1)S(1)}, u32[]{:S(2)}, u32[]{:S(2)}) collective-permute-start(bf16[4,16,1024]{2,1,0:T(8,128)(2,1)S(1)} %get-tuple-element.40), channel_id=1, source_target_pairs={{0,16},{8,24},{16,0},{24,8},{1,17},{9,25},{17,1},{25,9},{2,18},{10... | collective-permute-start | bytes 393224 | tf_op jit(solution)/shard_map/ppermute | solution.py:414
  3.8 7.0 %collective-permute-start.5 = (bf16[4,16,1024]{2,1,0:T(8,128)(2,1)S(1)}, bf16[4,16,1024]{2,1,0:T(8,128)(2,1)S(1)}, u32[]{:S(2)}, u32[]{:S(2)}) collective-permute-start(bf16[4,16,1024]{2,1,0:T(8,128)(2,1)S(1)} %get-tuple-element.41), channel_id=1, source_target_pairs={{0,24},{8,16},{16,8},{24,0},{1,25},{9,17},{17,9},{25,1},{2,26},{10... | collective-permute-start | bytes 393224 | tf_op jit(solution)/shard_map/ppermute | solution.py:414
  6.1 4.7 %collective-permute-start.3 = (bf16[4,16,1024]{2,1,0:T(8,128)(2,1)S(1)}, bf16[4,16,1024]{2,1,0:T(8,128)(2,1)S(1)}, u32[]{:S(2)}, u32[]{:S(2)}) collective-permute-start(bf16[4,16,1024]{2,1,0:T(8,128)(2,1)S(1)} %get-tuple-element.39), channel_id=1, source_target_pairs={{0,8},{8,0},{16,24},{24,16},{1,9},{9,1},{17,25},{25,17},{2,10},{10... | collective-permute-start | bytes 393224 | tf_op jit(solution)/shard_map/ppermute | solution.py:414
  6.5 7.0 %collective-permute-start = (bf16[4,16,1024]{2,1,0:T(8,128)(2,1)S(1)}, bf16[4,16,1024]{2,1,0:T(8,128)(2,1)S(1)}, u32[]{:S(2)}, u32[]{:S(2)}) collective-permute-start(bf16[4,16,1024]{2,1,0:T(8,128)(2,1)S(1)} %get-tuple-element.28), channel_id=1, source_target_pairs={{0,8},{8,0},{16,24},{24,16},{1,9},{9,1},{17,25},{25,17},{2,10},{10... | collective-permute-start | bytes 393224 | tf_op jit(solution)/shard_map/ppermute | solution.py:414
  6.7 6.8 %collective-permute-start.1 = (bf16[4,16,1024]{2,1,0:T(8,128)(2,1)S(1)}, bf16[4,16,1024]{2,1,0:T(8,128)(2,1)S(1)}, u32[]{:S(2)}, u32[]{:S(2)}) collective-permute-start(bf16[4,16,1024]{2,1,0:T(8,128)(2,1)S(1)} %get-tuple-element.29), channel_id=1, source_target_pairs={{0,16},{8,24},{16,0},{24,8},{1,17},{9,25},{17,1},{25,9},{2,18},{10... | collective-permute-start | bytes 393224 | tf_op jit(solution)/shard_map/ppermute | solution.py:414
  8.4 7.6 %collective-permute-start.2 = (bf16[4,16,1024]{2,1,0:T(8,128)(2,1)S(1)}, bf16[4,16,1024]{2,1,0:T(8,128)(2,1)S(1)}, u32[]{:S(2)}, u32[]{:S(2)}) collective-permute-start(bf16[4,16,1024]{2,1,0:T(8,128)(2,1)S(1)} %get-tuple-element.30), channel_id=1, source_target_pairs={{0,24},{8,16},{16,8},{24,0},{1,25},{9,17},{17,9},{25,1},{2,26},{10... | collective-permute-start | bytes 393224 | tf_op jit(solution)/shard_map/ppermute | solution.py:414
  18.5 21.3 %all-to-all-start = ((bf16[32,64,128]{2,1,0:T(8,128)(2,1)}), bf16[32,64,128]{2,1,0:T(8,128)(2,1)S(1)}, u32[]{:S(2)}, u32[]{:S(2)}) async-start(bf16[32,64,128]{2,1,0:T(8,128)(2,1)} %get-tuple-element.50), calls=%async_computation | async-start | bytes 1048576 | tf_op jit(solution)/shard_map/all_to_all | solution.py:460
  25.2 2.2 %collective-permute-start.6 = (bf16[32,1024]{1,0:T(8,128)(2,1)S(1)}, bf16[32,1024]{1,0:T(8,128)(2,1)S(1)}, u32[]{:S(2)}, u32[]{:S(2)}) collective-permute-start(bf16[32,1024]{1,0:T(8,128)(2,1)S(1)} %get-tuple-element.46), channel_id=1, source_target_pairs={{0,8},{8,0},{16,24},{24,16},{1,9},{9,1},{17,25},{25,17},{2,10},{10... | collective-permute-start | bytes 196616 | tf_op jit(solution)/shard_map/ppermute | solution.py:473
  25.6 5.8 %collective-permute-start.7 = (bf16[32,1024]{1,0:T(8,128)(2,1)S(1)}, bf16[32,1024]{1,0:T(8,128)(2,1)S(1)}, u32[]{:S(2)}, u32[]{:S(2)}) collective-permute-start(bf16[32,1024]{1,0:T(8,128)(2,1)S(1)} %get-tuple-element.47), channel_id=1, source_target_pairs={{0,16},{8,24},{16,0},{24,8},{1,17},{9,25},{17,1},{25,9},{2,18},{10... | collective-permute-start | bytes 196616 | tf_op jit(solution)/shard_map/ppermute | solution.py:473
  27.1 6.5 %collective-permute-start.8 = (bf16[32,1024]{1,0:T(8,128)(2,1)S(1)}, bf16[32,1024]{1,0:T(8,128)(2,1)S(1)}, u32[]{:S(2)}, u32[]{:S(2)}) collective-permute-start(bf16[32,1024]{1,0:T(8,128)(2,1)S(1)} %get-tuple-element.48), channel_id=1, source_target_pairs={{0,24},{8,16},{16,8},{24,0},{1,25},{9,17},{17,9},{25,1},{2,26},{10... | collective-permute-start | bytes 196616 | tf_op jit(solution)/shard_map/ppermute | solution.py:473
